TPU v7x, 32 devices: a whole 2x2x4 slice. The times are simulated.
32 devices in a mesh: region: 16 (over z, x, core), member: 2 (over y).
Axes of the slice: x: 2, y: 2, z: 4, core: 2. Of those that a mesh axis runs over, the one named last changes fastest.
Arguments:
- state: float32 [1024, 32, 256], P('member', 'region'), may hold values from -8 to 8
- neighbours: int32 [32, 5], replicated, may hold values from 0 to 31, as said below
- obs_cell: int32 [32, 2, 64], replicated, may hold values from 0 to 255
- obs_values: float32 [32, 2, 64], replicated, may hold values from -6 to 6
- obs_var: float32 [32, 2, 64], replicated, may hold values from 0.25 to 1
Outputs:
- analysis: float32 [1024, 32, 256], P('member', 'region')
Inputs may be any that keep to these rules, and one draw needn't show every extreme that they name: `neighbours`: patch g lies in region g // 2. Each patch lists 5 different patches in some order: two of the region before its own and two of the region after it (regions wrap around), and one other patch of its own region.
All inputs are finite; a program needn't handle non-finite values.
Results may differ from a plain program's by a relative error of at most 0.0003.
Values sent between devices are 32-bit elements; how exact they have to be, the bound alone decides.
No kernel may reach another device: no remote copies, remote signals or barrier semaphores. Data moves between devices by JAX's collectives and lax.ppermute only.
A program may use at most 128 MiB of HBM per device.

v0:
```python
import functools
import math

import jax
import jax.numpy as jnp
from jax import lax
from jax.experimental import pallas as pl
from jax.experimental.pallas import tpu as pltpu
from jax.sharding import PartitionSpec as P

NBATCH = 2
HIGHEST = lax.Precision.HIGHEST
F32 = jnp.float32
BF16 = jnp.bfloat16
VMEM = pl.BlockSpec(memory_space=pltpu.VMEM)
SMEM = pl.BlockSpec(memory_space=pltpu.SMEM)
NN = (((1,), (0,)), ((), ()))
NT = (((1,), (1,)), ((), ()))
TN = (((0,), (0,)), ((), ()))
RESIDUAL = 1e-3
MOST_STEPS = 15
TILE = 256


def call(kernel, outs, ins, args, scratch=(), flops=0, limit=48):
    shapes = [jax.ShapeDtypeStruct(shape, dtype) for shape, dtype, _ in outs]
    moved = sum(math.prod(s.shape) * s.dtype.itemsize for s in shapes)
    moved += sum(a.size * a.dtype.itemsize for a in args)
    return pl.pallas_call(
        kernel,
        out_shape=shapes,
        in_specs=ins,
        out_specs=[space for _, _, space in outs],
        scratch_shapes=list(scratch),
        compiler_params=pltpu.CompilerParams(vmem_limit_bytes=limit * 1024 * 1024),
        cost_estimate=pl.CostEstimate(flops=flops, bytes_accessed=moved, transcendentals=0),
    )(*args)


def split(x):
    high = x.astype(BF16)
    return high, (x - high.astype(F32)).astype(BF16)


def dot(a, b, dims=NN):
    return lax.dot_general(a, b, dims, preferred_element_type=F32)


def dot3(a, b, dims=NN):
    (left,), (right,) = dims[0]
    lhs = jnp.concatenate([a[0], a[0], a[1]], axis=left)
    rhs = jnp.concatenate([b[0], b[1], b[0]], axis=right)
    return dot(lhs, rhs, dims)


def dot2(a, b, dims=NN):
    (left,), (right,) = dims[0]
    return dot(jnp.concatenate([a[0], a[0]], axis=left), jnp.concatenate(b, axis=right), dims)


def select(hot, parts, dims):
    (left,), (right,) = dims[0]
    hot = hot.astype(BF16)
    lhs = jnp.concatenate([hot] * len(parts), axis=left)
    return dot(lhs, jnp.concatenate(parts, axis=right), dims)


def split_all(x):
    high, middle = split(x)
    low = x - high.astype(F32) - middle.astype(F32)
    return high, middle, low.astype(BF16)


def step_limits():
    limits = []
    for steps in range(MOST_STEPS):
        rho = RESIDUAL
        for _ in range(steps):
            rho = math.sqrt(2.0 * rho / (1.0 + rho))
        limits.append(2.0 * rho / (1.0 - rho) if rho < 1.0 else math.inf)
    return limits


def diagonal(n, columns, first):
    row = lax.broadcasted_iota(jnp.int32, (n, columns), 0)
    column = lax.broadcasted_iota(jnp.int32, (n, columns), 1)
    return row + first == column


def selector(picks, cells, scratch):
    per_patch = picks.shape[1]
    scratch[...] = jnp.full_like(scratch, -1)
    scratch[0:1, 0:per_patch] = picks
    grid = lax.broadcasted_iota(jnp.int32, (cells, scratch.shape[1]), 0)
    hot = (grid == scratch[0:1, :]).astype(F32)
    return jnp.transpose(hot)[0:per_patch, :]


def pick_kernel(first_ref, cells_hbm, state_hbm, rows_ref, cells_ref, state_ref, scratch, field_ref, sems):
    members, patches, cells = state_ref.shape
    chunks = sems.shape[0] - 1
    size = members // chunks
    spans = [pl.ds(i * size, size) for i in range(chunks)]
    first = pltpu.make_async_copy(cells_hbm, cells_ref, sems.at[chunks])
    first.start()
    copies = []
    for i, span in enumerate(spans):
        copies.append(pltpu.make_async_copy(state_hbm.at[span], state_ref.at[span], sems.at[i]))
        copies[-1].start()
    first.wait()
    hots = [selector(cells_ref[pl.ds(first_ref[0] + p, 1), 0, :], cells, scratch) for p in range(patches)]
    for i, span in enumerate(spans):
        copies[i].wait()
        for p in range(patches):
            field_ref[p, span] = state_ref[span, p, :]
            rows_ref[p, :, i * size : (i + 1) * size] = select(hots[p], split_all(field_ref[p, span]), NT)


def sort_kernel(place_ref, values_hbm, var_hbm, state_ref, *refs):
    keep_ref, send_ref, values_ref, var_ref, sems = refs[-5:]
    copies = [
        pltpu.make_async_copy(values_hbm, values_ref, sems.at[0]),
        pltpu.make_async_copy(var_hbm, var_ref, sems.at[1]),
    ]
    for copy in copies:
        copy.start()
    column = place_ref[0]
    first, second = state_ref[:, 0, :], state_ref[:, 1, :]
    keep_ref[...] = jnp.where(column == 0, first, second)
    send_ref[...] = jnp.where(column == 0, second, first)
    for copy in copies:
        copy.wait()


def factor_kernel(pieces, batch, members, ids_ref, values_ref, var_ref, *refs):
    count = len(refs) - 12
    sources = refs[:count]
    sh_ref, sl_ref, d_ref, g_ref, xh_ref, xl_ref, n_ref, flat, eye_ref, x_ref, wa, wb = refs[count:]
    per_patch = values_ref.shape[2]
    flat[...] = jnp.ones_like(flat)
    blocks = len(pieces)
    own = ids_ref[blocks]
    for i in range(blocks):
        patch = ids_ref[i]
        widening = (patch == own).astype(jnp.int32)
        for j in range(ids_ref.shape[0] - blocks - 1):
            widening = widening + (ids_ref[blocks + 1 + j] == patch).astype(jnp.int32) * (j + 2)
        flat[i : i + 1, 0:per_patch] = values_ref[pl.ds(patch, 1), batch, :]
        noise = var_ref[pl.ds(patch, 1), batch, :] * widening.astype(F32)
        flat[blocks + i : blocks + i + 1, 0:per_patch] = noise
    upright = jnp.transpose(flat[...])
    for i, halves in enumerate(pieces):
        rows = [sources[which][index] for which, index, _ in halves]
        total = sum(jnp.sum(part, axis=1, keepdims=True) for part in rows)
        mean = total * (1.0 / members)
        noise = upright[0:per_patch, blocks + i : blocks + i + 1]
        scale = lax.rsqrt(noise * (members - 1.0))
        at = slice(i * per_patch, (i + 1) * per_patch)
        for part, (_, _, start) in zip(rows, halves):
            size = part.shape[1]
            high, low = split((part - mean) * scale)
            lanes = slice(start * size, (start + 1) * size)
            sh_ref[at, lanes] = high
            sl_ref[at, lanes] = low
        shift = (upright[0:per_patch, i : i + 1] - mean) * scale
        d_ref[at, :] = jnp.broadcast_to(shift, (per_patch, d_ref.shape[1]))
    n = sh_ref.shape[0]
    head = min(TILE, n)
    tail = n - head
    s = (sh_ref[...], sl_ref[...])
    left = dot3(s, [part[0:head] for part in s], NT)
    g_ref[:, 0:head] = left
    g_ref[0:head, head:n] = jnp.transpose(left[head:n])
    low = [part[head:n] for part in s]
    g_ref[head:n, head:n] = dot3(low, low, NT)
    g = g_ref[...]
    square = jnp.sum(jnp.sum(g * g, axis=0, keepdims=True), axis=1, keepdims=True)
    norm = jnp.sqrt(square) * (1.0 + 1e-5)
    size = square[0, 0]
    limits = step_limits()
    pairs = jnp.int32(0)
    for k in range(5, MOST_STEPS - 2, 2):
        limit = limits[k] * (1.0 - 1e-4)
        pairs = pairs + (size > limit * limit).astype(jnp.int32)
    n_ref[0] = (size > 1.6e7).astype(jnp.int32) + (size > 1e8).astype(jnp.int32)
    eye_ref[...] = diagonal(n, n, 0).astype(F32)
    eye = eye_ref[...]
    first = 2.0 / (2.0 + norm)
    rho = norm * (0.5 * first)
    rho2 = rho * rho
    weight = 2.0 / (2.0 - rho2)
    keep = 0.5 * rho2 * weight
    r = (1.0 - first) * eye - first * g
    parts = split(r)
    x = (weight * first) * (eye + r)
    x_ref[...] = x
    for i, part in enumerate(split(x)):
        wa[i, :, n : 2 * n] = part

    def store(targets, start, left, corner):
        blocks = [(slice(0, n), slice(start, start + head), left)]
        blocks.append((slice(head, n), slice(start + head, start + n), corner))
        blocks.append((slice(0, head), slice(start + head, start + n), jnp.transpose(left[head:n])))
        for rows, columns, block in blocks:
            for target, part in zip(targets, split(block)):
                target[rows, columns] = part

    def corner_of(weight, keep, left, corner):
        left = weight * left - keep * eye_ref[:, 0:head]
        return left, weight * corner - keep * eye_ref[head:n, head:n]

    left = dot3(parts, [part[:, 0:head] for part in parts])
    corner = dot3([part[head:n] for part in parts], [part[:, head:n] for part in parts])
    store((wa.at[0], wa.at[1]), 0, *corner_of(weight, keep, left, corner))

    def advance(source, target, rho2, exact):
        weight = 2.0 / (2.0 - rho2)
        keep = 0.5 * rho2 * weight
        parts = (source[0, :, 0:n], source[1, :, 0:n])
        ends = [jnp.concatenate([source[i, :, head:n], source[i, :, n + head : 2 * n]], axis=1) for i in (0, 1)]
        times = dot3 if exact else dot2
        left = times(parts, (source[0, :, 0:head], source[1, :, 0:head]))
        corners = times([part[head:n] for part in parts], ends)
        both = (target.at[0], target.at[1])
        store(both, 0, *corner_of(weight, keep, left, corners[:, 0:tail]))
        left = dot2(parts, (source[0, :, n : n + head], source[1, :, n : n + head]))
        left = weight * (x_ref[:, 0:head] + left)
        corner = weight * (x_ref[head:n, head:n] + corners[:, tail : 2 * tail])
        x_ref[:, 0:head] = left
        x_ref[head:n, head:n] = corner
        store(both, n, left, corner)
        return keep * keep

    rho2 = advance(wa, wb, keep * keep, True)

    def twice(_, rho2):
        return advance(wa, wb, advance(wb, wa, rho2, True), True)

    rho2 = lax.fori_loop(0, pairs, twice, rho2)
    rho2 = advance(wa, wb, advance(wb, wa, rho2, False), False)
    weight = 2.0 / (2.0 - rho2)
    parts = (wb[0, :, 0:n], wb[1, :, 0:n])
    left = dot2(parts, (wb[0, :, n : n + head], wb[1, :, n : n + head]))
    corner = dot2([part[head:n] for part in parts], (wb[0, :, n + head : 2 * n], wb[1, :, n + head : 2 * n]))
    left = weight * (x_ref[:, 0:head] + left)
    corner = weight * (x_ref[head:n, head:n] + corner)
    store((xh_ref, xl_ref), 0, left, corner)


def solve(n_ref, s, g_ref, x, fields, z_ref):
    members = sum(field.shape[0] for field in fields)
    mean = sum(jnp.sum(field, axis=0, keepdims=True) for field in fields) * (1.0 / members)
    pairs = [split(field - mean) for field in fields]
    anomaly = [jnp.concatenate(parts, axis=0) for parts in zip(*pairs)]
    cross = dot3(s, anomaly)
    z = dot3(x, split(cross))
    g = g_ref[...]
    left = cross - z - dot3(split(g), split(z))
    z_ref[...] = z + dot3(x, split(left))

    def refine(_, carry):
        z = z_ref[...]
        gz = lax.dot_general(g_ref[...], z, NN, precision=HIGHEST, preferred_element_type=F32)
        z_ref[...] = z + dot3(x, split(cross - z - gz))
        return carry

    lax.fori_loop(0, n_ref[0], refine, 0)
    return anomaly, mean


def gain_kernel(parts, n_ref, picks_ref, sh_ref, sl_ref, d_ref, g_ref, xh_ref, xl_ref, *refs):
    states = refs[:parts]
    z_ref, rows_ref, scratch = refs[parts:]
    fields = [state[...] for state in states]
    s = (sh_ref[...], sl_ref[...])
    anomaly, mean = solve(n_ref, s, g_ref, (xh_ref[...], xl_ref[...]), fields, z_ref)
    hot = selector(picks_ref[...], mean.shape[1], scratch)
    zt = split(select(hot, split(z_ref[...]), NT))
    base = jnp.sum(hot * mean, axis=1, keepdims=True) + dot3(zt, split(d_ref[...]))[:, 0:1]
    rows_ref[...] = base + select(hot, anomaly, NT) - 0.5 * dot3(zt, s)


def updated(field, start, s, shift, z):
    size = field.shape[0]
    return field + shift - 0.5 * dot3([h[:, start : start + size] for h in s], z, TN)


def shift_of(z, d_ref):
    return jnp.sum(z * d_ref[:, 0:1], axis=0, keepdims=True)


def update_kernel(starts, sh_ref, sl_ref, d_ref, z_ref, *refs):
    states, outs = refs[: len(starts)], refs[len(starts) :]
    z = z_ref[...]
    shift = shift_of(z, d_ref)
    s, zs = (sh_ref[...], sl_ref[...]), split(z)
    for start, state, out in zip(starts, states, outs):
        out[...] = updated(state[...], start, s, shift, zs)


def last_kernel(parts, n_ref, sh_ref, sl_ref, d_ref, g_ref, xh_ref, xl_ref, *refs):
    states, (z_ref, out_ref) = refs[:parts], refs[parts:]
    fields = [state[...] for state in states]
    s = (sh_ref[...], sl_ref[...])
    solve(n_ref, s, g_ref, (xh_ref[...], xl_ref[...]), fields, z_ref)
    z = z_ref[...]
    start = sum(field.shape[0] for field in fields[:-1])
    out_ref[...] = updated(states[-1][...], start, s, shift_of(z, d_ref), split(z))


def join_kernel(place_ref, mine_ref, theirs_ref, out_ref, both, sems):
    chunks = sems.shape[0]
    size = both.shape[0] // chunks
    column = place_ref[0]
    copies = []
    for i in range(chunks):
        at = slice(i * size, (i + 1) * size)
        mine, theirs = mine_ref[at, :], theirs_ref[at, :]
        both[at, 0, :] = jnp.where(column == 0, mine, theirs)
        both[at, 1, :] = jnp.where(column == 0, theirs, mine)
        span = pl.ds(i * size, size)
        copies.append(pltpu.make_async_copy(both.at[span], out_ref.at[span], sems.at[i]))
        copies[-1].start()
    for copy in copies:
        copy.wait()


def factor(pieces, batch, members, ids, values, var, sources):
    per_patch = values.shape[2]
    n = len(pieces) * per_patch
    outs = [
        ((n, members), BF16, VMEM),
        ((n, members), BF16, VMEM),
        ((n, 128), F32, VMEM),
        ((n, n), F32, VMEM),
        ((n, n), BF16, VMEM),
        ((n, n), BF16, VMEM),
        ((1,), jnp.int32, SMEM),
    ]
    scratch = [
        pltpu.VMEM((128, 128), F32),
        pltpu.VMEM((n, n), F32),
        pltpu.VMEM((n, n), F32),
        pltpu.VMEM((2, n, 2 * n), BF16),
        pltpu.VMEM((2, n, 2 * n), BF16),
    ]
    kernel = functools.partial(factor_kernel, pieces, batch, members)
    args = [ids, values, var, *sources]
    flops = 6 * n * n * members + 60 * n * n * n
    return call(kernel, outs, [SMEM] + [VMEM] * (2 + len(sources)), args, scratch, flops)


def gain(picks, factored, states):
    sh, sl, d, g, xh, xl, more = factored
    n, members = sh.shape
    kernel = functools.partial(gain_kernel, len(states))
    outs = [((n, states[0].shape[1]), F32, VMEM), ((picks.shape[1], members), F32, VMEM)]
    ins = [SMEM] + [VMEM] * (7 + len(states))
    args = [more, picks, sh, sl, d, g, xh, xl, *states]
    flops = 8 * n * members * states[0].shape[1]
    return call(kernel, outs, ins, args, [pltpu.VMEM((8, 128), jnp.int32)], flops)


def update(factored, z, states, starts):
    sh, sl, d = factored[:3]
    kernel = functools.partial(update_kernel, starts)
    outs = [(state.shape, F32, VMEM) for state in states]
    flops = 6 * sh.shape[0] * sh.shape[1] * z.shape[1]
    return call(kernel, outs, [VMEM] * (4 + len(states)), [sh, sl, d, z, *states], (), flops)


def last(factored, states):
    sh, sl, d, g, xh, xl, more = factored
    kernel = functools.partial(last_kernel, len(states))
    n, width = sh.shape[0], states[0].shape[1]
    outs = [((n, width), F32, VMEM), (states[-1].shape, F32, VMEM)]
    args = [more, sh, sl, d, g, xh, xl, *states]
    flops = 12 * sh.shape[0] * sh.shape[1] * width
    return call(kernel, outs, [SMEM] + [VMEM] * (6 + len(states)), args, (), flops)


def rings(size):
    up = [(i, (i + 1) % size) for i in range(size)]
    return up, [(j, i) for i, j in up]


BOTH = ("region", "member")


def permute(x, moves, regions):
    table = []
    for region in range(regions):
        for column in range(2):
            pair, parity, to = moves(region // 2, region % 2, column)
            pair %= regions // 2
            table.append((region * 2 + column, (pair * 2 + parity) * 2 + to))
    return lax.ppermute(x, BOTH, table)


def paired(state, neighbours, obs_cell, obs_values, obs_var):
    half, _, cells = state.shape
    members = 2 * half
    regions = lax.axis_size("region")
    region, column = lax.axis_index("region"), lax.axis_index("member")
    parity = region % 2
    mate = region + 1 - 2 * parity
    outer = (region + regions + 2 * parity - 1) % regions
    own = region * 2 + column
    place = column.astype(jnp.int32)[None]
    links = lax.dynamic_index_in_dim(neighbours, own, 0, keepdims=False)
    around = (region, mate, outer)
    ids_first = [r * 2 + p for r in around for p in (0, 1)]
    ids_next = [r * 2 + p for r in around for p in (column, 1 - column)]
    ids_first = jnp.concatenate([jnp.stack(ids_first + [own]).astype(jnp.int32), links])
    ids_next = jnp.concatenate([jnp.stack(ids_next + [own]).astype(jnp.int32), links])

    def across(x):
        return permute(x, lambda c, q, m: (c, q, 1 - m), regions)

    def beside(x):
        return permute(x, lambda c, q, m: (c, 1 - q, m), regions)

    def outside(x):
        return permute(x, lambda c, q, m: (c + 2 * q - 1, 1 - q, m), regions)

    anywhere = pl.BlockSpec(memory_space=pl.ANY)
    (rows,) = call(
        pick_kernel,
        [((2, obs_cell.shape[2], half), F32, VMEM)],
        [SMEM, anywhere, anywhere],
        [(region * 2).astype(jnp.int32)[None], obs_cell, state],
        [
            pltpu.VMEM(obs_cell.shape, jnp.int32),
            pltpu.VMEM(state.shape, F32),
            pltpu.VMEM((8, 128), jnp.int32),
            pltpu.VMEM((2, half, cells), F32),
            pltpu.SemaphoreType.DMA((3,)),
        ],
        limit=56,
    )
    other = across(rows)
    sources = [rows, beside(rows), outside(rows), other, beside(other), outside(other)]
    pieces = [[(i, (p,), 0), (3 + i, (p,), 1)] for i in range(3) for p in range(2)]
    shape = ((half, cells), F32, VMEM)
    keep, send, values, var = call(
        sort_kernel,
        [shape, shape, (obs_values.shape, F32, VMEM), (obs_var.shape, F32, VMEM)],
        [SMEM, anywhere, anywhere, VMEM, anywhere],
        [place, obs_values, obs_var, state, other],
        [pltpu.SemaphoreType.DMA((2,))],
    )
    states = [keep, across(send)]
    factored = factor(pieces, 0, members, ids_first, values, var, sources)
    everything = slice(None)
    low, high = (everything, slice(0, half)), (everything, slice(half, members))
    pieces = []
    for i in range(3):
        pieces += [[(i, low, 0), (i, high, 1)], [(3 + i, high, 0), (3 + i, low, 1)]]
    for batch in range(1, NBATCH):
        picks = lax.dynamic_slice_in_dim(obs_cell[:, batch, :], own, 1, 0)
        z, rows = gain(picks, factored, states)
        other = across(rows)
        out = outside(rows)
        sources = [rows, beside(rows), out, other, beside(other), across(out)]
        states = update(factored, z, states, (0, half))
        factored = factor(pieces, batch, members, ids_next, values, var, sources)
    z, theirs = last(factored, states)
    theirs = across(theirs)
    (mine,) = update(factored, z, states[:1], (0,))
    return pl.pallas_call(
        join_kernel,
        out_shape=jax.ShapeDtypeStruct(state.shape, F32),
        in_specs=[SMEM, VMEM, VMEM],
        out_specs=anywhere,
        scratch_shapes=[pltpu.VMEM(state.shape, F32), pltpu.SemaphoreType.DMA((4,))],
        compiler_params=pltpu.CompilerParams(vmem_limit_bytes=48 * 1024 * 1024),
    )(place, mine, theirs)


def general(state, neighbours, obs_cell, obs_values, obs_var):
    ensemble = lax.all_to_all(state, "member", split_axis=1, concat_axis=0, tiled=True)
    members, owned, cells = ensemble.shape
    regions = lax.axis_size("region")
    region_patches = owned * lax.axis_size("member")
    region = lax.axis_index("region")
    first = region * region_patches + lax.axis_index("member") * owned
    up, down = rings(regions)
    fields = [ensemble[:, p, :] for p in range(owned)]
    grid = jnp.arange(cells, dtype=jnp.int32)
    for batch in range(NBATCH):
        picks = lax.dynamic_slice_in_dim(obs_cell, first, owned, 0)[:, batch, :]
        hot = (picks[:, :, None] == grid[None, None, :]).astype(F32)
        own_rows = jnp.einsum("poc,pkc->pok", hot, jnp.stack(fields), precision=HIGHEST)
        region_rows = lax.all_gather(own_rows, "member", axis=0, tiled=True)
        before = lax.ppermute(region_rows, "region", up)
        after = lax.ppermute(region_rows, "region", down)
        beside = jnp.concatenate([before, region_rows, after], axis=0)
        new = []
        for p in range(owned):
            own = first + p
            links = lax.dynamic_index_in_dim(neighbours, own, 0, keepdims=False)
            ids = jnp.concatenate([own[None], links]).astype(jnp.int32)
            table = jnp.concatenate([ids, own[None], links]).astype(jnp.int32)
            home = (ids // region_patches - region + 1) % regions
            rows = jnp.take(beside, home * region_patches + ids % region_patches, axis=0)
            pieces = [[(0, (i,), 0)] for i in range(ids.shape[0])]
            factored = factor(pieces, batch, members, table, obs_values, obs_var, [rows])
            new.append(last(factored, [fields[p]])[1])
        fields = new
    ensemble = jnp.stack(fields, axis=1)
    return lax.all_to_all(ensemble, "member", split_axis=0, concat_axis=1, tiled=True)


def on_device(state, neighbours, obs_cell, obs_values, obs_var):
    patches, links = state.shape[1], neighbours.shape[1]
    even = lax.axis_size("region") % 2 == 0
    if even and patches == 2 and lax.axis_size("member") == 2 and links + 1 == 3 * patches:
        return paired(state, neighbours, obs_cell, obs_values, obs_var)
    return general(state, neighbours, obs_cell, obs_values, obs_var)


def solution(mesh):
    in_specs = (P("member", "region", None), P(), P(), P(), P())
    out_specs = P("member", "region", None)
    return jax.shard_map(
        on_device, mesh=mesh, in_specs=in_specs, out_specs=out_specs, check_vma=False
    )
```

profile of v0, /device:TPU:0, one launch (start us, length us, event | category | flops | bytes accessed | tf_op | source)
XLA Modules:
  0.0 80.3 jit_solution(1384279314935292677)
XLA Ops:
  0.0 2.8 %shard_map.55.refs_0_ = f32[2,64,512]{2,1,0:T(8,128)} custom-call(s32[1]{0:T(128)} %bitcast.7.first_ref, s32[32,2,64]{2,1,0:T(2,128)} %cells_hbm.1, f32[512,2,256]{2,1,0:T(2,128)} %state_ref.1), custom_call_target="tpu_custom_call" | custom-call | bytes 1327108 | tf_op jit(solution)/shard_map/pallas_call | solution.py:29
  2.9 3.0 %collective-permute-start = (f32[2,64,512]{2,1,0:T(8,128)}, f32[2,64,512]{2,1,0:T(8,128)S(1)}, u32[]{:S(2)}, u32[]{:S(2)}) collective-permute-start(f32[2,64,512]{2,1,0:T(8,128)} %shard_map.55.refs_0_), channel_id=1, source_target_pairs={{0,1},{1,0},{2,3},{3,2},{4,5},{5,4},{6,7},{7,6},{8,9},{9,8},{10,11... | collective-permute-start | bytes 786440 | tf_op jit(solution)/shard_map/ppermute | solution.py:397
  5.9 3.7 %collective-permute-start.2 = (f32[2,64,512]{2,1,0:T(8,128)}, f32[2,64,512]{2,1,0:T(8,128)S(1)}, u32[]{:S(2)}, u32[]{:S(2)}) collective-permute-start(f32[2,64,512]{2,1,0:T(8,128)} %shard_map.55.refs_0_), channel_id=1, source_target_pairs={{0,30},{1,31},{2,4},{3,5},{4,2},{5,3},{6,8},{7,9},{8,6},{9,7},{10,... | collective-permute-start | bytes 786440 | tf_op jit(solution)/shard_map/ppermute | solution.py:397
  9.6 2.8 %collective-permute-done.refs_0_.refs_3_ = f32[2,64,512]{2,1,0:T(8,128)S(1)} collective-permute-done((f32[2,64,512]{2,1,0:T(8,128)}, f32[2,64,512]{2,1,0:T(8,128)S(1)}, u32[]{:S(2)}, u32[]{:S(2)}) %collective-permute-start) | collective-permute-done | bytes 262176 | tf_op jit(solution)/shard_map/ppermute | solution.py:397
  12.4 3.3 %collective-permute-start.4 = (f32[2,64,512]{2,1,0:T(8,128)S(1)}, f32[2,64,512]{2,1,0:T(8,128)}, u32[]{:S(2)}, u32[]{:S(2)}) collective-permute-start(f32[2,64,512]{2,1,0:T(8,128)S(1)} %collective-permute-done.refs_0_.refs_3_), channel_id=1, source_target_pairs={{0,30},{1,31},{2,4},{3,5},{4,2},{5,3},{6,8},{7,9},{8,6},{9,7},{10,... | collective-permute-start | bytes 786440 | tf_op jit(solution)/shard_map/ppermute | solution.py:397
  15.8 1.5 %shard_map.56 = (f32[512,256]{1,0:T(8,128)S(1)}, f32[512,256]{1,0:T(8,128)}, f32[32,2,64]{2,1,0:T(2,128)S(1)}, f32[32,2,64]{2,1,0:T(2,128)S(1)}) custom-call(s32[1]{0:T(128)} %bitcast.place_ref, f32[32,2,64]{2,1,0:T(2,128)S(1)} %copy-done.3, f32[32,2,64]{2,1,0:T(2,128)S(1)} %copy-done.4, f32[512,2,256]{2,1,0:T(2,128)S(1)} %copy-done.1, ...), custom_call_target="tpu_custom_call" | custom-call | bytes 2424836 | tf_op jit(solution)/shard_map/pallas_call | solution.py:29
  17.3 0.0 copy-start.9
  17.3 1.6 %collective-permute-start.5 = (f32[512,256]{1,0:T(8,128)}, f32[512,256]{1,0:T(8,128)S(1)}, u32[]{:S(2)}, u32[]{:S(2)}) collective-permute-start(f32[512,256]{1,0:T(8,128)} %get-tuple-element.39), channel_id=1, source_target_pairs={{0,1},{1,0},{2,3},{3,2},{4,5},{5,4},{6,7},{7,6},{8,9},{9,8},{10,11... | collective-permute-start | bytes 1572872 | tf_op jit(solution)/shard_map/ppermute | solution.py:397
  18.9 0.2 dynamic-slice_reduce_fusion
  19.1 0.1 concatenate.7.ids_ref
  19.2 0.7 copy-done.5
  19.9 0.7 copy-done.7
  20.6 0.5 collective-permute-done.4.refs_5_
  21.1 0.9 %copy-done.6 = f32[2,64,512]{2,1,0:T(8,128)S(1)} copy-done((f32[2,64,512]{2,1,0:T(8,128)S(1)}, f32[2,64,512]{2,1,0:T(8,128)}, u32[]{:S(2)}) %copy-start.6) | copy-done | bytes 262168
  22.1 0.9 %copy-done.8 = f32[2,64,512]{2,1,0:T(8,128)S(1)} copy-done((f32[2,64,512]{2,1,0:T(8,128)S(1)}, f32[2,64,512]{2,1,0:T(8,128)}, u32[]{:S(2)}) %copy-start.8) | copy-done | bytes 262168
  23.0 8.1 %shard_map.57 = (bf16[384,1024]{1,0:T(8,128)(2,1)S(1)}, bf16[384,1024]{1,0:T(8,128)(2,1)S(1)}, f32[384,128]{1,0:T(8,128)S(1)}, f32[384,384]{1,0:T(8,128)S(1)}, b...) custom-call(s32[12]{0:T(128)S(1)} %concatenate.7.ids_ref, ...), custom_call_target="tpu_custom_call" | custom-call | flops 4303355904 | bytes 4554804 | tf_op jit(solution)/shard_map/pallas_call | solution.py:29
  31.2 0.7 collective-permute-done.5.refs_1_
  31.9 5.1 %shard_map.58 = (f32[384,256]{1,0:T(8,128)S(1)}, f32[64,1024]{1,0:T(8,128)S(1)}) custom-call(s32[1]{0:T(128)} %get-tuple-element.31.n_ref, s32[1,64]{1,0:T(1,128)S(1)} %dynamic-slice_bitcast_fusion.picks_ref, bf16[384,1024]{1,0:T(8,128)(2,1)S(1)} %get-tuple-element.32.sh_ref, bf16[384,1024]{1,0:T(8,128)(2,1)S(1)} %get-tuple-element.33.sl_ref, ...), custom_call_target="tpu_custom_call" | custom-call | flops 805306368 | bytes 4653316 | tf_op jit(solution)/shard_map/pallas_call | solution.py:29
  37.0 1.6 %collective-permute-start.8 = (f32[64,1024]{1,0:T(8,128)S(1)}, f32[64,1024]{1,0:T(8,128)}, u32[]{:S(2)}, u32[]{:S(2)}) collective-permute-start(f32[64,1024]{1,0:T(8,128)S(1)} %get-tuple-element.40.refs_0_), channel_id=1, source_target_pairs={{0,1},{1,0},{2,3},{3,2},{4,5},{5,4},{6,7},{7,6},{8,9},{9,8},{10,11... | collective-permute-start | bytes 786440 | tf_op jit(solution)/shard_map/ppermute | solution.py:397
  38.5 2.4 %collective-permute-start.7 = (f32[64,1024]{1,0:T(8,128)S(1)}, f32[64,1024]{1,0:T(8,128)}, u32[]{:S(2)}, u32[]{:S(2)}) collective-permute-start(f32[64,1024]{1,0:T(8,128)S(1)} %get-tuple-element.40.refs_0_), channel_id=1, source_target_pairs={{0,30},{1,31},{2,4},{3,5},{4,2},{5,3},{6,8},{7,9},{8,6},{9,7},{10,... | collective-permute-start | bytes 786440 | tf_op jit(solution)/shard_map/ppermute | solution.py:397
  40.9 4.1 %collective-permute-done.8.refs_3_ = f32[64,1024]{1,0:T(8,128)} collective-permute-done((f32[64,1024]{1,0:T(8,128)S(1)}, f32[64,1024]{1,0:T(8,128)}, u32[]{:S(2)}, u32[]{:S(2)}) %collective-permute-start.8) | collective-permute-done | bytes 262176 | tf_op jit(solution)/shard_map/ppermute | solution.py:397
  45.0 2.1 %collective-permute-done.7.refs_2_ = f32[64,1024]{1,0:T(8,128)} collective-permute-done((f32[64,1024]{1,0:T(8,128)S(1)}, f32[64,1024]{1,0:T(8,128)}, u32[]{:S(2)}, u32[]{:S(2)}) %collective-permute-start.7) | collective-permute-done | bytes 262176 | tf_op jit(solution)/shard_map/ppermute | solution.py:397
  47.1 0.5 collective-permute-start.10
  47.6 0.1 concatenate.6.ids_ref
  47.7 0.9 %shard_map.60 = (f32[512,256]{1,0:T(8,128)S(1)}, f32[512,256]{1,0:T(8,128)S(1)}) custom-call(bf16[384,1024]{1,0:T(8,128)(2,1)S(1)} %get-tuple-element.32.sh_ref, bf16[384,1024]{1,0:T(8,128)(2,1)S(1)} %get-tuple-element.33.sl_ref, f32[384,128]{1,0:T(8,128)S(1)} %get-tuple-element.34.d_ref, f32[384,256]{1,0:T(8,128)S(1)} %get-tuple-element.48.z_ref, ...), custom_call_target="tpu_custom_call" | custom-call | flops 603979776 | bytes 4259840 | tf_op jit(solution)/shard_map/pallas_call | solution.py:29
  48.7 5.4 %collective-permute-done.10.refs_5_ = f32[64,1024]{1,0:T(8,128)} collective-permute-done((f32[64,1024]{1,0:T(8,128)}, f32[64,1024]{1,0:T(8,128)}, u32[]{:S(2)}, u32[]{:S(2)}) %collective-permute-start.10) | collective-permute-done | bytes 262176 | tf_op jit(solution)/shard_map/ppermute | solution.py:397
  54.1 8.3 %shard_map.59 = (bf16[384,1024]{1,0:T(8,128)(2,1)S(1)}, bf16[384,1024]{1,0:T(8,128)(2,1)S(1)}, f32[384,128]{1,0:T(8,128)S(1)}, f32[384,384]{1,0:T(8,128)S(1)}, b...) custom-call(s32[12]{0:T(128)S(1)} %concatenate.6.ids_ref, ...), custom_call_target="tpu_custom_call" | custom-call | flops 4303355904 | bytes 4554804 | tf_op jit(solution)/shard_map/pallas_call | solution.py:29
  62.4 4.4 %shard_map.61 = (f32[384,256]{1,0:T(8,128)S(1)}, f32[512,256]{1,0:T(8,128)S(1)}) custom-call(s32[1]{0:T(128)} %get-tuple-element.44.n_ref, bf16[384,1024]{1,0:T(8,128)(2,1)S(1)} %get-tuple-element.41.sh_ref, bf16[384,1024]{1,0:T(8,128)(2,1)S(1)} %get-tuple-element.42.sl_ref, f32[384,128]{1,0:T(8,128)S(1)} %get-tuple-element.43.d_ref, ...), custom_call_target="tpu_custom_call" | custom-call | flops 1207959552 | bytes 4915204 | tf_op jit(solution)/shard_map/pallas_call | solution.py:29
  66.8 1.6 %collective-permute-start.11 = (f32[512,256]{1,0:T(8,128)S(1)}, f32[512,256]{1,0:T(8,128)S(1)}, u32[]{:S(2)}, u32[]{:S(2)}) collective-permute-start(f32[512,256]{1,0:T(8,128)S(1)} %get-tuple-element.52), channel_id=1, source_target_pairs={{0,1},{1,0},{2,3},{3,2},{4,5},{5,4},{6,7},{7,6},{8,9},{9,8},{10,11... | collective-permute-start | bytes 1572872 | tf_op jit(solution)/shard_map/ppermute | solution.py:397
  68.4 0.6 shard_map.62.mine_ref
  69.0 10.0 %collective-permute-done.11.theirs_ref = f32[512,256]{1,0:T(8,128)S(1)} collective-permute-done((f32[512,256]{1,0:T(8,128)S(1)}, f32[512,256]{1,0:T(8,128)S(1)}, u32[]{:S(2)}, u32[]{:S(2)}) %collective-permute-start.11) | collective-permute-done | bytes 524320 | tf_op jit(solution)/shard_map/ppermute | solution.py:397
  79.0 1.1 %shard_map.63 = f32[512,2,256]{2,1,0:T(2,128)} custom-call(s32[1]{0:T(128)} %bitcast.place_ref, f32[512,256]{1,0:T(8,128)S(1)} %shard_map.62.mine_ref, f32[512,256]{1,0:T(8,128)S(1)} %collective-permute-done.11.theirs_ref), custom_call_target="tpu_custom_call" | custom-call | tf_op jit(solution)/shard_map/pallas_call | solution.py:470
  (26 shorter events, 0.1 us)
Async XLA Ops:
  0.0 18.9 %copy-start = (s32[32,5]{0,1:T(8,128)S(1)}, s32[32,5]{0,1:T(8,128)}, u32[]{:S(2)}) copy-start(s32[32,5]{0,1:T(8,128)} %param.6) | copy-start | bytes 1924
  0.0 15.7 %copy-start.1 = (f32[512,2,256]{2,1,0:T(2,128)S(1)}, f32[512,2,256]{2,1,0:T(2,128)}, u32[]{:S(2)}) copy-start(f32[512,2,256]{2,1,0:T(2,128)} %state_ref.1) | copy-start | bytes 3145732
  0.0 15.7 %copy-start.3 = (f32[32,2,64]{2,1,0:T(2,128)S(1)}, f32[32,2,64]{2,1,0:T(2,128)}, u32[]{:S(2)}) copy-start(f32[32,2,64]{2,1,0:T(2,128)} %values_hbm.1) | copy-start | bytes 49156
  0.0 15.7 %copy-start.4 = (f32[32,2,64]{2,1,0:T(2,128)S(1)}, f32[32,2,64]{2,1,0:T(2,128)}, u32[]{:S(2)}) copy-start(f32[32,2,64]{2,1,0:T(2,128)} %var_hbm.1) | copy-start | bytes 49156
  2.9 9.5 %collective-permute-start = (f32[2,64,512]{2,1,0:T(8,128)}, f32[2,64,512]{2,1,0:T(8,128)S(1)}, u32[]{:S(2)}, u32[]{:S(2)}) collective-permute-start(f32[2,64,512]{2,1,0:T(8,128)} %shard_map.55.refs_0_), channel_id=1, source_target_pairs={{0,1},{1,0},{2,3},{3,2},{4,5},{5,4},{6,7},{7,6},{8,9},{9,8},{10,11... | collective-permute-start | bytes 786440 | tf_op jit(solution)/shard_map/ppermute | solution.py:397
  5.9 13.3 %collective-permute-start.2 = (f32[2,64,512]{2,1,0:T(8,128)}, f32[2,64,512]{2,1,0:T(8,128)S(1)}, u32[]{:S(2)}, u32[]{:S(2)}) collective-permute-start(f32[2,64,512]{2,1,0:T(8,128)} %shard_map.55.refs_0_), channel_id=1, source_target_pairs={{0,30},{1,31},{2,4},{3,5},{4,2},{5,3},{6,8},{7,9},{8,6},{9,7},{10,... | collective-permute-start | bytes 786440 | tf_op jit(solution)/shard_map/ppermute | solution.py:397
  9.6 10.3 %collective-permute-start.1 = (f32[2,64,512]{2,1,0:T(8,128)}, f32[2,64,512]{2,1,0:T(8,128)S(1)}, u32[]{:S(2)}, u32[]{:S(2)}) collective-permute-start(f32[2,64,512]{2,1,0:T(8,128)} %shard_map.55.refs_0_), channel_id=1, source_target_pairs={{0,2},{1,3},{2,0},{3,1},{4,6},{5,7},{6,4},{7,5},{8,10},{9,11},{10,... | collective-permute-start | bytes 786440 | tf_op jit(solution)/shard_map/ppermute | solution.py:397
  12.4 8.7 %collective-permute-start.4 = (f32[2,64,512]{2,1,0:T(8,128)S(1)}, f32[2,64,512]{2,1,0:T(8,128)}, u32[]{:S(2)}, u32[]{:S(2)}) collective-permute-start(f32[2,64,512]{2,1,0:T(8,128)S(1)} %collective-permute-done.refs_0_.refs_3_), channel_id=1, source_target_pairs={{0,30},{1,31},{2,4},{3,5},{4,2},{5,3},{6,8},{7,9},{8,6},{9,7},{10,... | collective-permute-start | bytes 786440 | tf_op jit(solution)/shard_map/ppermute | solution.py:397
  15.7 5.4 %collective-permute-start.3 = (f32[2,64,512]{2,1,0:T(8,128)S(1)}, f32[2,64,512]{2,1,0:T(8,128)}, u32[]{:S(2)}, u32[]{:S(2)}) collective-permute-start(f32[2,64,512]{2,1,0:T(8,128)S(1)} %collective-permute-done.refs_0_.refs_3_), channel_id=1, source_target_pairs={{0,2},{1,3},{2,0},{3,1},{4,6},{5,7},{6,4},{7,5},{8,10},{9,11},{10,... | collective-permute-start | bytes 786440 | tf_op jit(solution)/shard_map/ppermute | solution.py:397
  15.8 5.4 %copy-start.2 = (f32[2,64,512]{2,1,0:T(8,128)S(1)}, f32[2,64,512]{2,1,0:T(8,128)}, u32[]{:S(2)}) copy-start(f32[2,64,512]{2,1,0:T(8,128)} %shard_map.55.refs_0_) | copy-start | bytes 786436
  17.3 1.6 %copy-start.9 = (s32[32,2,64]{2,1,0:T(2,128)S(1)}, s32[32,2,64]{2,1,0:T(2,128)}, u32[]{:S(2)}) copy-start(s32[32,2,64]{2,1,0:T(2,128)} %cells_hbm.1) | copy-start | bytes 49156
  17.3 14.6 %collective-permute-start.5 = (f32[512,256]{1,0:T(8,128)}, f32[512,256]{1,0:T(8,128)S(1)}, u32[]{:S(2)}, u32[]{:S(2)}) collective-permute-start(f32[512,256]{1,0:T(8,128)} %get-tuple-element.39), channel_id=1, source_target_pairs={{0,1},{1,0},{2,3},{3,2},{4,5},{5,4},{6,7},{7,6},{8,9},{9,8},{10,11... | collective-permute-start | bytes 1572872 | tf_op jit(solution)/shard_map/ppermute | solution.py:397
  19.2 0.7 copy-start.5
  19.9 0.7 copy-start.7
  21.1 1.0 %copy-start.6 = (f32[2,64,512]{2,1,0:T(8,128)S(1)}, f32[2,64,512]{2,1,0:T(8,128)}, u32[]{:S(2)}) copy-start(f32[2,64,512]{2,1,0:T(8,128)} %copy-done.5) | copy-start | bytes 786436
  22.1 0.9 %copy-start.8 = (f32[2,64,512]{2,1,0:T(8,128)S(1)}, f32[2,64,512]{2,1,0:T(8,128)}, u32[]{:S(2)}) copy-start(f32[2,64,512]{2,1,0:T(8,128)} %copy-done.7) | copy-start | bytes 786436
  37.0 8.1 %collective-permute-start.8 = (f32[64,1024]{1,0:T(8,128)S(1)}, f32[64,1024]{1,0:T(8,128)}, u32[]{:S(2)}, u32[]{:S(2)}) collective-permute-start(f32[64,1024]{1,0:T(8,128)S(1)} %get-tuple-element.40.refs_0_), channel_id=1, source_target_pairs={{0,1},{1,0},{2,3},{3,2},{4,5},{5,4},{6,7},{7,6},{8,9},{9,8},{10,11... | collective-permute-start | bytes 786440 | tf_op jit(solution)/shard_map/ppermute | solution.py:397
  38.5 8.6 %collective-permute-start.7 = (f32[64,1024]{1,0:T(8,128)S(1)}, f32[64,1024]{1,0:T(8,128)}, u32[]{:S(2)}, u32[]{:S(2)}) collective-permute-start(f32[64,1024]{1,0:T(8,128)S(1)} %get-tuple-element.40.refs_0_), channel_id=1, source_target_pairs={{0,30},{1,31},{2,4},{3,5},{4,2},{5,3},{6,8},{7,9},{8,6},{9,7},{10,... | collective-permute-start | bytes 786440 | tf_op jit(solution)/shard_map/ppermute | solution.py:397
  40.9 7.8 %collective-permute-start.6 = (f32[64,1024]{1,0:T(8,128)S(1)}, f32[64,1024]{1,0:T(8,128)}, u32[]{:S(2)}, u32[]{:S(2)}) collective-permute-start(f32[64,1024]{1,0:T(8,128)S(1)} %get-tuple-element.40.refs_0_), channel_id=1, source_target_pairs={{0,2},{1,3},{2,0},{3,1},{4,6},{5,7},{6,4},{7,5},{8,10},{9,11},{10,... | collective-permute-start | bytes 786440 | tf_op jit(solution)/shard_map/ppermute | solution.py:397
  45.0 3.6 %collective-permute-start.9 = (f32[64,1024]{1,0:T(8,128)}, f32[64,1024]{1,0:T(8,128)}, u32[]{:S(2)}, u32[]{:S(2)}) collective-permute-start(f32[64,1024]{1,0:T(8,128)} %collective-permute-done.8.refs_3_), channel_id=1, source_target_pairs={{0,2},{1,3},{2,0},{3,1},{4,6},{5,7},{6,4},{7,5},{8,10},{9,11},{10,... | collective-permute-start | bytes 786440 | tf_op jit(solution)/shard_map/ppermute | solution.py:397
  47.1 7.0 %collective-permute-start.10 = (f32[64,1024]{1,0:T(8,128)}, f32[64,1024]{1,0:T(8,128)}, u32[]{:S(2)}, u32[]{:S(2)}) collective-permute-start(f32[64,1024]{1,0:T(8,128)} %collective-permute-done.7.refs_2_), channel_id=1, source_target_pairs={{0,1},{1,0},{2,3},{3,2},{4,5},{5,4},{6,7},{7,6},{8,9},{9,8},{10,11... | collective-permute-start | bytes 786440 | tf_op jit(solution)/shard_map/ppermute | solution.py:397
  66.8 12.2 %collective-permute-start.11 = (f32[512,256]{1,0:T(8,128)S(1)}, f32[512,256]{1,0:T(8,128)S(1)}, u32[]{:S(2)}, u32[]{:S(2)}) collective-permute-start(f32[512,256]{1,0:T(8,128)S(1)} %get-tuple-element.52), channel_id=1, source_target_pairs={{0,1},{1,0},{2,3},{3,2},{4,5},{5,4},{6,7},{7,6},{8,9},{9,8},{10,11... | collective-permute-start | bytes 1572872 | tf_op jit(solution)/shard_map/ppermute | solution.py:397
where the time goes:
time: 80.5 us; the launch traced here: 80.3 us
  Pallas kernels  32.9 us (41%)
  waiting for transfers between devices  25.7 us (32%)
  starting transfers between devices  17.7 us (22%)
  local copies, waits for them, and re-layouts  3.7 us (5%)
    pallas_call x8, Pallas kernels, call(): pl.pallas_call(kernel, out_shape=shapes, in_specs=ins, out_specs=[space f...  31.8 us
    ppermute x12, waiting for transfers between devices, permute(): return lax.ppermute(x, BOTH, table)  25.7 us
    ppermute x12, starting transfers between devices, permute(): return lax.ppermute(x, BOTH, table)  17.7 us
    unnamed x20, local copies, waits for them, and re-layouts  3.32 us
  transfers between devices with their start and end apart: 12, of which 7 were waited for; matrix products, arithmetic and copies ran while one was open for 0% of the time, Pallas kernels for 14%

commit v1 on v0

--- a/solution.py
+++ b/solution.py
@@ -18,11 +18,12 @@
 NT = (((1,), (1,)), ((), ()))
 TN = (((0,), (0,)), ((), ()))
 RESIDUAL = 1e-3
+FACTOR_LIMIT = 24
 MOST_STEPS = 15
 TILE = 256
 
 
-def call(kernel, outs, ins, args, scratch=(), flops=0, limit=48):
+def call(kernel, outs, ins, args, scratch=(), flops=0, limit=16):
     shapes = [jax.ShapeDtypeStruct(shape, dtype) for shape, dtype, _ in outs]
     moved = sum(math.prod(s.shape) * s.dtype.itemsize for s in shapes)
     moved += sum(a.size * a.dtype.itemsize for a in args)
@@ -53,11 +54,6 @@
     return dot(lhs, rhs, dims)
 
 
-def dot2(a, b, dims=NN):
-    (left,), (right,) = dims[0]
-    return dot(jnp.concatenate([a[0], a[0]], axis=left), jnp.concatenate(b, axis=right), dims)
-
-
 def select(hot, parts, dims):
     (left,), (right,) = dims[0]
     hot = hot.astype(BF16)
@@ -96,24 +92,12 @@
     return jnp.transpose(hot)[0:per_patch, :]
 
 
-def pick_kernel(first_ref, cells_hbm, state_hbm, rows_ref, cells_ref, state_ref, scratch, field_ref, sems):
-    members, patches, cells = state_ref.shape
-    chunks = sems.shape[0] - 1
-    size = members // chunks
-    spans = [pl.ds(i * size, size) for i in range(chunks)]
-    first = pltpu.make_async_copy(cells_hbm, cells_ref, sems.at[chunks])
-    first.start()
-    copies = []
-    for i, span in enumerate(spans):
-        copies.append(pltpu.make_async_copy(state_hbm.at[span], state_ref.at[span], sems.at[i]))
-        copies[-1].start()
-    first.wait()
-    hots = [selector(cells_ref[pl.ds(first_ref[0] + p, 1), 0, :], cells, scratch) for p in range(patches)]
-    for i, span in enumerate(spans):
-        copies[i].wait()
-        for p in range(patches):
-            field_ref[p, span] = state_ref[span, p, :]
-            rows_ref[p, :, i * size : (i + 1) * size] = select(hots[p], split_all(field_ref[p, span]), NT)
+def pick_kernel(picks_ref, state_ref, rows_ref, scratch, field_ref):
+    patches, cells = state_ref.shape[1:]
+    for p in range(patches):
+        field_ref[p] = state_ref[:, p, :]
+        hot = selector(picks_ref[p : p + 1, :], cells, scratch)
+        rows_ref[p] = select(hot, split_all(field_ref[p]), NT)
 
 
 def sort_kernel(place_ref, values_hbm, var_hbm, state_ref, *refs):
@@ -179,7 +163,7 @@
     size = square[0, 0]
     limits = step_limits()
     pairs = jnp.int32(0)
-    for k in range(5, MOST_STEPS - 2, 2):
+    for k in range(7, MOST_STEPS - 2, 2):
         limit = limits[k] * (1.0 - 1e-4)
         pairs = pairs + (size > limit * limit).astype(jnp.int32)
     n_ref[0] = (size > 1.6e7).astype(jnp.int32) + (size > 1e8).astype(jnp.int32)
@@ -213,17 +197,16 @@
     corner = dot3([part[head:n] for part in parts], [part[:, head:n] for part in parts])
     store((wa.at[0], wa.at[1]), 0, *corner_of(weight, keep, left, corner))
 
-    def advance(source, target, rho2, exact):
+    def advance(source, target, rho2):
         weight = 2.0 / (2.0 - rho2)
         keep = 0.5 * rho2 * weight
         parts = (source[0, :, 0:n], source[1, :, 0:n])
         ends = [jnp.concatenate([source[i, :, head:n], source[i, :, n + head : 2 * n]], axis=1) for i in (0, 1)]
-        times = dot3 if exact else dot2
-        left = times(parts, (source[0, :, 0:head], source[1, :, 0:head]))
-        corners = times([part[head:n] for part in parts], ends)
+        left = dot3(parts, (source[0, :, 0:head], source[1, :, 0:head]))
+        corners = dot3([part[head:n] for part in parts], ends)
         both = (target.at[0], target.at[1])
         store(both, 0, *corner_of(weight, keep, left, corners[:, 0:tail]))
-        left = dot2(parts, (source[0, :, n : n + head], source[1, :, n : n + head]))
+        left = dot3(parts, (source[0, :, n : n + head], source[1, :, n : n + head]))
         left = weight * (x_ref[:, 0:head] + left)
         corner = weight * (x_ref[head:n, head:n] + corners[:, tail : 2 * tail])
         x_ref[:, 0:head] = left
@@ -231,17 +214,17 @@
         store(both, n, left, corner)
         return keep * keep
 
-    rho2 = advance(wa, wb, keep * keep, True)
-
     def twice(_, rho2):
-        return advance(wa, wb, advance(wb, wa, rho2, True), True)
-
-    rho2 = lax.fori_loop(0, pairs, twice, rho2)
-    rho2 = advance(wa, wb, advance(wb, wa, rho2, False), False)
+        return advance(wb, wa, advance(wa, wb, rho2))
+
+    rho2 = lax.fori_loop(0, pairs, twice, keep * keep)
+    for source, target in ((wa, wb), (wb, wa)) * 2 + ((wa, wb),):
+        rho2 = advance(source, target, rho2)
     weight = 2.0 / (2.0 - rho2)
     parts = (wb[0, :, 0:n], wb[1, :, 0:n])
-    left = dot2(parts, (wb[0, :, n : n + head], wb[1, :, n : n + head]))
-    corner = dot2([part[head:n] for part in parts], (wb[0, :, n + head : 2 * n], wb[1, :, n + head : 2 * n]))
+    left = dot3(parts, (wb[0, :, n : n + head], wb[1, :, n : n + head]))
+    ends = [wb[i, :, n + head : 2 * n] for i in (0, 1)]
+    corner = dot3([part[head:n] for part in parts], ends)
     left = weight * (x_ref[:, 0:head] + left)
     corner = weight * (x_ref[head:n, head:n] + corner)
     store((xh_ref, xl_ref), 0, left, corner)
@@ -347,7 +330,7 @@
     kernel = functools.partial(factor_kernel, pieces, batch, members)
     args = [ids, values, var, *sources]
     flops = 6 * n * n * members + 60 * n * n * n
-    return call(kernel, outs, [SMEM] + [VMEM] * (2 + len(sources)), args, scratch, flops)
+    return call(kernel, outs, [SMEM] + [VMEM] * (2 + len(sources)), args, scratch, flops, FACTOR_LIMIT)
 
 
 def gain(picks, factored, states):
@@ -424,19 +407,14 @@
         return permute(x, lambda c, q, m: (c + 2 * q - 1, 1 - q, m), regions)
 
     anywhere = pl.BlockSpec(memory_space=pl.ANY)
+    per_patch = obs_cell.shape[2]
+    picks = lax.dynamic_slice(obs_cell, (region * 2, 0, 0), (2, 1, per_patch)).reshape(2, per_patch)
     (rows,) = call(
         pick_kernel,
-        [((2, obs_cell.shape[2], half), F32, VMEM)],
-        [SMEM, anywhere, anywhere],
-        [(region * 2).astype(jnp.int32)[None], obs_cell, state],
-        [
-            pltpu.VMEM(obs_cell.shape, jnp.int32),
-            pltpu.VMEM(state.shape, F32),
-            pltpu.VMEM((8, 128), jnp.int32),
-            pltpu.VMEM((2, half, cells), F32),
-            pltpu.SemaphoreType.DMA((3,)),
-        ],
-        limit=56,
+        [((2, per_patch, half), F32, VMEM)],
+        [VMEM, VMEM],
+        [picks, state],
+        [pltpu.VMEM((8, 128), jnp.int32), pltpu.VMEM((2, half, cells), F32)],
     )
     other = across(rows)
     sources = [rows, beside(rows), outside(rows), other, beside(other), outside(other)]
@@ -457,11 +435,10 @@
     for i in range(3):
         pieces += [[(i, low, 0), (i, high, 1)], [(3 + i, high, 0), (3 + i, low, 1)]]
     for batch in range(1, NBATCH):
-        picks = lax.dynamic_slice_in_dim(obs_cell[:, batch, :], own, 1, 0)
+        picks = lax.dynamic_slice(obs_cell, (own, batch, 0), (1, 1, per_patch)).reshape(1, per_patch)
         z, rows = gain(picks, factored, states)
         other = across(rows)
-        out = outside(rows)
-        sources = [rows, beside(rows), out, other, beside(other), across(out)]
+        sources = [rows, beside(rows), outside(rows), other, beside(other), outside(other)]
         states = update(factored, z, states, (0, half))
         factored = factor(pieces, batch, members, ids_next, values, var, sources)
     z, theirs = last(factored, states)
@@ -473,7 +450,7 @@
         in_specs=[SMEM, VMEM, VMEM],
         out_specs=anywhere,
         scratch_shapes=[pltpu.VMEM(state.shape, F32), pltpu.SemaphoreType.DMA((4,))],
-        compiler_params=pltpu.CompilerParams(vmem_limit_bytes=48 * 1024 * 1024),
+        compiler_params=pltpu.CompilerParams(vmem_limit_bytes=16 * 1024 * 1024),
     )(place, mine, theirs)
 
 

time: 80.5 us -> 79.5 us (0.988)
  waiting for transfers between devices: 25.7 us -> 24.5 us
  local copies, waits for them, and re-layouts: 3.7 us -> 4.7 us
    ppermute x12, waiting for transfers between devices: 25.7 us -> 24.5 us  [permute(): return lax.ppermute(x, BOTH, table)]
    unnamed x20, local copies, waits for them, and re-layouts: 3.32 us -> 4.34 us
  transfers between devices with their start and end apart: 12 -> 12, of which waited for: 7 -> 7; matrix products, arithmetic and copies ran while one was open for 0% -> 0% of each run, Pallas kernels for 14% -> 15%
where the time goes in v1:
time: 79.5 us; the launch traced here: 79.2 us
  Pallas kernels  32.2 us (41%)
  waiting for transfers between devices  24.5 us (31%)
  starting transfers between devices  17.5 us (22%)
  local copies, waits for them, and re-layouts  4.7 us (6%)
    pallas_call x8, Pallas kernels, call(): pl.pallas_call(kernel, out_shape=shapes, in_specs=ins, out_specs=[space f...  31.1 us
    ppermute x12, waiting for transfers between devices, permute(): return lax.ppermute(x, BOTH, table)  24.5 us
    ppermute x12, starting transfers between devices, permute(): return lax.ppermute(x, BOTH, table)  17.5 us
    unnamed x20, local copies, waits for them, and re-layouts  4.34 us
  transfers between devices with their start and end apart: 12, of which 7 were waited for; matrix products, arithmetic and copies ran while one was open for 0% of the time, Pallas kernels for 15%

profile of v1, /device:TPU:0, one launch (start us, length us, event | category | flops | bytes accessed | tf_op | source)
XLA Modules:
  0.0 79.2 jit_solution(4537675954727521066)
XLA Ops:
  0.0 0.8 copy-done
  0.8 1.2 %copy-done.1 = f32[512,2,256]{2,1,0:T(2,128)S(1)} copy-done((f32[512,2,256]{2,1,0:T(2,128)S(1)}, f32[512,2,256]{2,1,0:T(2,128)}, u32[]{:S(2)}) %copy-start.1) | copy-done | bytes 1048600
  2.0 0.8 %shard_map.55.refs_0_ = f32[2,64,512]{2,1,0:T(8,128)S(1)} custom-call(s32[2,64]{1,0:T(2,128)S(1)} %bitcast.16, f32[512,2,256]{2,1,0:T(2,128)S(1)} %copy-done.1), custom_call_target="tpu_custom_call" | custom-call | bytes 1311232 | tf_op jit(solution)/shard_map/pallas_call | solution.py:30
  2.8 3.0 %collective-permute-start = (f32[2,64,512]{2,1,0:T(8,128)S(1)}, f32[2,64,512]{2,1,0:T(8,128)S(1)}, u32[]{:S(2)}, u32[]{:S(2)}) collective-permute-start(f32[2,64,512]{2,1,0:T(8,128)S(1)} %shard_map.55.refs_0_), channel_id=1, source_target_pairs={{0,1},{1,0},{2,3},{3,2},{4,5},{5,4},{6,7},{7,6},{8,9},{9,8},{10,11... | collective-permute-start | bytes 786440 | tf_op jit(solution)/shard_map/ppermute | solution.py:380
  5.8 3.7 %collective-permute-start.2 = (f32[2,64,512]{2,1,0:T(8,128)S(1)}, f32[2,64,512]{2,1,0:T(8,128)S(1)}, u32[]{:S(2)}, u32[]{:S(2)}) collective-permute-start(f32[2,64,512]{2,1,0:T(8,128)S(1)} %shard_map.55.refs_0_), channel_id=1, source_target_pairs={{0,30},{1,31},{2,4},{3,5},{4,2},{5,3},{6,8},{7,9},{8,6},{9,7},{10,... | collective-permute-start | bytes 786440 | tf_op jit(solution)/shard_map/ppermute | solution.py:380
  9.5 2.6 %collective-permute-done.refs_0_.refs_3_ = f32[2,64,512]{2,1,0:T(8,128)S(1)} collective-permute-done((f32[2,64,512]{2,1,0:T(8,128)S(1)}, f32[2,64,512]{2,1,0:T(8,128)S(1)}, u32[]{:S(2)}, u32[]{:S(2)}) %collective-permute-start) | collective-permute-done | bytes 262176 | tf_op jit(solution)/shard_map/ppermute | solution.py:380
  12.2 3.3 %collective-permute-start.4 = (f32[2,64,512]{2,1,0:T(8,128)S(1)}, f32[2,64,512]{2,1,0:T(8,128)}, u32[]{:S(2)}, u32[]{:S(2)}) collective-permute-start(f32[2,64,512]{2,1,0:T(8,128)S(1)} %collective-permute-done.refs_0_.refs_3_), channel_id=1, source_target_pairs={{0,30},{1,31},{2,4},{3,5},{4,2},{5,3},{6,8},{7,9},{8,6},{9,7},{10,... | collective-permute-start | bytes 786440 | tf_op jit(solution)/shard_map/ppermute | solution.py:380
  15.5 1.5 %shard_map.56 = (f32[512,256]{1,0:T(8,128)S(1)}, f32[512,256]{1,0:T(8,128)}, f32[32,2,64]{2,1,0:T(2,128)S(1)}, f32[32,2,64]{2,1,0:T(2,128)S(1)}) custom-call(s32[1]{0:T(128)} %bitcast.place_ref, f32[32,2,64]{2,1,0:T(2,128)S(1)} %copy-done.3, f32[32,2,64]{2,1,0:T(2,128)S(1)} %copy-done.4, f32[512,2,256]{2,1,0:T(2,128)S(1)} %copy-done.2, ...), custom_call_target="tpu_custom_call" | custom-call | bytes 2424836 | tf_op jit(solution)/shard_map/pallas_call | solution.py:30
  17.0 1.6 %collective-permute-start.5 = (f32[512,256]{1,0:T(8,128)}, f32[512,256]{1,0:T(8,128)S(1)}, u32[]{:S(2)}, u32[]{:S(2)}) collective-permute-start(f32[512,256]{1,0:T(8,128)} %get-tuple-element.39), channel_id=1, source_target_pairs={{0,1},{1,0},{2,3},{3,2},{4,5},{5,4},{6,7},{7,6},{8,9},{9,8},{10,11... | collective-permute-start | bytes 1572872 | tf_op jit(solution)/shard_map/ppermute | solution.py:380
  18.6 0.7 copy-done.9
  19.3 0.2 dynamic-slice_reduce_fusion
  19.4 0.1 concatenate.7.ids_ref
  19.6 0.7 copy-done.5
  20.3 0.6 collective-permute-done.4.refs_5_
  20.9 0.9 %copy-done.6 = f32[2,64,512]{2,1,0:T(8,128)S(1)} copy-done((f32[2,64,512]{2,1,0:T(8,128)S(1)}, f32[2,64,512]{2,1,0:T(8,128)}, u32[]{:S(2)}) %copy-start.6) | copy-done | bytes 262168
  21.8 8.7 %shard_map.57 = (bf16[384,1024]{1,0:T(8,128)(2,1)S(1)}, bf16[384,1024]{1,0:T(8,128)(2,1)S(1)}, f32[384,128]{1,0:T(8,128)S(1)}, f32[384,384]{1,0:T(8,128)S(1)}, b...) custom-call(s32[12]{0:T(128)S(1)} %concatenate.7.ids_ref, ...), custom_call_target="tpu_custom_call" | custom-call | flops 4303355904 | bytes 4554804 | tf_op jit(solution)/shard_map/pallas_call | solution.py:30
  30.6 1.0 %collective-permute-done.5.refs_1_ = f32[512,256]{1,0:T(8,128)S(1)} collective-permute-done((f32[512,256]{1,0:T(8,128)}, f32[512,256]{1,0:T(8,128)S(1)}, u32[]{:S(2)}, u32[]{:S(2)}) %collective-permute-start.5) | collective-permute-done | bytes 524320 | tf_op jit(solution)/shard_map/ppermute | solution.py:380
  31.6 5.1 %shard_map.58 = (f32[384,256]{1,0:T(8,128)S(1)}, f32[64,1024]{1,0:T(8,128)S(1)}) custom-call(s32[1]{0:T(128)} %get-tuple-element.31.n_ref, s32[1,64]{1,0:T(1,128)S(1)} %fusion.picks_ref, bf16[384,1024]{1,0:T(8,128)(2,1)S(1)} %get-tuple-element.32.sh_ref, bf16[384,1024]{1,0:T(8,128)(2,1)S(1)} %get-tuple-element.33.sl_ref, ...), custom_call_target="tpu_custom_call" | custom-call | flops 805306368 | bytes 4653316 | tf_op jit(solution)/shard_map/pallas_call | solution.py:30
  36.7 1.6 %collective-permute-start.8 = (f32[64,1024]{1,0:T(8,128)S(1)}, f32[64,1024]{1,0:T(8,128)}, u32[]{:S(2)}, u32[]{:S(2)}) collective-permute-start(f32[64,1024]{1,0:T(8,128)S(1)} %get-tuple-element.40.refs_0_), channel_id=1, source_target_pairs={{0,1},{1,0},{2,3},{3,2},{4,5},{5,4},{6,7},{7,6},{8,9},{9,8},{10,11... | collective-permute-start | bytes 786440 | tf_op jit(solution)/shard_map/ppermute | solution.py:380
  38.2 2.0 %collective-permute-start.7 = (f32[64,1024]{1,0:T(8,128)S(1)}, f32[64,1024]{1,0:T(8,128)}, u32[]{:S(2)}, u32[]{:S(2)}) collective-permute-start(f32[64,1024]{1,0:T(8,128)S(1)} %get-tuple-element.40.refs_0_), channel_id=1, source_target_pairs={{0,30},{1,31},{2,4},{3,5},{4,2},{5,3},{6,8},{7,9},{8,6},{9,7},{10,... | collective-permute-start | bytes 786440 | tf_op jit(solution)/shard_map/ppermute | solution.py:380
  40.3 4.5 %collective-permute-done.8.refs_3_ = f32[64,1024]{1,0:T(8,128)} collective-permute-done((f32[64,1024]{1,0:T(8,128)S(1)}, f32[64,1024]{1,0:T(8,128)}, u32[]{:S(2)}, u32[]{:S(2)}) %collective-permute-start.8) | collective-permute-done | bytes 262176 | tf_op jit(solution)/shard_map/ppermute | solution.py:380
  44.8 0.6 collective-permute-start.10
  45.4 0.1 concatenate.6.ids_ref
  45.5 0.9 %shard_map.60 = (f32[512,256]{1,0:T(8,128)S(1)}, f32[512,256]{1,0:T(8,128)S(1)}) custom-call(bf16[384,1024]{1,0:T(8,128)(2,1)S(1)} %get-tuple-element.32.sh_ref, bf16[384,1024]{1,0:T(8,128)(2,1)S(1)} %get-tuple-element.33.sl_ref, f32[384,128]{1,0:T(8,128)S(1)} %get-tuple-element.34.d_ref, f32[384,256]{1,0:T(8,128)S(1)} %get-tuple-element.48.z_ref, ...), custom_call_target="tpu_custom_call" | custom-call | flops 603979776 | bytes 4259840 | tf_op jit(solution)/shard_map/pallas_call | solution.py:30
  46.4 0.4 collective-permute-done.7.refs_2_
  46.8 6.7 %collective-permute-done.10.refs_5_ = f32[64,1024]{1,0:T(8,128)} collective-permute-done((f32[64,1024]{1,0:T(8,128)}, f32[64,1024]{1,0:T(8,128)}, u32[]{:S(2)}, u32[]{:S(2)}) %collective-permute-start.10) | collective-permute-done | bytes 262176 | tf_op jit(solution)/shard_map/ppermute | solution.py:380
  53.6 8.9 %shard_map.59 = (bf16[384,1024]{1,0:T(8,128)(2,1)S(1)}, bf16[384,1024]{1,0:T(8,128)(2,1)S(1)}, f32[384,128]{1,0:T(8,128)S(1)}, f32[384,384]{1,0:T(8,128)S(1)}, b...) custom-call(s32[12]{0:T(128)S(1)} %concatenate.6.ids_ref, ...), custom_call_target="tpu_custom_call" | custom-call | flops 4303355904 | bytes 4554804 | tf_op jit(solution)/shard_map/pallas_call | solution.py:30
  62.5 4.6 %shard_map.61 = (f32[384,256]{1,0:T(8,128)S(1)}, f32[512,256]{1,0:T(8,128)S(1)}) custom-call(s32[1]{0:T(128)} %get-tuple-element.44.n_ref, bf16[384,1024]{1,0:T(8,128)(2,1)S(1)} %get-tuple-element.41.sh_ref, bf16[384,1024]{1,0:T(8,128)(2,1)S(1)} %get-tuple-element.42.sl_ref, f32[384,128]{1,0:T(8,128)S(1)} %get-tuple-element.43.d_ref, ...), custom_call_target="tpu_custom_call" | custom-call | flops 1207959552 | bytes 4915204 | tf_op jit(solution)/shard_map/pallas_call | solution.py:30
  67.1 1.6 %collective-permute-start.11 = (f32[512,256]{1,0:T(8,128)S(1)}, f32[512,256]{1,0:T(8,128)S(1)}, u32[]{:S(2)}, u32[]{:S(2)}) collective-permute-start(f32[512,256]{1,0:T(8,128)S(1)} %get-tuple-element.52), channel_id=1, source_target_pairs={{0,1},{1,0},{2,3},{3,2},{4,5},{5,4},{6,7},{7,6},{8,9},{9,8},{10,11... | collective-permute-start | bytes 1572872 | tf_op jit(solution)/shard_map/ppermute | solution.py:380
  68.7 0.6 shard_map.62.mine_ref
  69.2 8.6 %collective-permute-done.11.theirs_ref = f32[512,256]{1,0:T(8,128)S(1)} collective-permute-done((f32[512,256]{1,0:T(8,128)S(1)}, f32[512,256]{1,0:T(8,128)S(1)}, u32[]{:S(2)}, u32[]{:S(2)}) %collective-permute-start.11) | collective-permute-done | bytes 524320 | tf_op jit(solution)/shard_map/ppermute | solution.py:380
  77.9 1.1 %shard_map.63 = f32[512,2,256]{2,1,0:T(2,128)} custom-call(s32[1]{0:T(128)} %bitcast.place_ref, f32[512,256]{1,0:T(8,128)S(1)} %shard_map.62.mine_ref, f32[512,256]{1,0:T(8,128)S(1)} %collective-permute-done.11.theirs_ref), custom_call_target="tpu_custom_call" | custom-call | tf_op jit(solution)/shard_map/pallas_call | solution.py:447
  (26 shorter events, 0.1 us)
Async XLA Ops:
  0.0 0.8 copy-start
  0.8 1.2 %copy-start.1 = (f32[512,2,256]{2,1,0:T(2,128)S(1)}, f32[512,2,256]{2,1,0:T(2,128)}, u32[]{:S(2)}) copy-start(f32[512,2,256]{2,1,0:T(2,128)} %state_ref.3) | copy-start | bytes 3145732
  2.0 13.5 %copy-start.2 = (f32[512,2,256]{2,1,0:T(2,128)S(1)}, f32[512,2,256]{2,1,0:T(2,128)}, u32[]{:S(2)}) copy-start(f32[512,2,256]{2,1,0:T(2,128)} %state_ref.3) | copy-start | bytes 3145732
  2.0 13.5 %copy-start.3 = (f32[32,2,64]{2,1,0:T(2,128)S(1)}, f32[32,2,64]{2,1,0:T(2,128)}, u32[]{:S(2)}) copy-start(f32[32,2,64]{2,1,0:T(2,128)} %values_hbm.1) | copy-start | bytes 49156
  2.0 13.5 %copy-start.4 = (f32[32,2,64]{2,1,0:T(2,128)S(1)}, f32[32,2,64]{2,1,0:T(2,128)}, u32[]{:S(2)}) copy-start(f32[32,2,64]{2,1,0:T(2,128)} %var_hbm.1) | copy-start | bytes 49156
  2.8 9.3 %collective-permute-start = (f32[2,64,512]{2,1,0:T(8,128)S(1)}, f32[2,64,512]{2,1,0:T(8,128)S(1)}, u32[]{:S(2)}, u32[]{:S(2)}) collective-permute-start(f32[2,64,512]{2,1,0:T(8,128)S(1)} %shard_map.55.refs_0_), channel_id=1, source_target_pairs={{0,1},{1,0},{2,3},{3,2},{4,5},{5,4},{6,7},{7,6},{8,9},{9,8},{10,11... | collective-permute-start | bytes 786440 | tf_op jit(solution)/shard_map/ppermute | solution.py:380
  5.8 13.7 %collective-permute-start.2 = (f32[2,64,512]{2,1,0:T(8,128)S(1)}, f32[2,64,512]{2,1,0:T(8,128)S(1)}, u32[]{:S(2)}, u32[]{:S(2)}) collective-permute-start(f32[2,64,512]{2,1,0:T(8,128)S(1)} %shard_map.55.refs_0_), channel_id=1, source_target_pairs={{0,30},{1,31},{2,4},{3,5},{4,2},{5,3},{6,8},{7,9},{8,6},{9,7},{10,... | collective-permute-start | bytes 786440 | tf_op jit(solution)/shard_map/ppermute | solution.py:380
  9.5 10.7 %collective-permute-start.1 = (f32[2,64,512]{2,1,0:T(8,128)S(1)}, f32[2,64,512]{2,1,0:T(8,128)}, u32[]{:S(2)}, u32[]{:S(2)}) collective-permute-start(f32[2,64,512]{2,1,0:T(8,128)S(1)} %shard_map.55.refs_0_), channel_id=1, source_target_pairs={{0,2},{1,3},{2,0},{3,1},{4,6},{5,7},{6,4},{7,5},{8,10},{9,11},{10,... | collective-permute-start | bytes 786440 | tf_op jit(solution)/shard_map/ppermute | solution.py:380
  12.2 8.7 %collective-permute-start.4 = (f32[2,64,512]{2,1,0:T(8,128)S(1)}, f32[2,64,512]{2,1,0:T(8,128)}, u32[]{:S(2)}, u32[]{:S(2)}) collective-permute-start(f32[2,64,512]{2,1,0:T(8,128)S(1)} %collective-permute-done.refs_0_.refs_3_), channel_id=1, source_target_pairs={{0,30},{1,31},{2,4},{3,5},{4,2},{5,3},{6,8},{7,9},{8,6},{9,7},{10,... | collective-permute-start | bytes 786440 | tf_op jit(solution)/shard_map/ppermute | solution.py:380
  15.5 5.4 %collective-permute-start.3 = (f32[2,64,512]{2,1,0:T(8,128)S(1)}, f32[2,64,512]{2,1,0:T(8,128)}, u32[]{:S(2)}, u32[]{:S(2)}) collective-permute-start(f32[2,64,512]{2,1,0:T(8,128)S(1)} %collective-permute-done.refs_0_.refs_3_), channel_id=1, source_target_pairs={{0,2},{1,3},{2,0},{3,1},{4,6},{5,7},{6,4},{7,5},{8,10},{9,11},{10,... | collective-permute-start | bytes 786440 | tf_op jit(solution)/shard_map/ppermute | solution.py:380
  17.0 3.9 %copy-start.7 = (f32[32,2,64]{2,1,0:T(2,128)}, f32[32,2,64]{2,1,0:T(2,128)S(1)}, u32[]{:S(2)}) copy-start(f32[32,2,64]{2,1,0:T(2,128)S(1)} %get-tuple-element.30.var_ref) | copy-start | bytes 49156
  17.0 14.6 %collective-permute-start.5 = (f32[512,256]{1,0:T(8,128)}, f32[512,256]{1,0:T(8,128)S(1)}, u32[]{:S(2)}, u32[]{:S(2)}) collective-permute-start(f32[512,256]{1,0:T(8,128)} %get-tuple-element.39), channel_id=1, source_target_pairs={{0,1},{1,0},{2,3},{3,2},{4,5},{5,4},{6,7},{7,6},{8,9},{9,8},{10,11... | collective-permute-start | bytes 1572872 | tf_op jit(solution)/shard_map/ppermute | solution.py:380
  18.6 0.7 copy-start.9
  19.6 0.7 copy-start.5
  20.9 1.0 %copy-start.6 = (f32[2,64,512]{2,1,0:T(8,128)S(1)}, f32[2,64,512]{2,1,0:T(8,128)}, u32[]{:S(2)}) copy-start(f32[2,64,512]{2,1,0:T(8,128)} %copy-done.5) | copy-start | bytes 786436
  36.7 8.1 %collective-permute-start.8 = (f32[64,1024]{1,0:T(8,128)S(1)}, f32[64,1024]{1,0:T(8,128)}, u32[]{:S(2)}, u32[]{:S(2)}) collective-permute-start(f32[64,1024]{1,0:T(8,128)S(1)} %get-tuple-element.40.refs_0_), channel_id=1, source_target_pairs={{0,1},{1,0},{2,3},{3,2},{4,5},{5,4},{6,7},{7,6},{8,9},{9,8},{10,11... | collective-permute-start | bytes 786440 | tf_op jit(solution)/shard_map/ppermute | solution.py:380
  38.2 8.6 %collective-permute-start.7 = (f32[64,1024]{1,0:T(8,128)S(1)}, f32[64,1024]{1,0:T(8,128)}, u32[]{:S(2)}, u32[]{:S(2)}) collective-permute-start(f32[64,1024]{1,0:T(8,128)S(1)} %get-tuple-element.40.refs_0_), channel_id=1, source_target_pairs={{0,30},{1,31},{2,4},{3,5},{4,2},{5,3},{6,8},{7,9},{8,6},{9,7},{10,... | collective-permute-start | bytes 786440 | tf_op jit(solution)/shard_map/ppermute | solution.py:380
  40.3 6.6 %collective-permute-start.6 = (f32[64,1024]{1,0:T(8,128)S(1)}, f32[64,1024]{1,0:T(8,128)}, u32[]{:S(2)}, u32[]{:S(2)}) collective-permute-start(f32[64,1024]{1,0:T(8,128)S(1)} %get-tuple-element.40.refs_0_), channel_id=1, source_target_pairs={{0,2},{1,3},{2,0},{3,1},{4,6},{5,7},{6,4},{7,5},{8,10},{9,11},{10,... | collective-permute-start | bytes 786440 | tf_op jit(solution)/shard_map/ppermute | solution.py:380
  44.8 8.8 %collective-permute-start.10 = (f32[64,1024]{1,0:T(8,128)}, f32[64,1024]{1,0:T(8,128)}, u32[]{:S(2)}, u32[]{:S(2)}) collective-permute-start(f32[64,1024]{1,0:T(8,128)} %collective-permute-done.8.refs_3_), channel_id=1, source_target_pairs={{0,30},{1,31},{2,4},{3,5},{4,2},{5,3},{6,8},{7,9},{8,6},{9,7},{10,... | collective-permute-start | bytes 786440 | tf_op jit(solution)/shard_map/ppermute | solution.py:380
  45.4 8.2 %collective-permute-start.9 = (f32[64,1024]{1,0:T(8,128)}, f32[64,1024]{1,0:T(8,128)}, u32[]{:S(2)}, u32[]{:S(2)}) collective-permute-start(f32[64,1024]{1,0:T(8,128)} %collective-permute-done.8.refs_3_), channel_id=1, source_target_pairs={{0,2},{1,3},{2,0},{3,1},{4,6},{5,7},{6,4},{7,5},{8,10},{9,11},{10,... | collective-permute-start | bytes 786440 | tf_op jit(solution)/shard_map/ppermute | solution.py:380
  45.5 8.1 %copy-start.8 = (f32[32,2,64]{2,1,0:T(2,128)S(1)}, f32[32,2,64]{2,1,0:T(2,128)}, u32[]{:S(2)}) copy-start(f32[32,2,64]{2,1,0:T(2,128)} %copy-done.7) | copy-start | bytes 49156
  67.1 10.8 %collective-permute-start.11 = (f32[512,256]{1,0:T(8,128)S(1)}, f32[512,256]{1,0:T(8,128)S(1)}, u32[]{:S(2)}, u32[]{:S(2)}) collective-permute-start(f32[512,256]{1,0:T(8,128)S(1)} %get-tuple-element.52), channel_id=1, source_target_pairs={{0,1},{1,0},{2,3},{3,2},{4,5},{5,4},{6,7},{7,6},{8,9},{9,8},{10,11... | collective-permute-start | bytes 1572872 | tf_op jit(solution)/shard_map/ppermute | solution.py:380

commit v2 on v1

--- a/solution.py
+++ b/solution.py
@@ -21,6 +21,7 @@
 FACTOR_LIMIT = 24
 MOST_STEPS = 15
 TILE = 256
+CHUNK = 128
 
 
 def call(kernel, outs, ins, args, scratch=(), flops=0, limit=16):
@@ -101,7 +102,9 @@
 
 
 def sort_kernel(place_ref, values_hbm, var_hbm, state_ref, *refs):
-    keep_ref, send_ref, values_ref, var_ref, sems = refs[-5:]
+    first_ref, second_ref, keep_ref, send_ref, values_ref, var_ref, near_ref, sems = refs[-8:]
+    near_ref[0] = first_ref[...]
+    near_ref[1] = second_ref[...]
     copies = [
         pltpu.make_async_copy(values_hbm, values_ref, sems.at[0]),
         pltpu.make_async_copy(var_hbm, var_ref, sems.at[1]),
@@ -116,7 +119,7 @@
         copy.wait()
 
 
-def factor_kernel(pieces, batch, members, ids_ref, values_ref, var_ref, *refs):
+def factor_kernel(pieces, batch, members, chunk, ids_ref, values_ref, var_ref, *refs):
     count = len(refs) - 12
     sources = refs[:count]
     sh_ref, sl_ref, d_ref, g_ref, xh_ref, xl_ref, n_ref, flat, eye_ref, x_ref, wa, wb = refs[count:]
@@ -218,23 +221,79 @@
         return advance(wb, wa, advance(wa, wb, rho2))
 
     rho2 = lax.fori_loop(0, pairs, twice, keep * keep)
-    for source, target in ((wa, wb), (wb, wa)) * 2 + ((wa, wb),):
-        rho2 = advance(source, target, rho2)
+    chunks = [(i, min(i + chunk, n)) for i in range(0, n, chunk)]
+
+    def sides(source, span):
+        return [source[i, span[0] : span[1], 0:n] for i in (0, 1)]
+
+    def put(targets, start, span, block):
+        for target, part in zip(targets, split(block)):
+            target[span[0] : span[1], start : start + head] = part
+        low = max(span[0], head)
+        if low < span[1]:
+            for target, part in zip(targets, split(jnp.transpose(block[low - span[0] :]))):
+                target[0:head, start + low : start + span[1]] = part
+
+    def put_corner(targets, start, block):
+        for target, part in zip(targets, split(block)):
+            target[head:n, start + head : start + n] = part
+
+    def put_x(targets, start, weight, span, product):
+        x = weight * (x_ref[span[0] : span[1], 0:head] + product)
+        x_ref[span[0] : span[1], 0:head] = x
+        put(targets, start, span, x)
+
+    def put_x_corner(targets, start, weight, product):
+        x = weight * (x_ref[head:n, head:n] + product)
+        x_ref[head:n, head:n] = x
+        put_corner(targets, start, x)
+
+    waiting = None
+    source, target = wa, wb
+    for _ in range(5):
+        weight = 2.0 / (2.0 - rho2)
+        keep = 0.5 * rho2 * weight
+        first = (source[0, :, 0:head], source[1, :, 0:head])
+        r = []
+        for k, span in enumerate(chunks):
+            r.append(dot3(sides(source, span), first))
+            if waiting is not None:
+                put_x((source.at[0], source.at[1]), n, waiting[0], span, waiting[1][k])
+        if waiting is not None:
+            put_x_corner((source.at[0], source.at[1]), n, waiting[0], waiting[2])
+        ends = [jnp.concatenate([source[i, :, head:n], source[i, :, n + head : 2 * n]], axis=1) for i in (0, 1)]
+        corners = dot3(sides(source, (head, n)), ends)
+        first = (source[0, :, n : n + head], source[1, :, n : n + head])
+        both = (target.at[0], target.at[1])
+        x = []
+        for k, span in enumerate(chunks):
+            x.append(dot3(sides(source, span), first))
+            put(both, 0, span, weight * r[k] - keep * eye_ref[span[0] : span[1], 0:head])
+        put_corner(both, 0, weight * corners[:, 0:tail] - keep * eye_ref[head:n, head:n])
+        waiting = (weight, x, corners[:, tail : 2 * tail])
+        rho2 = keep * keep
+        source, target = target, source
+    for k, span in enumerate(chunks):
+        put_x((source.at[0], source.at[1]), n, waiting[0], span, waiting[1][k])
+    put_x_corner((source.at[0], source.at[1]), n, waiting[0], waiting[2])
     weight = 2.0 / (2.0 - rho2)
-    parts = (wb[0, :, 0:n], wb[1, :, 0:n])
-    left = dot3(parts, (wb[0, :, n : n + head], wb[1, :, n : n + head]))
-    ends = [wb[i, :, n + head : 2 * n] for i in (0, 1)]
-    corner = dot3([part[head:n] for part in parts], ends)
-    left = weight * (x_ref[:, 0:head] + left)
-    corner = weight * (x_ref[head:n, head:n] + corner)
-    store((xh_ref, xl_ref), 0, left, corner)
-
-
-def solve(n_ref, s, g_ref, x, fields, z_ref):
+    first = (source[0, :, n : n + head], source[1, :, n : n + head])
+    done = (xh_ref, xl_ref)
+    ends = [source[i, :, n + head : 2 * n] for i in (0, 1)]
+    put_x_corner(done, 0, weight, dot3(sides(source, (head, n)), ends))
+    x = [dot3(sides(source, span), first) for span in chunks]
+    for k, span in enumerate(chunks):
+        put_x(done, 0, weight, span, x[k])
+
+
+def centred(fields):
     members = sum(field.shape[0] for field in fields)
     mean = sum(jnp.sum(field, axis=0, keepdims=True) for field in fields) * (1.0 / members)
     pairs = [split(field - mean) for field in fields]
-    anomaly = [jnp.concatenate(parts, axis=0) for parts in zip(*pairs)]
+    return [jnp.concatenate(parts, axis=0) for parts in zip(*pairs)], mean
+
+
+def solve(n_ref, s, g_ref, x, anomaly, z_ref):
     cross = dot3(s, anomaly)
     z = dot3(x, split(cross))
     g = g_ref[...]
@@ -248,7 +307,6 @@
         return carry
 
     lax.fori_loop(0, n_ref[0], refine, 0)
-    return anomaly, mean
 
 
 def gain_kernel(parts, n_ref, picks_ref, sh_ref, sl_ref, d_ref, g_ref, xh_ref, xl_ref, *refs):
@@ -256,7 +314,8 @@
     z_ref, rows_ref, scratch = refs[parts:]
     fields = [state[...] for state in states]
     s = (sh_ref[...], sl_ref[...])
-    anomaly, mean = solve(n_ref, s, g_ref, (xh_ref[...], xl_ref[...]), fields, z_ref)
+    anomaly, mean = centred(fields)
+    solve(n_ref, s, g_ref, (xh_ref[...], xl_ref[...]), anomaly, z_ref)
     hot = selector(picks_ref[...], mean.shape[1], scratch)
     zt = split(select(hot, split(z_ref[...]), NT))
     base = jnp.sum(hot * mean, axis=1, keepdims=True) + dot3(zt, split(d_ref[...]))[:, 0:1]
@@ -273,22 +332,27 @@
 
 
 def update_kernel(starts, sh_ref, sl_ref, d_ref, z_ref, *refs):
-    states, outs = refs[: len(starts)], refs[len(starts) :]
+    count = len(starts)
+    states, outs, parts = refs[:count], refs[count : 2 * count], refs[2 * count :]
     z = z_ref[...]
     shift = shift_of(z, d_ref)
     s, zs = (sh_ref[...], sl_ref[...]), split(z)
     for start, state, out in zip(starts, states, outs):
         out[...] = updated(state[...], start, s, shift, zs)
-
-
-def last_kernel(parts, n_ref, sh_ref, sl_ref, d_ref, g_ref, xh_ref, xl_ref, *refs):
-    states, (z_ref, out_ref) = refs[:parts], refs[parts:]
-    fields = [state[...] for state in states]
+    if parts:
+        anomaly, _ = centred([out[...] for out in outs])
+        for ref, part in zip(parts, anomaly):
+            ref[...] = part
+
+
+def last_kernel(n_ref, sh_ref, sl_ref, d_ref, g_ref, xh_ref, xl_ref, *refs):
+    (state_ref, *parts), (z_ref, out_ref) = refs[:-2], refs[-2:]
     s = (sh_ref[...], sl_ref[...])
-    solve(n_ref, s, g_ref, (xh_ref[...], xl_ref[...]), fields, z_ref)
+    anomaly = [part[...] for part in parts] if parts else centred([state_ref[...]])[0]
+    solve(n_ref, s, g_ref, (xh_ref[...], xl_ref[...]), anomaly, z_ref)
     z = z_ref[...]
-    start = sum(field.shape[0] for field in fields[:-1])
-    out_ref[...] = updated(states[-1][...], start, s, shift_of(z, d_ref), split(z))
+    start = sh_ref.shape[1] - state_ref.shape[0]
+    out_ref[...] = updated(state_ref[...], start, s, shift_of(z, d_ref), split(z))
 
 
 def join_kernel(place_ref, mine_ref, theirs_ref, out_ref, both, sems):
@@ -308,7 +372,7 @@
         copy.wait()
 
 
-def factor(pieces, batch, members, ids, values, var, sources):
+def factor(pieces, batch, members, chunk, ids, values, var, sources):
     per_patch = values.shape[2]
     n = len(pieces) * per_patch
     outs = [
@@ -327,7 +391,7 @@
         pltpu.VMEM((2, n, 2 * n), BF16),
         pltpu.VMEM((2, n, 2 * n), BF16),
     ]
-    kernel = functools.partial(factor_kernel, pieces, batch, members)
+    kernel = functools.partial(factor_kernel, pieces, batch, members, chunk)
     args = [ids, values, var, *sources]
     flops = 6 * n * n * members + 60 * n * n * n
     return call(kernel, outs, [SMEM] + [VMEM] * (2 + len(sources)), args, scratch, flops, FACTOR_LIMIT)
@@ -344,22 +408,23 @@
     return call(kernel, outs, ins, args, [pltpu.VMEM((8, 128), jnp.int32)], flops)
 
 
-def update(factored, z, states, starts):
+def update(factored, z, states, starts, more=False):
     sh, sl, d = factored[:3]
     kernel = functools.partial(update_kernel, starts)
     outs = [(state.shape, F32, VMEM) for state in states]
+    if more:
+        outs += [((sh.shape[1], z.shape[1]), BF16, VMEM)] * 2
     flops = 6 * sh.shape[0] * sh.shape[1] * z.shape[1]
     return call(kernel, outs, [VMEM] * (4 + len(states)), [sh, sl, d, z, *states], (), flops)
 
 
-def last(factored, states):
+def last(factored, state, anomaly=()):
     sh, sl, d, g, xh, xl, more = factored
-    kernel = functools.partial(last_kernel, len(states))
-    n, width = sh.shape[0], states[0].shape[1]
-    outs = [((n, width), F32, VMEM), (states[-1].shape, F32, VMEM)]
-    args = [more, sh, sl, d, g, xh, xl, *states]
+    n, width = sh.shape[0], state.shape[1]
+    outs = [((n, width), F32, VMEM), (state.shape, F32, VMEM)]
+    args = [more, sh, sl, d, g, xh, xl, state, *anomaly]
     flops = 12 * sh.shape[0] * sh.shape[1] * width
-    return call(kernel, outs, [SMEM] + [VMEM] * (6 + len(states)), args, (), flops)
+    return call(last_kernel, outs, [SMEM] + [VMEM] * (len(args) - 1), args, (), flops)
 
 
 def rings(size):
@@ -418,17 +483,24 @@
     )
     other = across(rows)
     sources = [rows, beside(rows), outside(rows), other, beside(other), outside(other)]
-    pieces = [[(i, (p,), 0), (3 + i, (p,), 1)] for i in range(3) for p in range(2)]
     shape = ((half, cells), F32, VMEM)
-    keep, send, values, var = call(
+    outs = [shape, shape, (obs_values.shape, F32, VMEM), (obs_var.shape, F32, VMEM)]
+    keep, send, values, var, near = call(
         sort_kernel,
-        [shape, shape, (obs_values.shape, F32, VMEM), (obs_var.shape, F32, VMEM)],
-        [SMEM, anywhere, anywhere, VMEM, anywhere],
-        [place, obs_values, obs_var, state, other],
+        outs + [((2, *rows.shape), F32, VMEM)],
+        [SMEM, anywhere, anywhere, VMEM, anywhere, VMEM, VMEM],
+        [place, obs_values, obs_var, state, other, sources[1], sources[2]],
         [pltpu.SemaphoreType.DMA((2,))],
     )
+    sources[1:3] = [near]
+    pieces = []
+    for p in range(2):
+        pieces.append([(0, (p,), 0), (2, (p,), 1)])
+    for i in range(2):
+        for p in range(2):
+            pieces.append([(1, (i, p), 0), (3 + i, (p,), 1)])
     states = [keep, across(send)]
-    factored = factor(pieces, 0, members, ids_first, values, var, sources)
+    factored = factor(pieces, 0, members, CHUNK, ids_first, values, var, sources)
     everything = slice(None)
     low, high = (everything, slice(0, half)), (everything, slice(half, members))
     pieces = []
@@ -439,9 +511,10 @@
         z, rows = gain(picks, factored, states)
         other = across(rows)
         sources = [rows, beside(rows), outside(rows), other, beside(other), outside(other)]
-        states = update(factored, z, states, (0, half))
-        factored = factor(pieces, batch, members, ids_next, values, var, sources)
-    z, theirs = last(factored, states)
+        mine, theirs, *anomaly = update(factored, z, states, (0, half), True)
+        states = [mine, theirs]
+        factored = factor(pieces, batch, members, 3 * CHUNK, ids_next, values, var, sources)
+    z, theirs = last(factored, states[1], anomaly)
     theirs = across(theirs)
     (mine,) = update(factored, z, states[:1], (0,))
     return pl.pallas_call(
@@ -481,8 +554,8 @@
             home = (ids // region_patches - region + 1) % regions
             rows = jnp.take(beside, home * region_patches + ids % region_patches, axis=0)
             pieces = [[(0, (i,), 0)] for i in range(ids.shape[0])]
-            factored = factor(pieces, batch, members, table, obs_values, obs_var, [rows])
-            new.append(last(factored, [fields[p]])[1])
+            factored = factor(pieces, batch, members, CHUNK, table, obs_values, obs_var, [rows])
+            new.append(last(factored, fields[p])[1])
         fields = new
     ensemble = jnp.stack(fields, axis=1)
     return lax.all_to_all(ensemble, "member", split_axis=0, concat_axis=1, tiled=True)

time: 79.5 us -> 80 us (level)
  waiting for transfers between devices: 24.5 us -> 27.2 us
  starting transfers between devices: 17.5 us -> 15.4 us
    ppermute x12, waiting for transfers between devices: 24.5 us -> 27.2 us  [permute(): return lax.ppermute(x, BOTH, table)]
    ppermute x12, starting transfers between devices: 17.5 us -> 15.4 us  [permute(): return lax.ppermute(x, BOTH, table)]
  transfers between devices with their start and end apart: 12 -> 12, of which waited for: 7 -> 7; matrix products, arithmetic and copies ran while one was open for 0% -> 0% of each run, Pallas kernels for 15% -> 14%
where the time goes in v2:
time: 80 us; the launch traced here: 79.7 us
  Pallas kernels  31.9 us (40%)
  waiting for transfers between devices  27.2 us (34%)
  starting transfers between devices  15.4 us (19%)
  local copies, waits for them, and re-layouts  4.88 us (6%)
    pallas_call x8, Pallas kernels, call(): pl.pallas_call(kernel, out_shape=shapes, in_specs=ins, out_specs=[space f...  30.8 us
    ppermute x12, waiting for transfers between devices, permute(): return lax.ppermute(x, BOTH, table)  27.2 us
    ppermute x12, starting transfers between devices, permute(): return lax.ppermute(x, BOTH, table)  15.4 us
    unnamed x20, local copies, waits for them, and re-layouts  4.52 us
  transfers between devices with their start and end apart: 12, of which 7 were waited for; matrix products, arithmetic and copies ran while one was open for 0% of the time, Pallas kernels for 14%

profile of v2, /device:TPU:0, one launch (start us, length us, event | category | flops | bytes accessed | tf_op | source)
XLA Modules:
  0.0 79.7 jit_solution(8166719585860835609)
XLA Ops:
  0.0 0.8 copy-done
  0.8 1.2 %copy-done.1 = f32[512,2,256]{2,1,0:T(2,128)S(1)} copy-done((f32[512,2,256]{2,1,0:T(2,128)S(1)}, f32[512,2,256]{2,1,0:T(2,128)}, u32[]{:S(2)}) %copy-start.1) | copy-done | bytes 1048600
  2.0 0.8 %shard_map.55.refs_0_ = f32[2,64,512]{2,1,0:T(8,128)S(1)} custom-call(s32[2,64]{1,0:T(2,128)S(1)} %bitcast.16, f32[512,2,256]{2,1,0:T(2,128)S(1)} %copy-done.1), custom_call_target="tpu_custom_call" | custom-call | bytes 1311232 | tf_op jit(solution)/shard_map/pallas_call | solution.py:31
  2.8 3.0 %collective-permute-start = (f32[2,64,512]{2,1,0:T(8,128)S(1)}, f32[2,64,512]{2,1,0:T(8,128)S(1)}, u32[]{:S(2)}, u32[]{:S(2)}) collective-permute-start(f32[2,64,512]{2,1,0:T(8,128)S(1)} %shard_map.55.refs_0_), channel_id=1, source_target_pairs={{0,1},{1,0},{2,3},{3,2},{4,5},{5,4},{6,7},{7,6},{8,9},{9,8},{10,11... | collective-permute-start | bytes 786440 | tf_op jit(solution)/shard_map/ppermute | solution.py:445
  5.8 3.7 %collective-permute-start.2 = (f32[2,64,512]{2,1,0:T(8,128)S(1)}, f32[2,64,512]{2,1,0:T(8,128)S(1)}, u32[]{:S(2)}, u32[]{:S(2)}) collective-permute-start(f32[2,64,512]{2,1,0:T(8,128)S(1)} %shard_map.55.refs_0_), channel_id=1, source_target_pairs={{0,30},{1,31},{2,4},{3,5},{4,2},{5,3},{6,8},{7,9},{8,6},{9,7},{10,... | collective-permute-start | bytes 786440 | tf_op jit(solution)/shard_map/ppermute | solution.py:445
  9.5 2.6 %collective-permute-done.refs_0_.refs_2_ = f32[2,64,512]{2,1,0:T(8,128)S(1)} collective-permute-done((f32[2,64,512]{2,1,0:T(8,128)S(1)}, f32[2,64,512]{2,1,0:T(8,128)S(1)}, u32[]{:S(2)}, u32[]{:S(2)}) %collective-permute-start) | collective-permute-done | bytes 262176 | tf_op jit(solution)/shard_map/ppermute | solution.py:445
  12.2 3.3 %collective-permute-start.4 = (f32[2,64,512]{2,1,0:T(8,128)S(1)}, f32[2,64,512]{2,1,0:T(8,128)}, u32[]{:S(2)}, u32[]{:S(2)}) collective-permute-start(f32[2,64,512]{2,1,0:T(8,128)S(1)} %collective-permute-done.refs_0_.refs_2_), channel_id=1, source_target_pairs={{0,30},{1,31},{2,4},{3,5},{4,2},{5,3},{6,8},{7,9},{8,6},{9,7},{10,... | collective-permute-start | bytes 786440 | tf_op jit(solution)/shard_map/ppermute | solution.py:445
  15.5 0.0 collective-permute-start.3
  15.5 1.5 %shard_map.56 = (f32[512,256]{1,0:T(8,128)S(1)}, f32[512,256]{1,0:T(8,128)}, f32[32,2,64]{2,1,0:T(2,128)S(1)}, f32[32,2,64]{2,1,0:T(2,128)S(1)}, f32[2,2,64,512]{3,2,1,0:T(8,128)S(1)}) custom-call(s32[1]{0:T(128)} %bitcast.place_ref, f32[32,2,64]{2,1,0:T(2,128)S(1)} %copy-done.3, f32[32,2,64]{2,1,0:T(2,128)S(1)} %copy-done.4, f32[512,2,256]{2,1,0:T(2,128)S(1)} %copy-done.2, ...), custom_call_target="tpu_custom_call" | custom-call | bytes 3473412 | tf_op jit(solution)/shard_map/pallas_call | solution.py:31
  17.0 0.8 copy-done.5
  17.8 1.5 %collective-permute-start.5 = (f32[512,256]{1,0:T(8,128)}, f32[512,256]{1,0:T(8,128)S(1)}, u32[]{:S(2)}, u32[]{:S(2)}) collective-permute-start(f32[512,256]{1,0:T(8,128)} %get-tuple-element.43), channel_id=1, source_target_pairs={{0,1},{1,0},{2,3},{3,2},{4,5},{5,4},{6,7},{7,6},{8,9},{9,8},{10,11... | collective-permute-start | bytes 1572872 | tf_op jit(solution)/shard_map/ppermute | solution.py:445
  19.4 0.7 copy-done.9
  20.1 0.2 dynamic-slice_reduce_fusion
  20.2 0.1 concatenate.7.ids_ref
  20.3 0.5 collective-permute-done.4.refs_4_
  20.9 1.0 %copy-done.6 = f32[2,2,64,512]{3,2,1,0:T(8,128)S(1)} copy-done((f32[2,2,64,512]{3,2,1,0:T(8,128)S(1)}, f32[2,2,64,512]{3,2,1,0:T(8,128)}, u32[]{:S(2)}) %copy-start.6) | copy-done | bytes 524312
  21.9 8.0 %shard_map.57 = (bf16[384,1024]{1,0:T(8,128)(2,1)S(1)}, bf16[384,1024]{1,0:T(8,128)(2,1)S(1)}, f32[384,128]{1,0:T(8,128)S(1)}, f32[384,384]{1,0:T(8,128)S(1)}, b...) custom-call(s32[12]{0:T(128)S(1)} %concatenate.7.ids_ref, ...), custom_call_target="tpu_custom_call" | custom-call | flops 4303355904 | bytes 4554804 | tf_op jit(solution)/shard_map/pallas_call | solution.py:31
  29.9 2.4 %collective-permute-done.5.refs_1_ = f32[512,256]{1,0:T(8,128)S(1)} collective-permute-done((f32[512,256]{1,0:T(8,128)}, f32[512,256]{1,0:T(8,128)S(1)}, u32[]{:S(2)}, u32[]{:S(2)}) %collective-permute-start.5) | collective-permute-done | bytes 524320 | tf_op jit(solution)/shard_map/ppermute | solution.py:445
  32.4 5.1 %shard_map.58 = (f32[384,256]{1,0:T(8,128)S(1)}, f32[64,1024]{1,0:T(8,128)S(1)}) custom-call(s32[1]{0:T(128)} %get-tuple-element.35.n_ref, s32[1,64]{1,0:T(1,128)S(1)} %fusion.picks_ref, bf16[384,1024]{1,0:T(8,128)(2,1)S(1)} %get-tuple-element.36.sh_ref, bf16[384,1024]{1,0:T(8,128)(2,1)S(1)} %get-tuple-element.37.sl_ref, ...), custom_call_target="tpu_custom_call" | custom-call | flops 805306368 | bytes 4653316 | tf_op jit(solution)/shard_map/pallas_call | solution.py:31
  37.5 1.6 %collective-permute-start.8 = (f32[64,1024]{1,0:T(8,128)S(1)}, f32[64,1024]{1,0:T(8,128)}, u32[]{:S(2)}, u32[]{:S(2)}) collective-permute-start(f32[64,1024]{1,0:T(8,128)S(1)} %get-tuple-element.44.refs_0_), channel_id=1, source_target_pairs={{0,1},{1,0},{2,3},{3,2},{4,5},{5,4},{6,7},{7,6},{8,9},{9,8},{10,11... | collective-permute-start | bytes 786440 | tf_op jit(solution)/shard_map/ppermute | solution.py:445
  39.1 0.6 collective-permute-start.7
  39.7 5.9 %collective-permute-done.8.refs_3_ = f32[64,1024]{1,0:T(8,128)} collective-permute-done((f32[64,1024]{1,0:T(8,128)S(1)}, f32[64,1024]{1,0:T(8,128)}, u32[]{:S(2)}, u32[]{:S(2)}) %collective-permute-start.8) | collective-permute-done | bytes 262176 | tf_op jit(solution)/shard_map/ppermute | solution.py:445
  45.6 0.1 concatenate.6.ids_ref
  45.7 1.2 %shard_map.60 = (f32[512,256]{1,0:T(8,128)S(1)}, f32[512,256]{1,0:T(8,128)S(1)}, bf16[1024,256]{1,0:T(8,128)(2,1)S(1)}, bf16[1024,256]{1,0:T(8,128)(2,1)S(1)}) custom-call(bf16[384,1024]{1,0:T(8,128)(2,1)S(1)} %get-tuple-element.36.sh_ref, bf16[384,1024]{1,0:T(8,128)(2,1)S(1)} %get-tuple-element.37.sl_ref, f32[384,128]{1,0:T(8,128)S(1)} %get-tuple-element.38.d_ref, ...), custom_call_target="tpu_custom_call" | custom-call | flops 603979776 | bytes 5308416 | tf_op jit(solution)/shard_map/pallas_call | solution.py:31
  46.9 0.7 collective-permute-done.7.refs_2_
  47.7 6.7 %collective-permute-done.10.refs_5_ = f32[64,1024]{1,0:T(8,128)} collective-permute-done((f32[64,1024]{1,0:T(8,128)}, f32[64,1024]{1,0:T(8,128)}, u32[]{:S(2)}, u32[]{:S(2)}) %collective-permute-start.10) | collective-permute-done | bytes 262176 | tf_op jit(solution)/shard_map/ppermute | solution.py:445
  54.4 9.3 %shard_map.59 = (bf16[384,1024]{1,0:T(8,128)(2,1)S(1)}, bf16[384,1024]{1,0:T(8,128)(2,1)S(1)}, f32[384,128]{1,0:T(8,128)S(1)}, f32[384,384]{1,0:T(8,128)S(1)}, b...) custom-call(s32[12]{0:T(128)S(1)} %concatenate.6.ids_ref, ...), custom_call_target="tpu_custom_call" | custom-call | flops 4303355904 | bytes 4554804 | tf_op jit(solution)/shard_map/pallas_call | solution.py:31
  63.7 4.3 %shard_map.61 = (f32[384,256]{1,0:T(8,128)S(1)}, f32[512,256]{1,0:T(8,128)S(1)}) custom-call(s32[1]{0:T(128)} %get-tuple-element.48.n_ref, bf16[384,1024]{1,0:T(8,128)(2,1)S(1)} %get-tuple-element.45.sh_ref, bf16[384,1024]{1,0:T(8,128)(2,1)S(1)} %get-tuple-element.46.sl_ref, f32[384,128]{1,0:T(8,128)S(1)} %get-tuple-element.47.d_ref, ...), custom_call_target="tpu_custom_call" | custom-call | flops 1207959552 | bytes 5439492 | tf_op jit(solution)/shard_map/pallas_call | solution.py:31
  68.0 1.6 %collective-permute-start.11 = (f32[512,256]{1,0:T(8,128)S(1)}, f32[512,256]{1,0:T(8,128)S(1)}, u32[]{:S(2)}, u32[]{:S(2)}) collective-permute-start(f32[512,256]{1,0:T(8,128)S(1)} %get-tuple-element.58), channel_id=1, source_target_pairs={{0,1},{1,0},{2,3},{3,2},{4,5},{5,4},{6,7},{7,6},{8,9},{9,8},{10,11... | collective-permute-start | bytes 1572872 | tf_op jit(solution)/shard_map/ppermute | solution.py:445
  69.6 0.6 shard_map.62.mine_ref
  70.1 8.3 %collective-permute-done.11.theirs_ref = f32[512,256]{1,0:T(8,128)S(1)} collective-permute-done((f32[512,256]{1,0:T(8,128)S(1)}, f32[512,256]{1,0:T(8,128)S(1)}, u32[]{:S(2)}, u32[]{:S(2)}) %collective-permute-start.11) | collective-permute-done | bytes 524320 | tf_op jit(solution)/shard_map/ppermute | solution.py:445
  78.4 1.1 %shard_map.63 = f32[512,2,256]{2,1,0:T(2,128)} custom-call(s32[1]{0:T(128)} %bitcast.place_ref, f32[512,256]{1,0:T(8,128)S(1)} %shard_map.62.mine_ref, f32[512,256]{1,0:T(8,128)S(1)} %collective-permute-done.11.theirs_ref), custom_call_target="tpu_custom_call" | custom-call | tf_op jit(solution)/shard_map/pallas_call | solution.py:520
  (26 shorter events, 0.1 us)
Async XLA Ops:
  0.0 0.8 copy-start
  0.8 1.2 %copy-start.1 = (f32[512,2,256]{2,1,0:T(2,128)S(1)}, f32[512,2,256]{2,1,0:T(2,128)}, u32[]{:S(2)}) copy-start(f32[512,2,256]{2,1,0:T(2,128)} %state_ref.3) | copy-start | bytes 3145732
  2.0 13.5 %copy-start.2 = (f32[512,2,256]{2,1,0:T(2,128)S(1)}, f32[512,2,256]{2,1,0:T(2,128)}, u32[]{:S(2)}) copy-start(f32[512,2,256]{2,1,0:T(2,128)} %state_ref.3) | copy-start | bytes 3145732
  2.0 13.5 %copy-start.3 = (f32[32,2,64]{2,1,0:T(2,128)S(1)}, f32[32,2,64]{2,1,0:T(2,128)}, u32[]{:S(2)}) copy-start(f32[32,2,64]{2,1,0:T(2,128)} %values_hbm.1) | copy-start | bytes 49156
  2.0 13.5 %copy-start.4 = (f32[32,2,64]{2,1,0:T(2,128)S(1)}, f32[32,2,64]{2,1,0:T(2,128)}, u32[]{:S(2)}) copy-start(f32[32,2,64]{2,1,0:T(2,128)} %var_hbm.1) | copy-start | bytes 49156
  2.8 9.3 %collective-permute-start = (f32[2,64,512]{2,1,0:T(8,128)S(1)}, f32[2,64,512]{2,1,0:T(8,128)S(1)}, u32[]{:S(2)}, u32[]{:S(2)}) collective-permute-start(f32[2,64,512]{2,1,0:T(8,128)S(1)} %shard_map.55.refs_0_), channel_id=1, source_target_pairs={{0,1},{1,0},{2,3},{3,2},{4,5},{5,4},{6,7},{7,6},{8,9},{9,8},{10,11... | collective-permute-start | bytes 786440 | tf_op jit(solution)/shard_map/ppermute | solution.py:445
  5.8 9.6 %collective-permute-start.2 = (f32[2,64,512]{2,1,0:T(8,128)S(1)}, f32[2,64,512]{2,1,0:T(8,128)S(1)}, u32[]{:S(2)}, u32[]{:S(2)}) collective-permute-start(f32[2,64,512]{2,1,0:T(8,128)S(1)} %shard_map.55.refs_0_), channel_id=1, source_target_pairs={{0,30},{1,31},{2,4},{3,5},{4,2},{5,3},{6,8},{7,9},{8,6},{9,7},{10,... | collective-permute-start | bytes 786440 | tf_op jit(solution)/shard_map/ppermute | solution.py:445
  9.5 5.9 %collective-permute-start.1 = (f32[2,64,512]{2,1,0:T(8,128)S(1)}, f32[2,64,512]{2,1,0:T(8,128)S(1)}, u32[]{:S(2)}, u32[]{:S(2)}) collective-permute-start(f32[2,64,512]{2,1,0:T(8,128)S(1)} %shard_map.55.refs_0_), channel_id=1, source_target_pairs={{0,2},{1,3},{2,0},{3,1},{4,6},{5,7},{6,4},{7,5},{8,10},{9,11},{10,... | collective-permute-start | bytes 786440 | tf_op jit(solution)/shard_map/ppermute | solution.py:445
  12.2 8.7 %collective-permute-start.4 = (f32[2,64,512]{2,1,0:T(8,128)S(1)}, f32[2,64,512]{2,1,0:T(8,128)}, u32[]{:S(2)}, u32[]{:S(2)}) collective-permute-start(f32[2,64,512]{2,1,0:T(8,128)S(1)} %collective-permute-done.refs_0_.refs_2_), channel_id=1, source_target_pairs={{0,30},{1,31},{2,4},{3,5},{4,2},{5,3},{6,8},{7,9},{8,6},{9,7},{10,... | collective-permute-start | bytes 786440 | tf_op jit(solution)/shard_map/ppermute | solution.py:445
  15.5 5.4 %collective-permute-start.3 = (f32[2,64,512]{2,1,0:T(8,128)S(1)}, f32[2,64,512]{2,1,0:T(8,128)}, u32[]{:S(2)}, u32[]{:S(2)}) collective-permute-start(f32[2,64,512]{2,1,0:T(8,128)S(1)} %collective-permute-done.refs_0_.refs_2_), channel_id=1, source_target_pairs={{0,2},{1,3},{2,0},{3,1},{4,6},{5,7},{6,4},{7,5},{8,10},{9,11},{10,... | collective-permute-start | bytes 786440 | tf_op jit(solution)/shard_map/ppermute | solution.py:445
  17.0 0.8 %copy-start.5 = (f32[2,2,64,512]{3,2,1,0:T(8,128)}, f32[2,2,64,512]{3,2,1,0:T(8,128)S(1)}, u32[]{:S(2)}) copy-start(f32[2,2,64,512]{3,2,1,0:T(8,128)S(1)} %get-tuple-element.34.refs_1_) | copy-start | bytes 1572868
  17.8 3.0 %copy-start.7 = (f32[32,2,64]{2,1,0:T(2,128)}, f32[32,2,64]{2,1,0:T(2,128)S(1)}, u32[]{:S(2)}) copy-start(f32[32,2,64]{2,1,0:T(2,128)S(1)} %get-tuple-element.33.var_ref) | copy-start | bytes 49156
  17.8 14.5 %collective-permute-start.5 = (f32[512,256]{1,0:T(8,128)}, f32[512,256]{1,0:T(8,128)S(1)}, u32[]{:S(2)}, u32[]{:S(2)}) collective-permute-start(f32[512,256]{1,0:T(8,128)} %get-tuple-element.43), channel_id=1, source_target_pairs={{0,1},{1,0},{2,3},{3,2},{4,5},{5,4},{6,7},{7,6},{8,9},{9,8},{10,11... | collective-permute-start | bytes 1572872 | tf_op jit(solution)/shard_map/ppermute | solution.py:445
  19.4 0.7 copy-start.9
  20.9 1.0 %copy-start.6 = (f32[2,2,64,512]{3,2,1,0:T(8,128)S(1)}, f32[2,2,64,512]{3,2,1,0:T(8,128)}, u32[]{:S(2)}) copy-start(f32[2,2,64,512]{3,2,1,0:T(8,128)} %copy-done.5) | copy-start | bytes 1572868
  37.5 8.1 %collective-permute-start.8 = (f32[64,1024]{1,0:T(8,128)S(1)}, f32[64,1024]{1,0:T(8,128)}, u32[]{:S(2)}, u32[]{:S(2)}) collective-permute-start(f32[64,1024]{1,0:T(8,128)S(1)} %get-tuple-element.44.refs_0_), channel_id=1, source_target_pairs={{0,1},{1,0},{2,3},{3,2},{4,5},{5,4},{6,7},{7,6},{8,9},{9,8},{10,11... | collective-permute-start | bytes 786440 | tf_op jit(solution)/shard_map/ppermute | solution.py:445
  39.1 8.6 %collective-permute-start.7 = (f32[64,1024]{1,0:T(8,128)S(1)}, f32[64,1024]{1,0:T(8,128)}, u32[]{:S(2)}, u32[]{:S(2)}) collective-permute-start(f32[64,1024]{1,0:T(8,128)S(1)} %get-tuple-element.44.refs_0_), channel_id=1, source_target_pairs={{0,30},{1,31},{2,4},{3,5},{4,2},{5,3},{6,8},{7,9},{8,6},{9,7},{10,... | collective-permute-start | bytes 786440 | tf_op jit(solution)/shard_map/ppermute | solution.py:445
  39.7 8.0 %collective-permute-start.6 = (f32[64,1024]{1,0:T(8,128)S(1)}, f32[64,1024]{1,0:T(8,128)}, u32[]{:S(2)}, u32[]{:S(2)}) collective-permute-start(f32[64,1024]{1,0:T(8,128)S(1)} %get-tuple-element.44.refs_0_), channel_id=1, source_target_pairs={{0,2},{1,3},{2,0},{3,1},{4,6},{5,7},{6,4},{7,5},{8,10},{9,11},{10,... | collective-permute-start | bytes 786440 | tf_op jit(solution)/shard_map/ppermute | solution.py:445
  45.6 8.8 %collective-permute-start.10 = (f32[64,1024]{1,0:T(8,128)}, f32[64,1024]{1,0:T(8,128)}, u32[]{:S(2)}, u32[]{:S(2)}) collective-permute-start(f32[64,1024]{1,0:T(8,128)} %collective-permute-done.8.refs_3_), channel_id=1, source_target_pairs={{0,30},{1,31},{2,4},{3,5},{4,2},{5,3},{6,8},{7,9},{8,6},{9,7},{10,... | collective-permute-start | bytes 786440 | tf_op jit(solution)/shard_map/ppermute | solution.py:445
  45.6 8.8 %collective-permute-start.9 = (f32[64,1024]{1,0:T(8,128)}, f32[64,1024]{1,0:T(8,128)}, u32[]{:S(2)}, u32[]{:S(2)}) collective-permute-start(f32[64,1024]{1,0:T(8,128)} %collective-permute-done.8.refs_3_), channel_id=1, source_target_pairs={{0,2},{1,3},{2,0},{3,1},{4,6},{5,7},{6,4},{7,5},{8,10},{9,11},{10,... | collective-permute-start | bytes 786440 | tf_op jit(solution)/shard_map/ppermute | solution.py:445
  45.7 8.7 %copy-start.8 = (f32[32,2,64]{2,1,0:T(2,128)S(1)}, f32[32,2,64]{2,1,0:T(2,128)}, u32[]{:S(2)}) copy-start(f32[32,2,64]{2,1,0:T(2,128)} %copy-done.7) | copy-start | bytes 49156
  68.0 10.4 %collective-permute-start.11 = (f32[512,256]{1,0:T(8,128)S(1)}, f32[512,256]{1,0:T(8,128)S(1)}, u32[]{:S(2)}, u32[]{:S(2)}) collective-permute-start(f32[512,256]{1,0:T(8,128)S(1)} %get-tuple-element.58), channel_id=1, source_target_pairs={{0,1},{1,0},{2,3},{3,2},{4,5},{5,4},{6,7},{7,6},{8,9},{9,8},{10,11... | collective-permute-start | bytes 1572872 | tf_op jit(solution)/shard_map/ppermute | solution.py:445

commit v3 on v2

--- a/solution.py
+++ b/solution.py
@@ -93,25 +93,23 @@
     return jnp.transpose(hot)[0:per_patch, :]
 
 
-def pick_kernel(picks_ref, state_ref, rows_ref, scratch, field_ref):
+def pick_kernel(place_ref, cells_ref, state_ref, rows_ref, scratch, field_ref):
     patches, cells = state_ref.shape[1:]
     for p in range(patches):
         field_ref[p] = state_ref[:, p, :]
-        hot = selector(picks_ref[p : p + 1, :], cells, scratch)
+        hot = selector(cells_ref[pl.ds(place_ref[0] * patches + p, 1), 0, :], cells, scratch)
         rows_ref[p] = select(hot, split_all(field_ref[p]), NT)
 
 
 def sort_kernel(place_ref, values_hbm, var_hbm, state_ref, *refs):
-    first_ref, second_ref, keep_ref, send_ref, values_ref, var_ref, near_ref, sems = refs[-8:]
-    near_ref[0] = first_ref[...]
-    near_ref[1] = second_ref[...]
+    keep_ref, send_ref, values_ref, var_ref, sems = refs[-5:]
     copies = [
         pltpu.make_async_copy(values_hbm, values_ref, sems.at[0]),
         pltpu.make_async_copy(var_hbm, var_ref, sems.at[1]),
     ]
     for copy in copies:
         copy.start()
-    column = place_ref[0]
+    column = place_ref[1]
     first, second = state_ref[:, 0, :], state_ref[:, 1, :]
     keep_ref[...] = jnp.where(column == 0, first, second)
     send_ref[...] = jnp.where(column == 0, second, first)
@@ -119,47 +117,58 @@
         copy.wait()
 
 
-def factor_kernel(pieces, batch, members, chunk, ids_ref, values_ref, var_ref, *refs):
+def factor_kernel(pieces, batch, members, chunk, patches_of, place_ref, near_ref, values_ref, var_ref, *refs):
     count = len(refs) - 12
     sources = refs[:count]
     sh_ref, sl_ref, d_ref, g_ref, xh_ref, xl_ref, n_ref, flat, eye_ref, x_ref, wa, wb = refs[count:]
     per_patch = values_ref.shape[2]
     flat[...] = jnp.ones_like(flat)
     blocks = len(pieces)
-    own = ids_ref[blocks]
+    ids, own = patches_of(place_ref)
     for i in range(blocks):
-        patch = ids_ref[i]
+        patch = ids[i]
         widening = (patch == own).astype(jnp.int32)
-        for j in range(ids_ref.shape[0] - blocks - 1):
-            widening = widening + (ids_ref[blocks + 1 + j] == patch).astype(jnp.int32) * (j + 2)
+        for j in range(near_ref.shape[0]):
+            widening = widening + (near_ref[j, own] == patch).astype(jnp.int32) * (j + 2)
         flat[i : i + 1, 0:per_patch] = values_ref[pl.ds(patch, 1), batch, :]
         noise = var_ref[pl.ds(patch, 1), batch, :] * widening.astype(F32)
         flat[blocks + i : blocks + i + 1, 0:per_patch] = noise
     upright = jnp.transpose(flat[...])
-    for i, halves in enumerate(pieces):
-        rows = [sources[which][index] for which, index, _ in halves]
+
+    def scaled(i):
+        rows = [sources[which][index] for which, index, _ in pieces[i]]
         total = sum(jnp.sum(part, axis=1, keepdims=True) for part in rows)
         mean = total * (1.0 / members)
         noise = upright[0:per_patch, blocks + i : blocks + i + 1]
         scale = lax.rsqrt(noise * (members - 1.0))
         at = slice(i * per_patch, (i + 1) * per_patch)
-        for part, (_, _, start) in zip(rows, halves):
+        for part, (_, _, start) in zip(rows, pieces[i]):
             size = part.shape[1]
-            high, low = split((part - mean) * scale)
             lanes = slice(start * size, (start + 1) * size)
-            sh_ref[at, lanes] = high
-            sl_ref[at, lanes] = low
+            sh_ref[at, lanes], sl_ref[at, lanes] = split((part - mean) * scale)
         shift = (upright[0:per_patch, i : i + 1] - mean) * scale
         d_ref[at, :] = jnp.broadcast_to(shift, (per_patch, d_ref.shape[1]))
+
     n = sh_ref.shape[0]
     head = min(TILE, n)
     tail = n - head
-    s = (sh_ref[...], sl_ref[...])
-    left = dot3(s, [part[0:head] for part in s], NT)
-    g_ref[:, 0:head] = left
-    g_ref[0:head, head:n] = jnp.transpose(left[head:n])
-    low = [part[head:n] for part in s]
+    chunks = [(i, min(i + chunk, n)) for i in range(0, n, chunk)]
+    first = head // per_patch
+    for i in range(first):
+        scaled(i)
+    left = (sh_ref[0:head], sl_ref[0:head])
+    rest = list(range(first, blocks))
+    for start, stop in chunks:
+        if stop <= head:
+            if rest:
+                scaled(rest.pop(0))
+        else:
+            while rest:
+                scaled(rest.pop(0))
+        g_ref[start:stop, 0:head] = dot3((sh_ref[start:stop], sl_ref[start:stop]), left, NT)
+    low = (sh_ref[head:n], sl_ref[head:n])
     g_ref[head:n, head:n] = dot3(low, low, NT)
+    g_ref[0:head, head:n] = jnp.transpose(g_ref[head:n, 0:head])
     g = g_ref[...]
     square = jnp.sum(jnp.sum(g * g, axis=0, keepdims=True), axis=1, keepdims=True)
     norm = jnp.sqrt(square) * (1.0 + 1e-5)
@@ -217,11 +226,7 @@
         store(both, n, left, corner)
         return keep * keep
 
-    def twice(_, rho2):
-        return advance(wb, wa, advance(wa, wb, rho2))
-
-    rho2 = lax.fori_loop(0, pairs, twice, keep * keep)
-    chunks = [(i, min(i + chunk, n)) for i in range(0, n, chunk)]
+    rho2 = keep * keep
 
     def sides(source, span):
         return [source[i, span[0] : span[1], 0:n] for i in (0, 1)]
@@ -276,6 +281,11 @@
     for k, span in enumerate(chunks):
         put_x((source.at[0], source.at[1]), n, waiting[0], span, waiting[1][k])
     put_x_corner((source.at[0], source.at[1]), n, waiting[0], waiting[2])
+
+    def twice(_, rho2):
+        return advance(target, source, advance(source, target, rho2))
+
+    rho2 = lax.fori_loop(0, pairs, twice, rho2)
     weight = 2.0 / (2.0 - rho2)
     first = (source[0, :, n : n + head], source[1, :, n : n + head])
     done = (xh_ref, xl_ref)
@@ -293,30 +303,66 @@
     return [jnp.concatenate(parts, axis=0) for parts in zip(*pairs)], mean
 
 
-def solve(n_ref, s, g_ref, x, anomaly, z_ref):
-    cross = dot3(s, anomaly)
-    z = dot3(x, split(cross))
-    g = g_ref[...]
-    left = cross - z - dot3(split(g), split(z))
-    z_ref[...] = z + dot3(x, split(left))
+def in_chunks(count, product, work):
+    waiting = None
+    for start in range(0, count, CHUNK):
+        span = slice(start, min(start + CHUNK, count))
+        result = product(span)
+        if waiting is not None:
+            work(*waiting)
+        waiting = (span, result)
+    work(*waiting)
+
+
+def solve(n_ref, s, g_ref, x, anomaly, z_ref, cross_ref, parts_ref):
+    n = z_ref.shape[0]
+
+    def keep(slot, span, value):
+        for i, part in enumerate(split(value)):
+            parts_ref[slot, i, span] = part
+
+    def kept(slot):
+        return parts_ref[slot, 0], parts_ref[slot, 1]
+
+    def some(parts, span):
+        return [part[span] for part in parts]
+
+    def crossed(span, value):
+        cross_ref[span] = value
+        keep(0, span, value)
+
+    def solved(span, value):
+        z_ref[span] = value
+        keep(1, span, value)
+
+    def left(span, value):
+        keep(0, span, cross_ref[span] - z_ref[span] - value)
+
+    def refined(span, value):
+        z_ref[span] = z_ref[span] + value
+
+    in_chunks(n, lambda span: dot3(some(s, span), anomaly), crossed)
+    in_chunks(n, lambda span: dot3(some(x, span), kept(0)), solved)
+    in_chunks(n, lambda span: dot3(split(g_ref[span]), kept(1)), left)
+    in_chunks(n, lambda span: dot3(some(x, span), kept(0)), refined)
 
     def refine(_, carry):
         z = z_ref[...]
         gz = lax.dot_general(g_ref[...], z, NN, precision=HIGHEST, preferred_element_type=F32)
-        z_ref[...] = z + dot3(x, split(cross - z - gz))
+        z_ref[...] = z + dot3([part[...] for part in x], split(cross_ref[...] - z - gz))
         return carry
 
     lax.fori_loop(0, n_ref[0], refine, 0)
 
 
-def gain_kernel(parts, n_ref, picks_ref, sh_ref, sl_ref, d_ref, g_ref, xh_ref, xl_ref, *refs):
+def gain_kernel(batch, parts, own_of, place_ref, n_ref, cells_ref, sh_ref, sl_ref, d_ref, g_ref, xh_ref, xl_ref, *refs):
     states = refs[:parts]
-    z_ref, rows_ref, scratch = refs[parts:]
-    fields = [state[...] for state in states]
+    z_ref, rows_ref, scratch, cross_ref, parts_ref = refs[parts:]
+    anomaly, mean = centred([state[...] for state in states])
+    solve(n_ref, (sh_ref, sl_ref), g_ref, (xh_ref, xl_ref), anomaly, z_ref, cross_ref, parts_ref)
     s = (sh_ref[...], sl_ref[...])
-    anomaly, mean = centred(fields)
-    solve(n_ref, s, g_ref, (xh_ref[...], xl_ref[...]), anomaly, z_ref)
-    hot = selector(picks_ref[...], mean.shape[1], scratch)
+    picks = cells_ref[pl.ds(own_of(place_ref), 1), batch, :]
+    hot = selector(picks, mean.shape[1], scratch)
     zt = split(select(hot, split(z_ref[...]), NT))
     base = jnp.sum(hot * mean, axis=1, keepdims=True) + dot3(zt, split(d_ref[...]))[:, 0:1]
     rows_ref[...] = base + select(hot, anomaly, NT) - 0.5 * dot3(zt, s)
@@ -346,19 +392,19 @@
 
 
 def last_kernel(n_ref, sh_ref, sl_ref, d_ref, g_ref, xh_ref, xl_ref, *refs):
-    (state_ref, *parts), (z_ref, out_ref) = refs[:-2], refs[-2:]
-    s = (sh_ref[...], sl_ref[...])
+    (state_ref, *parts), (z_ref, out_ref, cross_ref, parts_ref) = refs[:-4], refs[-4:]
     anomaly = [part[...] for part in parts] if parts else centred([state_ref[...]])[0]
-    solve(n_ref, s, g_ref, (xh_ref[...], xl_ref[...]), anomaly, z_ref)
+    solve(n_ref, (sh_ref, sl_ref), g_ref, (xh_ref, xl_ref), anomaly, z_ref, cross_ref, parts_ref)
     z = z_ref[...]
     start = sh_ref.shape[1] - state_ref.shape[0]
+    s = (sh_ref[...], sl_ref[...])
     out_ref[...] = updated(state_ref[...], start, s, shift_of(z, d_ref), split(z))
 
 
 def join_kernel(place_ref, mine_ref, theirs_ref, out_ref, both, sems):
     chunks = sems.shape[0]
     size = both.shape[0] // chunks
-    column = place_ref[0]
+    column = place_ref[1]
     copies = []
     for i in range(chunks):
         at = slice(i * size, (i + 1) * size)
@@ -372,7 +418,7 @@
         copy.wait()
 
 
-def factor(pieces, batch, members, chunk, ids, values, var, sources):
+def factor(pieces, batch, members, chunk, patches_of, place, near, values, var, sources):
     per_patch = values.shape[2]
     n = len(pieces) * per_patch
     outs = [
@@ -391,21 +437,27 @@
         pltpu.VMEM((2, n, 2 * n), BF16),
         pltpu.VMEM((2, n, 2 * n), BF16),
     ]
-    kernel = functools.partial(factor_kernel, pieces, batch, members, chunk)
-    args = [ids, values, var, *sources]
+    kernel = functools.partial(factor_kernel, pieces, batch, members, chunk, patches_of)
+    args = [place, near, values, var, *sources]
     flops = 6 * n * n * members + 60 * n * n * n
-    return call(kernel, outs, [SMEM] + [VMEM] * (2 + len(sources)), args, scratch, flops, FACTOR_LIMIT)
-
-
-def gain(picks, factored, states):
+    return call(kernel, outs, [SMEM, SMEM] + [VMEM] * (2 + len(sources)), args, scratch, flops, FACTOR_LIMIT)
+
+
+def solver_scratch(n, width):
+    return [pltpu.VMEM((n, width), F32), pltpu.VMEM((2, 2, n, width), BF16)]
+
+
+def gain(batch, own_of, place, cells, factored, states):
     sh, sl, d, g, xh, xl, more = factored
     n, members = sh.shape
-    kernel = functools.partial(gain_kernel, len(states))
-    outs = [((n, states[0].shape[1]), F32, VMEM), ((picks.shape[1], members), F32, VMEM)]
-    ins = [SMEM] + [VMEM] * (7 + len(states))
-    args = [more, picks, sh, sl, d, g, xh, xl, *states]
-    flops = 8 * n * members * states[0].shape[1]
-    return call(kernel, outs, ins, args, [pltpu.VMEM((8, 128), jnp.int32)], flops)
+    width = states[0].shape[1]
+    kernel = functools.partial(gain_kernel, batch, len(states), own_of)
+    outs = [((n, width), F32, VMEM), ((cells.shape[2], members), F32, VMEM)]
+    ins = [SMEM, SMEM] + [VMEM] * (7 + len(states))
+    args = [place, more, cells, sh, sl, d, g, xh, xl, *states]
+    flops = 8 * n * members * width
+    scratch = [pltpu.VMEM((8, 128), jnp.int32)] + solver_scratch(n, width)
+    return call(kernel, outs, ins, args, scratch, flops)
 
 
 def update(factored, z, states, starts, more=False):
@@ -424,7 +476,8 @@
     outs = [((n, width), F32, VMEM), (state.shape, F32, VMEM)]
     args = [more, sh, sl, d, g, xh, xl, state, *anomaly]
     flops = 12 * sh.shape[0] * sh.shape[1] * width
-    return call(last_kernel, outs, [SMEM] + [VMEM] * (len(args) - 1), args, (), flops)
+    ins = [SMEM] + [VMEM] * (len(args) - 1)
+    return call(last_kernel, outs, ins, args, solver_scratch(n, width), flops)
 
 
 def rings(size):
@@ -450,17 +503,23 @@
     members = 2 * half
     regions = lax.axis_size("region")
     region, column = lax.axis_index("region"), lax.axis_index("member")
-    parity = region % 2
-    mate = region + 1 - 2 * parity
-    outer = (region + regions + 2 * parity - 1) % regions
-    own = region * 2 + column
-    place = column.astype(jnp.int32)[None]
-    links = lax.dynamic_index_in_dim(neighbours, own, 0, keepdims=False)
-    around = (region, mate, outer)
-    ids_first = [r * 2 + p for r in around for p in (0, 1)]
-    ids_next = [r * 2 + p for r in around for p in (column, 1 - column)]
-    ids_first = jnp.concatenate([jnp.stack(ids_first + [own]).astype(jnp.int32), links])
-    ids_next = jnp.concatenate([jnp.stack(ids_next + [own]).astype(jnp.int32), links])
+    place = jnp.stack([region, column]).astype(jnp.int32)
+    near = neighbours.T
+
+    def own_of(place_ref):
+        return place_ref[0] * 2 + place_ref[1]
+
+    def around(place_ref, within):
+        region = place_ref[0]
+        side = 2 * lax.rem(region, 2) - 1
+        outer = lax.rem(region + regions + side, regions)
+        return [r * 2 + p for r in (region, region - side, outer) for p in within], own_of(place_ref)
+
+    def patches_first(place_ref):
+        return around(place_ref, (0, 1))
+
+    def patches_next(place_ref):
+        return around(place_ref, (place_ref[1], 1 - place_ref[1]))
 
     def across(x):
         return permute(x, lambda c, q, m: (c, q, 1 - m), regions)
@@ -472,48 +531,38 @@
         return permute(x, lambda c, q, m: (c + 2 * q - 1, 1 - q, m), regions)
 
     anywhere = pl.BlockSpec(memory_space=pl.ANY)
-    per_patch = obs_cell.shape[2]
-    picks = lax.dynamic_slice(obs_cell, (region * 2, 0, 0), (2, 1, per_patch)).reshape(2, per_patch)
     (rows,) = call(
         pick_kernel,
-        [((2, per_patch, half), F32, VMEM)],
-        [VMEM, VMEM],
-        [picks, state],
+        [((2, obs_cell.shape[2], half), F32, VMEM)],
+        [SMEM, VMEM, VMEM],
+        [place, obs_cell, state],
         [pltpu.VMEM((8, 128), jnp.int32), pltpu.VMEM((2, half, cells), F32)],
     )
     other = across(rows)
     sources = [rows, beside(rows), outside(rows), other, beside(other), outside(other)]
     shape = ((half, cells), F32, VMEM)
-    outs = [shape, shape, (obs_values.shape, F32, VMEM), (obs_var.shape, F32, VMEM)]
-    keep, send, values, var, near = call(
+    keep, send, values, var = call(
         sort_kernel,
-        outs + [((2, *rows.shape), F32, VMEM)],
-        [SMEM, anywhere, anywhere, VMEM, anywhere, VMEM, VMEM],
-        [place, obs_values, obs_var, state, other, sources[1], sources[2]],
+        [shape, shape, (obs_values.shape, F32, VMEM), (obs_var.shape, F32, VMEM)],
+        [SMEM, anywhere, anywhere, VMEM, anywhere],
+        [place, obs_values, obs_var, state, other],
         [pltpu.SemaphoreType.DMA((2,))],
     )
-    sources[1:3] = [near]
-    pieces = []
-    for p in range(2):
-        pieces.append([(0, (p,), 0), (2, (p,), 1)])
-    for i in range(2):
-        for p in range(2):
-            pieces.append([(1, (i, p), 0), (3 + i, (p,), 1)])
+    pieces = [[(i, (p,), 0), (3 + i, (p,), 1)] for i in range(3) for p in range(2)]
     states = [keep, across(send)]
-    factored = factor(pieces, 0, members, CHUNK, ids_first, values, var, sources)
+    factored = factor(pieces, 0, members, CHUNK, patches_first, place, near, values, var, sources)
     everything = slice(None)
     low, high = (everything, slice(0, half)), (everything, slice(half, members))
     pieces = []
     for i in range(3):
         pieces += [[(i, low, 0), (i, high, 1)], [(3 + i, high, 0), (3 + i, low, 1)]]
     for batch in range(1, NBATCH):
-        picks = lax.dynamic_slice(obs_cell, (own, batch, 0), (1, 1, per_patch)).reshape(1, per_patch)
-        z, rows = gain(picks, factored, states)
+        z, rows = gain(batch, own_of, place, obs_cell, factored, states)
         other = across(rows)
         sources = [rows, beside(rows), outside(rows), other, beside(other), outside(other)]
         mine, theirs, *anomaly = update(factored, z, states, (0, half), True)
         states = [mine, theirs]
-        factored = factor(pieces, batch, members, 3 * CHUNK, ids_next, values, var, sources)
+        factored = factor(pieces, batch, members, CHUNK // 2, patches_next, place, near, values, var, sources)
     z, theirs = last(factored, states[1], anomaly)
     theirs = across(theirs)
     (mine,) = update(factored, z, states[:1], (0,))
@@ -525,6 +574,11 @@
         scratch_shapes=[pltpu.VMEM(state.shape, F32), pltpu.SemaphoreType.DMA((4,))],
         compiler_params=pltpu.CompilerParams(vmem_limit_bytes=16 * 1024 * 1024),
     )(place, mine, theirs)
+
+
+def listed(table_ref):
+    blocks = table_ref.shape[0] - 1
+    return [table_ref[i] for i in range(blocks)], table_ref[blocks]
 
 
 def general(state, neighbours, obs_cell, obs_values, obs_var):
@@ -550,11 +604,13 @@
             own = first + p
             links = lax.dynamic_index_in_dim(neighbours, own, 0, keepdims=False)
             ids = jnp.concatenate([own[None], links]).astype(jnp.int32)
-            table = jnp.concatenate([ids, own[None], links]).astype(jnp.int32)
+            table = jnp.concatenate([ids, own[None]]).astype(jnp.int32)
             home = (ids // region_patches - region + 1) % regions
             rows = jnp.take(beside, home * region_patches + ids % region_patches, axis=0)
             pieces = [[(0, (i,), 0)] for i in range(ids.shape[0])]
-            factored = factor(pieces, batch, members, CHUNK, table, obs_values, obs_var, [rows])
+            factored = factor(
+                pieces, batch, members, CHUNK, listed, table, neighbours.T, obs_values, obs_var, [rows]
+            )
             new.append(last(factored, fields[p])[1])
         fields = new
     ensemble = jnp.stack(fields, axis=1)

time: 80 us -> 83.3 us (1.041)
  Pallas kernels: 31.9 us -> 36.7 us
  local copies, waits for them, and re-layouts: 4.88 us -> 2 us
    pallas_call x8, Pallas kernels: 30.8 us -> 35.1 us  [call(): pl.pallas_call(kernel, out_shape=shapes, in_specs=ins, out_specs=[space f...]
    unnamed x20 -> x14, local copies, waits for them, and re-layouts: 4.52 us -> 2 us
where the time goes in v3:
time: 83.3 us; the launch traced here: 83 us
  Pallas kernels  36.7 us (44%)
  waiting for transfers between devices  28 us (34%)
  starting transfers between devices  15.9 us (19%)
  local copies, waits for them, and re-layouts  2 us (2%)
    pallas_call x8, Pallas kernels, call(): pl.pallas_call(kernel, out_shape=shapes, in_specs=ins, out_specs=[space f...  35.1 us
    ppermute x12, waiting for transfers between devices, permute(): return lax.ppermute(x, BOTH, table)  28 us
    ppermute x12, starting transfers between devices, permute(): return lax.ppermute(x, BOTH, table)  15.9 us
    unnamed x14, local copies, waits for them, and re-layouts  2 us
  transfers between devices with their start and end apart: 12, of which 7 were waited for; matrix products, arithmetic and copies ran while one was open for 0% of the time, Pallas kernels for 14%

profile of v3, /device:TPU:0, one launch (start us, length us, event | category | flops | bytes accessed | tf_op | source)
XLA Modules:
  0.0 83.0 jit_solution(5752730411210238720)
XLA Ops:
  0.0 0.1 pad_add_fusion.place_ref
  0.1 1.2 %copy-done = f32[512,2,256]{2,1,0:T(2,128)S(1)} copy-done((f32[512,2,256]{2,1,0:T(2,128)S(1)}, f32[512,2,256]{2,1,0:T(2,128)}, u32[]{:S(2)}) %copy-start) | copy-done | bytes 1048600
  1.3 0.8 copy-done.2
  2.1 1.4 %shard_map.55.refs_0_ = f32[2,64,512]{2,1,0:T(8,128)S(1)} custom-call(s32[2]{0:T(128)S(1)} %pad_add_fusion.place_ref, s32[32,2,64]{2,1,0:T(2,128)S(1)} %copy-done.2, f32[512,2,256]{2,1,0:T(2,128)S(1)} %copy-done), custom_call_target="tpu_custom_call" | custom-call | bytes 1327112 | tf_op jit(solution)/shard_map/pallas_call | solution.py:31
  3.4 3.0 %collective-permute-start = (f32[2,64,512]{2,1,0:T(8,128)S(1)}, f32[2,64,512]{2,1,0:T(8,128)S(1)}, u32[]{:S(2)}, u32[]{:S(2)}) collective-permute-start(f32[2,64,512]{2,1,0:T(8,128)S(1)} %shard_map.55.refs_0_), channel_id=1, source_target_pairs={{0,1},{1,0},{2,3},{3,2},{4,5},{5,4},{6,7},{7,6},{8,9},{9,8},{10,11... | collective-permute-start | bytes 786440 | tf_op jit(solution)/shard_map/ppermute | solution.py:498
  6.5 3.7 %collective-permute-start.2 = (f32[2,64,512]{2,1,0:T(8,128)S(1)}, f32[2,64,512]{2,1,0:T(8,128)S(1)}, u32[]{:S(2)}, u32[]{:S(2)}) collective-permute-start(f32[2,64,512]{2,1,0:T(8,128)S(1)} %shard_map.55.refs_0_), channel_id=1, source_target_pairs={{0,30},{1,31},{2,4},{3,5},{4,2},{5,3},{6,8},{7,9},{8,6},{9,7},{10,... | collective-permute-start | bytes 786440 | tf_op jit(solution)/shard_map/ppermute | solution.py:498
  10.2 2.6 %collective-permute-done.refs_0_.refs_3_ = f32[2,64,512]{2,1,0:T(8,128)S(1)} collective-permute-done((f32[2,64,512]{2,1,0:T(8,128)S(1)}, f32[2,64,512]{2,1,0:T(8,128)S(1)}, u32[]{:S(2)}, u32[]{:S(2)}) %collective-permute-start) | collective-permute-done | bytes 262176 | tf_op jit(solution)/shard_map/ppermute | solution.py:498
  12.8 3.3 %collective-permute-start.4 = (f32[2,64,512]{2,1,0:T(8,128)S(1)}, f32[2,64,512]{2,1,0:T(8,128)S(1)}, u32[]{:S(2)}, u32[]{:S(2)}) collective-permute-start(f32[2,64,512]{2,1,0:T(8,128)S(1)} %collective-permute-done.refs_0_.refs_3_), channel_id=1, source_target_pairs={{0,30},{1,31},{2,4},{3,5},{4,2},{5,3},{6,8},{7,9},{8,6},{9,7},{10,... | collective-permute-start | bytes 786440 | tf_op jit(solution)/shard_map/ppermute | solution.py:498
  16.1 1.2 %shard_map.56 = (f32[512,256]{1,0:T(8,128)S(1)}, f32[512,256]{1,0:T(8,128)S(1)}, f32[32,2,64]{2,1,0:T(2,128)S(1)}, f32[32,2,64]{2,1,0:T(2,128)S(1)}) custom-call(s32[2]{0:T(128)S(1)} %pad_add_fusion.place_ref, f32[32,2,64]{2,1,0:T(2,128)S(1)} %copy-done.4, f32[32,2,64]{2,1,0:T(2,128)S(1)} %copy-done.5, f32[512,2,256]{2,1,0:T(2,128)S(1)} %copy-done.1, ...), custom_call_target="tpu_custom_call" | custom-call | bytes 2424840 | tf_op jit(solution)/shard_map/pallas_call | solution.py:31
  17.3 0.0 copy-start.6
  17.3 1.6 %collective-permute-start.5 = (f32[512,256]{1,0:T(8,128)S(1)}, f32[512,256]{1,0:T(8,128)S(1)}, u32[]{:S(2)}, u32[]{:S(2)}) collective-permute-start(f32[512,256]{1,0:T(8,128)S(1)} %get-tuple-element.41), channel_id=1, source_target_pairs={{0,1},{1,0},{2,3},{3,2},{4,5},{5,4},{6,7},{7,6},{8,9},{9,8},{10,11... | collective-permute-start | bytes 1572872 | tf_op jit(solution)/shard_map/ppermute | solution.py:498
  18.9 0.0 collective-permute-done.2.refs_2_
  18.9 2.4 %collective-permute-done.4.refs_5_ = f32[2,64,512]{2,1,0:T(8,128)S(1)} collective-permute-done((f32[2,64,512]{2,1,0:T(8,128)S(1)}, f32[2,64,512]{2,1,0:T(8,128)S(1)}, u32[]{:S(2)}, u32[]{:S(2)}) %collective-permute-start.4) | collective-permute-done | bytes 262176 | tf_op jit(solution)/shard_map/ppermute | solution.py:498
  21.4 8.4 %shard_map.57 = (bf16[384,1024]{1,0:T(8,128)(2,1)S(1)}, bf16[384,1024]{1,0:T(8,128)(2,1)S(1)}, f32[384,128]{1,0:T(8,128)S(1)}, f32[384,384]{1,0:T(8,128)S(1)}, b...) custom-call(s32[2]{0:T(128)S(1)} %pad_add_fusion.place_ref, s32[5,32]{1,0:T(8,128)S(1)} %bitcast.3, ...), custom_call_target="tpu_custom_call" | custom-call | flops 4303355904 | bytes 4555404 | tf_op jit(solution)/shard_map/pallas_call | solution.py:31
  29.8 1.9 %collective-permute-done.5.refs_1_ = f32[512,256]{1,0:T(8,128)S(1)} collective-permute-done((f32[512,256]{1,0:T(8,128)S(1)}, f32[512,256]{1,0:T(8,128)S(1)}, u32[]{:S(2)}, u32[]{:S(2)}) %collective-permute-start.5) | collective-permute-done | bytes 524320 | tf_op jit(solution)/shard_map/ppermute | solution.py:498
  31.7 5.2 %shard_map.58 = (f32[384,256]{1,0:T(8,128)S(1)}, f32[64,1024]{1,0:T(8,128)S(1)}) custom-call(s32[2]{0:T(128)S(1)} %pad_add_fusion.place_ref, s32[1]{0:T(128)} %get-tuple-element.33.n_ref, s32[32,2,64]{2,1,0:T(2,128)S(1)} %copy-done.3, bf16[384,1024]{1,0:T(8,128)(2,1)S(1)} %get-tuple-element.34.sh_ref, bf16[384,1024]{1,0:T(8,128)(2,1)S(1)} %get-tuple-element.35.sl_ref, ...), custom_call_target="tpu_custom_call" | custom-call | flops 805306368 | bytes 4669452 | tf_op jit(solution)/shard_map/pallas_call | solution.py:31
  37.0 1.6 %collective-permute-start.8 = (f32[64,1024]{1,0:T(8,128)S(1)}, f32[64,1024]{1,0:T(8,128)S(1)}, u32[]{:S(2)}, u32[]{:S(2)}) collective-permute-start(f32[64,1024]{1,0:T(8,128)S(1)} %get-tuple-element.42.refs_0_), channel_id=1, source_target_pairs={{0,1},{1,0},{2,3},{3,2},{4,5},{5,4},{6,7},{7,6},{8,9},{9,8},{10,11... | collective-permute-start | bytes 786440 | tf_op jit(solution)/shard_map/ppermute | solution.py:498
  38.5 1.1 %collective-permute-start.7 = (f32[64,1024]{1,0:T(8,128)S(1)}, f32[64,1024]{1,0:T(8,128)S(1)}, u32[]{:S(2)}, u32[]{:S(2)}) collective-permute-start(f32[64,1024]{1,0:T(8,128)S(1)} %get-tuple-element.42.refs_0_), channel_id=1, source_target_pairs={{0,30},{1,31},{2,4},{3,5},{4,2},{5,3},{6,8},{7,9},{8,6},{9,7},{10,... | collective-permute-start | bytes 786440 | tf_op jit(solution)/shard_map/ppermute | solution.py:498
  39.7 5.3 %collective-permute-done.8.refs_3_ = f32[64,1024]{1,0:T(8,128)S(1)} collective-permute-done((f32[64,1024]{1,0:T(8,128)S(1)}, f32[64,1024]{1,0:T(8,128)S(1)}, u32[]{:S(2)}, u32[]{:S(2)}) %collective-permute-start.8) | collective-permute-done | bytes 262176 | tf_op jit(solution)/shard_map/ppermute | solution.py:498
  44.9 0.0 collective-permute-start.10
  44.9 0.0 collective-permute-start.9
  44.9 1.2 %shard_map.60 = (f32[512,256]{1,0:T(8,128)S(1)}, f32[512,256]{1,0:T(8,128)S(1)}, bf16[1024,256]{1,0:T(8,128)(2,1)S(1)}, bf16[1024,256]{1,0:T(8,128)(2,1)S(1)}) custom-call(bf16[384,1024]{1,0:T(8,128)(2,1)S(1)} %get-tuple-element.34.sh_ref, bf16[384,1024]{1,0:T(8,128)(2,1)S(1)} %get-tuple-element.35.sl_ref, f32[384,128]{1,0:T(8,128)S(1)} %get-tuple-element.36.d_ref, ...), custom_call_target="tpu_custom_call" | custom-call | flops 603979776 | bytes 5308416 | tf_op jit(solution)/shard_map/pallas_call | solution.py:31
  46.2 0.9 %collective-permute-done.7.refs_2_ = f32[64,1024]{1,0:T(8,128)S(1)} collective-permute-done((f32[64,1024]{1,0:T(8,128)S(1)}, f32[64,1024]{1,0:T(8,128)S(1)}, u32[]{:S(2)}, u32[]{:S(2)}) %collective-permute-start.7) | collective-permute-done | bytes 262176 | tf_op jit(solution)/shard_map/ppermute | solution.py:498
  47.1 0.0 collective-permute-done.6.refs_1_
  47.1 6.4 %collective-permute-done.10.refs_5_ = f32[64,1024]{1,0:T(8,128)S(1)} collective-permute-done((f32[64,1024]{1,0:T(8,128)S(1)}, f32[64,1024]{1,0:T(8,128)S(1)}, u32[]{:S(2)}, u32[]{:S(2)}) %collective-permute-start.10) | collective-permute-done | bytes 262176 | tf_op jit(solution)/shard_map/ppermute | solution.py:498
  53.4 0.0 collective-permute-done.9.refs_4_
  53.4 13.3 %shard_map.59 = (bf16[384,1024]{1,0:T(8,128)(2,1)S(1)}, bf16[384,1024]{1,0:T(8,128)(2,1)S(1)}, f32[384,128]{1,0:T(8,128)S(1)}, f32[384,384]{1,0:T(8,128)S(1)}, b...) custom-call(s32[2]{0:T(128)S(1)} %pad_add_fusion.place_ref, s32[5,32]{1,0:T(8,128)S(1)} %bitcast.4, ...), custom_call_target="tpu_custom_call" | custom-call | flops 4303355904 | bytes 4555404 | tf_op jit(solution)/shard_map/pallas_call | solution.py:31
  66.7 3.8 %shard_map.61 = (f32[384,256]{1,0:T(8,128)S(1)}, f32[512,256]{1,0:T(8,128)S(1)}) custom-call(s32[1]{0:T(128)} %get-tuple-element.46.n_ref, bf16[384,1024]{1,0:T(8,128)(2,1)S(1)} %get-tuple-element.43.sh_ref, bf16[384,1024]{1,0:T(8,128)(2,1)S(1)} %get-tuple-element.44.sl_ref, f32[384,128]{1,0:T(8,128)S(1)} %get-tuple-element.45.d_ref, ...), custom_call_target="tpu_custom_call" | custom-call | flops 1207959552 | bytes 5439492 | tf_op jit(solution)/shard_map/pallas_call | solution.py:31
  70.6 1.6 %collective-permute-start.11 = (f32[512,256]{1,0:T(8,128)S(1)}, f32[512,256]{1,0:T(8,128)S(1)}, u32[]{:S(2)}, u32[]{:S(2)}) collective-permute-start(f32[512,256]{1,0:T(8,128)S(1)} %get-tuple-element.56), channel_id=1, source_target_pairs={{0,1},{1,0},{2,3},{3,2},{4,5},{5,4},{6,7},{7,6},{8,9},{9,8},{10,11... | collective-permute-start | bytes 1572872 | tf_op jit(solution)/shard_map/ppermute | solution.py:498
  72.2 0.6 shard_map.62.mine_ref
  72.7 8.5 %collective-permute-done.11.theirs_ref = f32[512,256]{1,0:T(8,128)S(1)} collective-permute-done((f32[512,256]{1,0:T(8,128)S(1)}, f32[512,256]{1,0:T(8,128)S(1)}, u32[]{:S(2)}, u32[]{:S(2)}) %collective-permute-start.11) | collective-permute-done | bytes 524320 | tf_op jit(solution)/shard_map/ppermute | solution.py:498
  81.2 1.6 %shard_map.63 = f32[512,2,256]{2,1,0:T(2,128)} custom-call(s32[2]{0:T(128)S(1)} %pad_add_fusion.place_ref, f32[512,256]{1,0:T(8,128)S(1)} %shard_map.62.mine_ref, f32[512,256]{1,0:T(8,128)S(1)} %collective-permute-done.11.theirs_ref), custom_call_target="tpu_custom_call" | custom-call | tf_op jit(solution)/shard_map/pallas_call | solution.py:569
  (16 shorter events, 0.0 us)
Async XLA Ops:
  0.1 1.2 %copy-start = (f32[512,2,256]{2,1,0:T(2,128)S(1)}, f32[512,2,256]{2,1,0:T(2,128)}, u32[]{:S(2)}) copy-start(f32[512,2,256]{2,1,0:T(2,128)} %state_ref.3) | copy-start | bytes 3145732
  1.3 0.8 copy-start.2
  2.1 14.0 %copy-start.1 = (f32[512,2,256]{2,1,0:T(2,128)S(1)}, f32[512,2,256]{2,1,0:T(2,128)}, u32[]{:S(2)}) copy-start(f32[512,2,256]{2,1,0:T(2,128)} %state_ref.3) | copy-start | bytes 3145732
  2.1 14.0 %copy-start.4 = (f32[32,2,64]{2,1,0:T(2,128)S(1)}, f32[32,2,64]{2,1,0:T(2,128)}, u32[]{:S(2)}) copy-start(f32[32,2,64]{2,1,0:T(2,128)} %values_hbm.1) | copy-start | bytes 49156
  2.1 14.0 %copy-start.5 = (f32[32,2,64]{2,1,0:T(2,128)S(1)}, f32[32,2,64]{2,1,0:T(2,128)}, u32[]{:S(2)}) copy-start(f32[32,2,64]{2,1,0:T(2,128)} %var_hbm.1) | copy-start | bytes 49156
  3.4 9.3 %collective-permute-start = (f32[2,64,512]{2,1,0:T(8,128)S(1)}, f32[2,64,512]{2,1,0:T(8,128)S(1)}, u32[]{:S(2)}, u32[]{:S(2)}) collective-permute-start(f32[2,64,512]{2,1,0:T(8,128)S(1)} %shard_map.55.refs_0_), channel_id=1, source_target_pairs={{0,1},{1,0},{2,3},{3,2},{4,5},{5,4},{6,7},{7,6},{8,9},{9,8},{10,11... | collective-permute-start | bytes 786440 | tf_op jit(solution)/shard_map/ppermute | solution.py:498
  6.5 12.5 %collective-permute-start.2 = (f32[2,64,512]{2,1,0:T(8,128)S(1)}, f32[2,64,512]{2,1,0:T(8,128)S(1)}, u32[]{:S(2)}, u32[]{:S(2)}) collective-permute-start(f32[2,64,512]{2,1,0:T(8,128)S(1)} %shard_map.55.refs_0_), channel_id=1, source_target_pairs={{0,30},{1,31},{2,4},{3,5},{4,2},{5,3},{6,8},{7,9},{8,6},{9,7},{10,... | collective-permute-start | bytes 786440 | tf_op jit(solution)/shard_map/ppermute | solution.py:498
  10.2 8.8 %collective-permute-start.1 = (f32[2,64,512]{2,1,0:T(8,128)S(1)}, f32[2,64,512]{2,1,0:T(8,128)S(1)}, u32[]{:S(2)}, u32[]{:S(2)}) collective-permute-start(f32[2,64,512]{2,1,0:T(8,128)S(1)} %shard_map.55.refs_0_), channel_id=1, source_target_pairs={{0,2},{1,3},{2,0},{3,1},{4,6},{5,7},{6,4},{7,5},{8,10},{9,11},{10,... | collective-permute-start | bytes 786440 | tf_op jit(solution)/shard_map/ppermute | solution.py:498
  12.8 8.6 %collective-permute-start.4 = (f32[2,64,512]{2,1,0:T(8,128)S(1)}, f32[2,64,512]{2,1,0:T(8,128)S(1)}, u32[]{:S(2)}, u32[]{:S(2)}) collective-permute-start(f32[2,64,512]{2,1,0:T(8,128)S(1)} %collective-permute-done.refs_0_.refs_3_), channel_id=1, source_target_pairs={{0,30},{1,31},{2,4},{3,5},{4,2},{5,3},{6,8},{7,9},{8,6},{9,7},{10,... | collective-permute-start | bytes 786440 | tf_op jit(solution)/shard_map/ppermute | solution.py:498
  16.1 5.3 %collective-permute-start.3 = (f32[2,64,512]{2,1,0:T(8,128)S(1)}, f32[2,64,512]{2,1,0:T(8,128)S(1)}, u32[]{:S(2)}, u32[]{:S(2)}) collective-permute-start(f32[2,64,512]{2,1,0:T(8,128)S(1)} %collective-permute-done.refs_0_.refs_3_), channel_id=1, source_target_pairs={{0,2},{1,3},{2,0},{3,1},{4,6},{5,7},{6,4},{7,5},{8,10},{9,11},{10,... | collective-permute-start | bytes 786440 | tf_op jit(solution)/shard_map/ppermute | solution.py:498
  17.3 4.0 %copy-start.6 = (s32[32,5]{0,1:T(8,128)S(1)}, s32[32,5]{0,1:T(8,128)}, u32[]{:S(2)}) copy-start(s32[32,5]{0,1:T(8,128)} %param.6) | copy-start | bytes 1924
  17.3 14.4 %collective-permute-start.5 = (f32[512,256]{1,0:T(8,128)S(1)}, f32[512,256]{1,0:T(8,128)S(1)}, u32[]{:S(2)}, u32[]{:S(2)}) collective-permute-start(f32[512,256]{1,0:T(8,128)S(1)} %get-tuple-element.41), channel_id=1, source_target_pairs={{0,1},{1,0},{2,3},{3,2},{4,5},{5,4},{6,7},{7,6},{8,9},{9,8},{10,11... | collective-permute-start | bytes 1572872 | tf_op jit(solution)/shard_map/ppermute | solution.py:498
  21.4 10.4 %copy-start.3 = (s32[32,2,64]{2,1,0:T(2,128)S(1)}, s32[32,2,64]{2,1,0:T(2,128)}, u32[]{:S(2)}) copy-start(s32[32,2,64]{2,1,0:T(2,128)} %cells_ref.3) | copy-start | bytes 49156
  37.0 8.0 %collective-permute-start.8 = (f32[64,1024]{1,0:T(8,128)S(1)}, f32[64,1024]{1,0:T(8,128)S(1)}, u32[]{:S(2)}, u32[]{:S(2)}) collective-permute-start(f32[64,1024]{1,0:T(8,128)S(1)} %get-tuple-element.42.refs_0_), channel_id=1, source_target_pairs={{0,1},{1,0},{2,3},{3,2},{4,5},{5,4},{6,7},{7,6},{8,9},{9,8},{10,11... | collective-permute-start | bytes 786440 | tf_op jit(solution)/shard_map/ppermute | solution.py:498
  38.5 8.5 %collective-permute-start.7 = (f32[64,1024]{1,0:T(8,128)S(1)}, f32[64,1024]{1,0:T(8,128)S(1)}, u32[]{:S(2)}, u32[]{:S(2)}) collective-permute-start(f32[64,1024]{1,0:T(8,128)S(1)} %get-tuple-element.42.refs_0_), channel_id=1, source_target_pairs={{0,30},{1,31},{2,4},{3,5},{4,2},{5,3},{6,8},{7,9},{8,6},{9,7},{10,... | collective-permute-start | bytes 786440 | tf_op jit(solution)/shard_map/ppermute | solution.py:498
  39.7 7.4 %collective-permute-start.6 = (f32[64,1024]{1,0:T(8,128)S(1)}, f32[64,1024]{1,0:T(8,128)S(1)}, u32[]{:S(2)}, u32[]{:S(2)}) collective-permute-start(f32[64,1024]{1,0:T(8,128)S(1)} %get-tuple-element.42.refs_0_), channel_id=1, source_target_pairs={{0,2},{1,3},{2,0},{3,1},{4,6},{5,7},{6,4},{7,5},{8,10},{9,11},{10,... | collective-permute-start | bytes 786440 | tf_op jit(solution)/shard_map/ppermute | solution.py:498
  44.9 8.5 %collective-permute-start.10 = (f32[64,1024]{1,0:T(8,128)S(1)}, f32[64,1024]{1,0:T(8,128)S(1)}, u32[]{:S(2)}, u32[]{:S(2)}) collective-permute-start(f32[64,1024]{1,0:T(8,128)S(1)} %collective-permute-done.8.refs_3_), channel_id=1, source_target_pairs={{0,30},{1,31},{2,4},{3,5},{4,2},{5,3},{6,8},{7,9},{8,6},{9,7},{10,... | collective-permute-start | bytes 786440 | tf_op jit(solution)/shard_map/ppermute | solution.py:498
  44.9 8.5 %collective-permute-start.9 = (f32[64,1024]{1,0:T(8,128)S(1)}, f32[64,1024]{1,0:T(8,128)S(1)}, u32[]{:S(2)}, u32[]{:S(2)}) collective-permute-start(f32[64,1024]{1,0:T(8,128)S(1)} %collective-permute-done.8.refs_3_), channel_id=1, source_target_pairs={{0,2},{1,3},{2,0},{3,1},{4,6},{5,7},{6,4},{7,5},{8,10},{9,11},{10,... | collective-permute-start | bytes 786440 | tf_op jit(solution)/shard_map/ppermute | solution.py:498
  70.6 10.7 %collective-permute-start.11 = (f32[512,256]{1,0:T(8,128)S(1)}, f32[512,256]{1,0:T(8,128)S(1)}, u32[]{:S(2)}, u32[]{:S(2)}) collective-permute-start(f32[512,256]{1,0:T(8,128)S(1)} %get-tuple-element.56), channel_id=1, source_target_pairs={{0,1},{1,0},{2,3},{3,2},{4,5},{5,4},{6,7},{7,6},{8,9},{9,8},{10,11... | collective-permute-start | bytes 1572872 | tf_op jit(solution)/shard_map/ppermute | solution.py:498

commit v4 on v3

--- a/solution.py
+++ b/solution.py
@@ -93,15 +93,15 @@
     return jnp.transpose(hot)[0:per_patch, :]
 
 
-def pick_kernel(place_ref, cells_ref, state_ref, rows_ref, scratch, field_ref):
+def pick_kernel(region_ref, cells_ref, state_ref, rows_ref, scratch, field_ref):
     patches, cells = state_ref.shape[1:]
     for p in range(patches):
         field_ref[p] = state_ref[:, p, :]
-        hot = selector(cells_ref[pl.ds(place_ref[0] * patches + p, 1), 0, :], cells, scratch)
+        hot = selector(cells_ref[pl.ds(region_ref[0] * patches + p, 1), 0, :], cells, scratch)
         rows_ref[p] = select(hot, split_all(field_ref[p]), NT)
 
 
-def sort_kernel(place_ref, values_hbm, var_hbm, state_ref, *refs):
+def sort_kernel(column_ref, values_hbm, var_hbm, state_ref, *refs):
     keep_ref, send_ref, values_ref, var_ref, sems = refs[-5:]
     copies = [
         pltpu.make_async_copy(values_hbm, values_ref, sems.at[0]),
@@ -109,7 +109,7 @@
     ]
     for copy in copies:
         copy.start()
-    column = place_ref[1]
+    column = column_ref[0]
     first, second = state_ref[:, 0, :], state_ref[:, 1, :]
     keep_ref[...] = jnp.where(column == 0, first, second)
     send_ref[...] = jnp.where(column == 0, second, first)
@@ -117,14 +117,16 @@
         copy.wait()
 
 
-def factor_kernel(pieces, batch, members, chunk, patches_of, place_ref, near_ref, values_ref, var_ref, *refs):
+def factor_kernel(pieces, batch, members, chunk, patches_of, places, *refs):
+    place_refs, refs = refs[:places], refs[places:]
+    near_ref, values_ref, var_ref, *refs = refs
     count = len(refs) - 12
     sources = refs[:count]
     sh_ref, sl_ref, d_ref, g_ref, xh_ref, xl_ref, n_ref, flat, eye_ref, x_ref, wa, wb = refs[count:]
     per_patch = values_ref.shape[2]
     flat[...] = jnp.ones_like(flat)
     blocks = len(pieces)
-    ids, own = patches_of(place_ref)
+    ids, own = patches_of(*place_refs)
     for i in range(blocks):
         patch = ids[i]
         widening = (patch == own).astype(jnp.int32)
@@ -157,15 +159,9 @@
     for i in range(first):
         scaled(i)
     left = (sh_ref[0:head], sl_ref[0:head])
-    rest = list(range(first, blocks))
-    for start, stop in chunks:
-        if stop <= head:
-            if rest:
-                scaled(rest.pop(0))
-        else:
-            while rest:
-                scaled(rest.pop(0))
-        g_ref[start:stop, 0:head] = dot3((sh_ref[start:stop], sl_ref[start:stop]), left, NT)
+    for i in range(first, blocks):
+        scaled(i)
+    g_ref[:, 0:head] = dot3((sh_ref[...], sl_ref[...]), left, NT)
     low = (sh_ref[head:n], sl_ref[head:n])
     g_ref[head:n, head:n] = dot3(low, low, NT)
     g_ref[0:head, head:n] = jnp.transpose(g_ref[head:n, 0:head])
@@ -341,7 +337,7 @@
     def refined(span, value):
         z_ref[span] = z_ref[span] + value
 
-    in_chunks(n, lambda span: dot3(some(s, span), anomaly), crossed)
+    in_chunks(n, lambda span: dot3(some(s, span), [part[...] for part in anomaly]), crossed)
     in_chunks(n, lambda span: dot3(some(x, span), kept(0)), solved)
     in_chunks(n, lambda span: dot3(split(g_ref[span]), kept(1)), left)
     in_chunks(n, lambda span: dot3(some(x, span), kept(0)), refined)
@@ -355,17 +351,22 @@
     lax.fori_loop(0, n_ref[0], refine, 0)
 
 
-def gain_kernel(batch, parts, own_of, place_ref, n_ref, cells_ref, sh_ref, sl_ref, d_ref, g_ref, xh_ref, xl_ref, *refs):
+def gain_kernel(batch, parts, own_of, region_ref, column_ref, n_ref, cells_ref, sh_ref, sl_ref, d_ref, g_ref, *refs):
+    xh_ref, xl_ref, *refs = refs
     states = refs[:parts]
-    z_ref, rows_ref, scratch, cross_ref, parts_ref = refs[parts:]
+    z_ref, rows_ref, scratch, anomaly_ref, cross_ref, parts_ref = refs[parts:]
     anomaly, mean = centred([state[...] for state in states])
+    for i, part in enumerate(anomaly):
+        anomaly_ref[i] = part
+    anomaly = (anomaly_ref.at[0], anomaly_ref.at[1])
     solve(n_ref, (sh_ref, sl_ref), g_ref, (xh_ref, xl_ref), anomaly, z_ref, cross_ref, parts_ref)
     s = (sh_ref[...], sl_ref[...])
-    picks = cells_ref[pl.ds(own_of(place_ref), 1), batch, :]
+    picks = cells_ref[pl.ds(own_of(region_ref, column_ref), 1), batch, :]
     hot = selector(picks, mean.shape[1], scratch)
     zt = split(select(hot, split(z_ref[...]), NT))
     base = jnp.sum(hot * mean, axis=1, keepdims=True) + dot3(zt, split(d_ref[...]))[:, 0:1]
-    rows_ref[...] = base + select(hot, anomaly, NT) - 0.5 * dot3(zt, s)
+    picked = select(hot, [part[...] for part in anomaly], NT)
+    rows_ref[...] = base + picked - 0.5 * dot3(zt, s)
 
 
 def updated(field, start, s, shift, z):
@@ -393,7 +394,7 @@
 
 def last_kernel(n_ref, sh_ref, sl_ref, d_ref, g_ref, xh_ref, xl_ref, *refs):
     (state_ref, *parts), (z_ref, out_ref, cross_ref, parts_ref) = refs[:-4], refs[-4:]
-    anomaly = [part[...] for part in parts] if parts else centred([state_ref[...]])[0]
+    anomaly = parts or centred([state_ref[...]])[0]
     solve(n_ref, (sh_ref, sl_ref), g_ref, (xh_ref, xl_ref), anomaly, z_ref, cross_ref, parts_ref)
     z = z_ref[...]
     start = sh_ref.shape[1] - state_ref.shape[0]
@@ -401,10 +402,10 @@
     out_ref[...] = updated(state_ref[...], start, s, shift_of(z, d_ref), split(z))
 
 
-def join_kernel(place_ref, mine_ref, theirs_ref, out_ref, both, sems):
+def join_kernel(column_ref, mine_ref, theirs_ref, out_ref, both, sems):
     chunks = sems.shape[0]
     size = both.shape[0] // chunks
-    column = place_ref[1]
+    column = column_ref[0]
     copies = []
     for i in range(chunks):
         at = slice(i * size, (i + 1) * size)
@@ -437,10 +438,10 @@
         pltpu.VMEM((2, n, 2 * n), BF16),
         pltpu.VMEM((2, n, 2 * n), BF16),
     ]
-    kernel = functools.partial(factor_kernel, pieces, batch, members, chunk, patches_of)
-    args = [place, near, values, var, *sources]
+    kernel = functools.partial(factor_kernel, pieces, batch, members, chunk, patches_of, len(place))
+    args = [*place, near, values, var, *sources]
     flops = 6 * n * n * members + 60 * n * n * n
-    return call(kernel, outs, [SMEM, SMEM] + [VMEM] * (2 + len(sources)), args, scratch, flops, FACTOR_LIMIT)
+    return call(kernel, outs, [SMEM] * (len(place) + 1) + [VMEM] * (2 + len(sources)), args, scratch, flops, FACTOR_LIMIT)
 
 
 def solver_scratch(n, width):
@@ -453,10 +454,11 @@
     width = states[0].shape[1]
     kernel = functools.partial(gain_kernel, batch, len(states), own_of)
     outs = [((n, width), F32, VMEM), ((cells.shape[2], members), F32, VMEM)]
-    ins = [SMEM, SMEM] + [VMEM] * (7 + len(states))
-    args = [place, more, cells, sh, sl, d, g, xh, xl, *states]
+    ins = [SMEM] * 3 + [VMEM] * (7 + len(states))
+    args = [*place, more, cells, sh, sl, d, g, xh, xl, *states]
     flops = 8 * n * members * width
-    scratch = [pltpu.VMEM((8, 128), jnp.int32)] + solver_scratch(n, width)
+    scratch = [pltpu.VMEM((8, 128), jnp.int32), pltpu.VMEM((2, members, width), BF16)]
+    scratch += solver_scratch(n, width)
     return call(kernel, outs, ins, args, scratch, flops)
 
 
@@ -503,23 +505,23 @@
     members = 2 * half
     regions = lax.axis_size("region")
     region, column = lax.axis_index("region"), lax.axis_index("member")
-    place = jnp.stack([region, column]).astype(jnp.int32)
+    place = (region.astype(jnp.int32)[None], column.astype(jnp.int32)[None])
     near = neighbours.T
 
-    def own_of(place_ref):
-        return place_ref[0] * 2 + place_ref[1]
-
-    def around(place_ref, within):
-        region = place_ref[0]
+    def own_of(region_ref, column_ref):
+        return region_ref[0] * 2 + column_ref[0]
+
+    def around(region, within):
         side = 2 * lax.rem(region, 2) - 1
         outer = lax.rem(region + regions + side, regions)
-        return [r * 2 + p for r in (region, region - side, outer) for p in within], own_of(place_ref)
-
-    def patches_first(place_ref):
-        return around(place_ref, (0, 1))
-
-    def patches_next(place_ref):
-        return around(place_ref, (place_ref[1], 1 - place_ref[1]))
+        return [r * 2 + p for r in (region, region - side, outer) for p in within]
+
+    def patches_first(region_ref, column_ref):
+        return around(region_ref[0], (0, 1)), own_of(region_ref, column_ref)
+
+    def patches_next(region_ref, column_ref):
+        column = column_ref[0]
+        return around(region_ref[0], (column, 1 - column)), own_of(region_ref, column_ref)
 
     def across(x):
         return permute(x, lambda c, q, m: (c, q, 1 - m), regions)
@@ -535,7 +537,7 @@
         pick_kernel,
         [((2, obs_cell.shape[2], half), F32, VMEM)],
         [SMEM, VMEM, VMEM],
-        [place, obs_cell, state],
+        [place[0], obs_cell, state],
         [pltpu.VMEM((8, 128), jnp.int32), pltpu.VMEM((2, half, cells), F32)],
     )
     other = across(rows)
@@ -545,7 +547,7 @@
         sort_kernel,
         [shape, shape, (obs_values.shape, F32, VMEM), (obs_var.shape, F32, VMEM)],
         [SMEM, anywhere, anywhere, VMEM, anywhere],
-        [place, obs_values, obs_var, state, other],
+        [place[1], obs_values, obs_var, state, other],
         [pltpu.SemaphoreType.DMA((2,))],
     )
     pieces = [[(i, (p,), 0), (3 + i, (p,), 1)] for i in range(3) for p in range(2)]
@@ -562,7 +564,7 @@
         sources = [rows, beside(rows), outside(rows), other, beside(other), outside(other)]
         mine, theirs, *anomaly = update(factored, z, states, (0, half), True)
         states = [mine, theirs]
-        factored = factor(pieces, batch, members, CHUNK // 2, patches_next, place, near, values, var, sources)
+        factored = factor(pieces, batch, members, 192, patches_next, place, near, values, var, sources)
     z, theirs = last(factored, states[1], anomaly)
     theirs = across(theirs)
     (mine,) = update(factored, z, states[:1], (0,))
@@ -573,7 +575,7 @@
         out_specs=anywhere,
         scratch_shapes=[pltpu.VMEM(state.shape, F32), pltpu.SemaphoreType.DMA((4,))],
         compiler_params=pltpu.CompilerParams(vmem_limit_bytes=16 * 1024 * 1024),
-    )(place, mine, theirs)
+    )(place[1], mine, theirs)
 
 
 def listed(table_ref):
@@ -609,7 +611,7 @@
             rows = jnp.take(beside, home * region_patches + ids % region_patches, axis=0)
             pieces = [[(0, (i,), 0)] for i in range(ids.shape[0])]
             factored = factor(
-                pieces, batch, members, CHUNK, listed, table, neighbours.T, obs_values, obs_var, [rows]
+                pieces, batch, members, CHUNK, listed, [table], neighbours.T, obs_values, obs_var, [rows]
             )
             new.append(last(factored, fields[p])[1])
         fields = new

time: 83.3 us -> 75.8 us (0.910)
  Pallas kernels: 36.7 us -> 28.7 us
    pallas_call x8, Pallas kernels: 35.1 us -> 27.6 us  [call(): pl.pallas_call(kernel, out_shape=shapes, in_specs=ins, out_specs=[space f...]
where the time goes in v4:
time: 75.8 us; the launch traced here: 75.5 us
  Pallas kernels  28.7 us (38%)
  waiting for transfers between devices  28.7 us (38%)
  starting transfers between devices  15.8 us (21%)
  local copies, waits for them, and re-layouts  2 us (3%)
    ppermute x12, waiting for transfers between devices, permute(): return lax.ppermute(x, BOTH, table)  28.7 us
    pallas_call x8, Pallas kernels, call(): pl.pallas_call(kernel, out_shape=shapes, in_specs=ins, out_specs=[space f...  27.6 us
    ppermute x12, starting transfers between devices, permute(): return lax.ppermute(x, BOTH, table)  15.8 us
    unnamed x14, local copies, waits for them, and re-layouts  2 us
  transfers between devices with their start and end apart: 12, of which 7 were waited for; matrix products, arithmetic and copies ran while one was open for 0% of the time, Pallas kernels for 14%

profile of v4, /device:TPU:0, one launch (start us, length us, event | category | flops | bytes accessed | tf_op | source)
XLA Modules:
  0.0 75.5 jit_solution(12582920406206599353)
XLA Ops:
  0.0 1.2 %copy-done = f32[512,2,256]{2,1,0:T(2,128)S(1)} copy-done((f32[512,2,256]{2,1,0:T(2,128)S(1)}, f32[512,2,256]{2,1,0:T(2,128)}, u32[]{:S(2)}) %copy-start) | copy-done | bytes 1048600
  1.2 0.8 %copy-done.2 = s32[32,2,64]{2,1,0:T(2,128)S(1)} copy-done((s32[32,2,64]{2,1,0:T(2,128)S(1)}, s32[32,2,64]{2,1,0:T(2,128)}, u32[]{:S(2)}) %copy-start.2) | copy-done | bytes 16408
  2.0 0.8 %shard_map.55.refs_5_ = f32[2,64,512]{2,1,0:T(8,128)S(1)} custom-call(s32[1]{0:T(128)} %bitcast.1.region_ref.refs_0_, s32[32,2,64]{2,1,0:T(2,128)S(1)} %copy-done.2, f32[512,2,256]{2,1,0:T(2,128)S(1)} %copy-done), custom_call_target="tpu_custom_call" | custom-call | bytes 1327108 | tf_op jit(solution)/shard_map/pallas_call | solution.py:31
  2.8 3.0 %collective-permute-start = (f32[2,64,512]{2,1,0:T(8,128)S(1)}, f32[2,64,512]{2,1,0:T(8,128)S(1)}, u32[]{:S(2)}, u32[]{:S(2)}) collective-permute-start(f32[2,64,512]{2,1,0:T(8,128)S(1)} %shard_map.55.refs_5_), channel_id=1, source_target_pairs={{0,1},{1,0},{2,3},{3,2},{4,5},{5,4},{6,7},{7,6},{8,9},{9,8},{10,11... | collective-permute-start | bytes 786440 | tf_op jit(solution)/shard_map/ppermute | solution.py:500
  5.8 3.7 %collective-permute-start.2 = (f32[2,64,512]{2,1,0:T(8,128)S(1)}, f32[2,64,512]{2,1,0:T(8,128)S(1)}, u32[]{:S(2)}, u32[]{:S(2)}) collective-permute-start(f32[2,64,512]{2,1,0:T(8,128)S(1)} %shard_map.55.refs_5_), channel_id=1, source_target_pairs={{0,30},{1,31},{2,4},{3,5},{4,2},{5,3},{6,8},{7,9},{8,6},{9,7},{10,... | collective-permute-start | bytes 786440 | tf_op jit(solution)/shard_map/ppermute | solution.py:500
  9.5 0.0 collective-permute-start.1
  9.5 2.6 %collective-permute-done.refs_0_.refs_8_ = f32[2,64,512]{2,1,0:T(8,128)S(1)} collective-permute-done((f32[2,64,512]{2,1,0:T(8,128)S(1)}, f32[2,64,512]{2,1,0:T(8,128)S(1)}, u32[]{:S(2)}, u32[]{:S(2)}) %collective-permute-start) | collective-permute-done | bytes 262176 | tf_op jit(solution)/shard_map/ppermute | solution.py:500
  12.1 3.3 %collective-permute-start.4 = (f32[2,64,512]{2,1,0:T(8,128)S(1)}, f32[2,64,512]{2,1,0:T(8,128)S(1)}, u32[]{:S(2)}, u32[]{:S(2)}) collective-permute-start(f32[2,64,512]{2,1,0:T(8,128)S(1)} %collective-permute-done.refs_0_.refs_8_), channel_id=1, source_target_pairs={{0,30},{1,31},{2,4},{3,5},{4,2},{5,3},{6,8},{7,9},{8,6},{9,7},{10,... | collective-permute-start | bytes 786440 | tf_op jit(solution)/shard_map/ppermute | solution.py:500
  15.5 0.7 shard_map.56
  16.2 0.0 copy-start.6
  16.2 1.6 %collective-permute-start.5 = (f32[512,256]{1,0:T(8,128)S(1)}, f32[512,256]{1,0:T(8,128)S(1)}, u32[]{:S(2)}, u32[]{:S(2)}) collective-permute-start(f32[512,256]{1,0:T(8,128)S(1)} %get-tuple-element.41), channel_id=1, source_target_pairs={{0,1},{1,0},{2,3},{3,2},{4,5},{5,4},{6,7},{7,6},{8,9},{9,8},{10,11... | collective-permute-start | bytes 1572872 | tf_op jit(solution)/shard_map/ppermute | solution.py:500
  17.8 0.0 collective-permute-done.2.refs_7_
  17.8 0.0 collective-permute-done.1.refs_6_
  17.8 3.0 %collective-permute-done.4.refs_10_ = f32[2,64,512]{2,1,0:T(8,128)S(1)} collective-permute-done((f32[2,64,512]{2,1,0:T(8,128)S(1)}, f32[2,64,512]{2,1,0:T(8,128)S(1)}, u32[]{:S(2)}, u32[]{:S(2)}) %collective-permute-start.4) | collective-permute-done | bytes 262176 | tf_op jit(solution)/shard_map/ppermute | solution.py:500
  20.7 0.0 collective-permute-done.3.refs_9_
  20.8 7.8 %shard_map.57 = (bf16[384,1024]{1,0:T(8,128)(2,1)S(1)}, bf16[384,1024]{1,0:T(8,128)(2,1)S(1)}, f32[384,128]{1,0:T(8,128)S(1)}, f32[384,384]{1,0:T(8,128)S(1)}, b...) custom-call(s32[1]{0:T(128)} %bitcast.1.region_ref.refs_0_, s32[1]{0:T(128)} %bitcast.column_ref.refs_1_, ...), custom_call_target="tpu_custom_call" | custom-call | flops 4303355904 | bytes 4555404 | tf_op jit(solution)/shard_map/pallas_call | solution.py:31
  28.5 2.0 %collective-permute-done.5.refs_3_.refs_1_ = f32[512,256]{1,0:T(8,128)S(1)} collective-permute-done((f32[512,256]{1,0:T(8,128)S(1)}, f32[512,256]{1,0:T(8,128)S(1)}, u32[]{:S(2)}, u32[]{:S(2)}) %collective-permute-start.5) | collective-permute-done | bytes 524320 | tf_op jit(solution)/shard_map/ppermute | solution.py:500
  30.6 4.7 %shard_map.58 = (f32[384,256]{1,0:T(8,128)S(1)}, f32[64,1024]{1,0:T(8,128)S(1)}) custom-call(s32[1]{0:T(128)} %bitcast.1.region_ref.refs_0_, s32[1]{0:T(128)} %bitcast.column_ref.refs_1_, s32[1]{0:T(128)} %get-tuple-element.33.n_ref, s32[32,2,64]{2,1,0:T(2,128)S(1)} %copy-done.3, bf16[384,1024]{1,0:T(8,128)(2,1)S(1)} %get-tuple-element.34.sh_ref, ...), custom_call_target="tpu_custom_call" | custom-call | flops 805306368 | bytes 4669452 | tf_op jit(solution)/shard_map/pallas_call | solution.py:31
  35.3 1.6 %collective-permute-start.8 = (f32[64,1024]{1,0:T(8,128)S(1)}, f32[64,1024]{1,0:T(8,128)S(1)}, u32[]{:S(2)}, u32[]{:S(2)}) collective-permute-start(f32[64,1024]{1,0:T(8,128)S(1)} %get-tuple-element.42.refs_5_), channel_id=1, source_target_pairs={{0,1},{1,0},{2,3},{3,2},{4,5},{5,4},{6,7},{7,6},{8,9},{9,8},{10,11... | collective-permute-start | bytes 786440 | tf_op jit(solution)/shard_map/ppermute | solution.py:500
  36.9 1.0 %collective-permute-start.7 = (f32[64,1024]{1,0:T(8,128)S(1)}, f32[64,1024]{1,0:T(8,128)S(1)}, u32[]{:S(2)}, u32[]{:S(2)}) collective-permute-start(f32[64,1024]{1,0:T(8,128)S(1)} %get-tuple-element.42.refs_5_), channel_id=1, source_target_pairs={{0,30},{1,31},{2,4},{3,5},{4,2},{5,3},{6,8},{7,9},{8,6},{9,7},{10,... | collective-permute-start | bytes 786440 | tf_op jit(solution)/shard_map/ppermute | solution.py:500
  37.9 5.4 %collective-permute-done.8.refs_8_ = f32[64,1024]{1,0:T(8,128)S(1)} collective-permute-done((f32[64,1024]{1,0:T(8,128)S(1)}, f32[64,1024]{1,0:T(8,128)S(1)}, u32[]{:S(2)}, u32[]{:S(2)}) %collective-permute-start.8) | collective-permute-done | bytes 262176 | tf_op jit(solution)/shard_map/ppermute | solution.py:500
  43.3 0.0 collective-permute-start.10
  43.3 0.0 collective-permute-start.9
  43.3 1.2 %shard_map.60 = (f32[512,256]{1,0:T(8,128)S(1)}, f32[512,256]{1,0:T(8,128)S(1)}, bf16[1024,256]{1,0:T(8,128)(2,1)S(1)}, bf16[1024,256]{1,0:T(8,128)(2,1)S(1)}) custom-call(bf16[384,1024]{1,0:T(8,128)(2,1)S(1)} %get-tuple-element.34.sh_ref, bf16[384,1024]{1,0:T(8,128)(2,1)S(1)} %get-tuple-element.35.sl_ref, f32[384,128]{1,0:T(8,128)S(1)} %get-tuple-element.36.d_ref, ...), custom_call_target="tpu_custom_call" | custom-call | flops 603979776 | bytes 5308416 | tf_op jit(solution)/shard_map/pallas_call | solution.py:31
  44.6 0.8 %collective-permute-done.7.refs_7_ = f32[64,1024]{1,0:T(8,128)S(1)} collective-permute-done((f32[64,1024]{1,0:T(8,128)S(1)}, f32[64,1024]{1,0:T(8,128)S(1)}, u32[]{:S(2)}, u32[]{:S(2)}) %collective-permute-start.7) | collective-permute-done | bytes 262176 | tf_op jit(solution)/shard_map/ppermute | solution.py:500
  45.4 6.4 %collective-permute-done.10.refs_10_ = f32[64,1024]{1,0:T(8,128)S(1)} collective-permute-done((f32[64,1024]{1,0:T(8,128)S(1)}, f32[64,1024]{1,0:T(8,128)S(1)}, u32[]{:S(2)}, u32[]{:S(2)}) %collective-permute-start.10) | collective-permute-done | bytes 262176 | tf_op jit(solution)/shard_map/ppermute | solution.py:500
  51.8 7.9 %shard_map.59 = (bf16[384,1024]{1,0:T(8,128)(2,1)S(1)}, bf16[384,1024]{1,0:T(8,128)(2,1)S(1)}, f32[384,128]{1,0:T(8,128)S(1)}, f32[384,384]{1,0:T(8,128)S(1)}, b...) custom-call(s32[1]{0:T(128)} %bitcast.1.region_ref.refs_0_, s32[1]{0:T(128)} %bitcast.column_ref.refs_1_, ...), custom_call_target="tpu_custom_call" | custom-call | flops 4303355904 | bytes 4555404 | tf_op jit(solution)/shard_map/pallas_call | solution.py:31
  59.8 3.8 %shard_map.61 = (f32[384,256]{1,0:T(8,128)S(1)}, f32[512,256]{1,0:T(8,128)S(1)}) custom-call(s32[1]{0:T(128)} %get-tuple-element.46.n_ref, bf16[384,1024]{1,0:T(8,128)(2,1)S(1)} %get-tuple-element.43.sh_ref, bf16[384,1024]{1,0:T(8,128)(2,1)S(1)} %get-tuple-element.44.sl_ref, f32[384,128]{1,0:T(8,128)S(1)} %get-tuple-element.45.d_ref, ...), custom_call_target="tpu_custom_call" | custom-call | flops 1207959552 | bytes 5439492 | tf_op jit(solution)/shard_map/pallas_call | solution.py:31
  63.6 1.6 %collective-permute-start.11 = (f32[512,256]{1,0:T(8,128)S(1)}, f32[512,256]{1,0:T(8,128)S(1)}, u32[]{:S(2)}, u32[]{:S(2)}) collective-permute-start(f32[512,256]{1,0:T(8,128)S(1)} %get-tuple-element.56), channel_id=1, source_target_pairs={{0,1},{1,0},{2,3},{3,2},{4,5},{5,4},{6,7},{7,6},{8,9},{9,8},{10,11... | collective-permute-start | bytes 1572872 | tf_op jit(solution)/shard_map/ppermute | solution.py:500
  65.2 0.6 shard_map.62.mine_ref
  65.8 8.5 %collective-permute-done.11.theirs_ref = f32[512,256]{1,0:T(8,128)S(1)} collective-permute-done((f32[512,256]{1,0:T(8,128)S(1)}, f32[512,256]{1,0:T(8,128)S(1)}, u32[]{:S(2)}, u32[]{:S(2)}) %collective-permute-start.11) | collective-permute-done | bytes 524320 | tf_op jit(solution)/shard_map/ppermute | solution.py:500
  74.3 1.1 %shard_map.63 = f32[512,2,256]{2,1,0:T(2,128)} custom-call(s32[1]{0:T(128)} %bitcast.column_ref.refs_1_, f32[512,256]{1,0:T(8,128)S(1)} %shard_map.62.mine_ref, f32[512,256]{1,0:T(8,128)S(1)} %collective-permute-done.11.theirs_ref), custom_call_target="tpu_custom_call" | custom-call | tf_op jit(solution)/shard_map/pallas_call | solution.py:571
  (15 shorter events, 0.0 us)
Async XLA Ops:
  0.0 1.2 %copy-start = (f32[512,2,256]{2,1,0:T(2,128)S(1)}, f32[512,2,256]{2,1,0:T(2,128)}, u32[]{:S(2)}) copy-start(f32[512,2,256]{2,1,0:T(2,128)} %state_ref.3) | copy-start | bytes 3145732
  1.2 0.8 %copy-start.2 = (s32[32,2,64]{2,1,0:T(2,128)S(1)}, s32[32,2,64]{2,1,0:T(2,128)}, u32[]{:S(2)}) copy-start(s32[32,2,64]{2,1,0:T(2,128)} %cells_ref.3) | copy-start | bytes 49156
  2.0 13.5 %copy-start.1 = (f32[512,2,256]{2,1,0:T(2,128)S(1)}, f32[512,2,256]{2,1,0:T(2,128)}, u32[]{:S(2)}) copy-start(f32[512,2,256]{2,1,0:T(2,128)} %state_ref.3) | copy-start | bytes 3145732
  2.0 13.5 %copy-start.4 = (f32[32,2,64]{2,1,0:T(2,128)S(1)}, f32[32,2,64]{2,1,0:T(2,128)}, u32[]{:S(2)}) copy-start(f32[32,2,64]{2,1,0:T(2,128)} %values_hbm.1) | copy-start | bytes 49156
  2.0 13.5 %copy-start.5 = (f32[32,2,64]{2,1,0:T(2,128)S(1)}, f32[32,2,64]{2,1,0:T(2,128)}, u32[]{:S(2)}) copy-start(f32[32,2,64]{2,1,0:T(2,128)} %var_hbm.1) | copy-start | bytes 49156
  2.8 9.3 %collective-permute-start = (f32[2,64,512]{2,1,0:T(8,128)S(1)}, f32[2,64,512]{2,1,0:T(8,128)S(1)}, u32[]{:S(2)}, u32[]{:S(2)}) collective-permute-start(f32[2,64,512]{2,1,0:T(8,128)S(1)} %shard_map.55.refs_5_), channel_id=1, source_target_pairs={{0,1},{1,0},{2,3},{3,2},{4,5},{5,4},{6,7},{7,6},{8,9},{9,8},{10,11... | collective-permute-start | bytes 786440 | tf_op jit(solution)/shard_map/ppermute | solution.py:500
  5.8 11.9 %collective-permute-start.2 = (f32[2,64,512]{2,1,0:T(8,128)S(1)}, f32[2,64,512]{2,1,0:T(8,128)S(1)}, u32[]{:S(2)}, u32[]{:S(2)}) collective-permute-start(f32[2,64,512]{2,1,0:T(8,128)S(1)} %shard_map.55.refs_5_), channel_id=1, source_target_pairs={{0,30},{1,31},{2,4},{3,5},{4,2},{5,3},{6,8},{7,9},{8,6},{9,7},{10,... | collective-permute-start | bytes 786440 | tf_op jit(solution)/shard_map/ppermute | solution.py:500
  9.5 8.3 %collective-permute-start.1 = (f32[2,64,512]{2,1,0:T(8,128)S(1)}, f32[2,64,512]{2,1,0:T(8,128)S(1)}, u32[]{:S(2)}, u32[]{:S(2)}) collective-permute-start(f32[2,64,512]{2,1,0:T(8,128)S(1)} %shard_map.55.refs_5_), channel_id=1, source_target_pairs={{0,2},{1,3},{2,0},{3,1},{4,6},{5,7},{6,4},{7,5},{8,10},{9,11},{10,... | collective-permute-start | bytes 786440 | tf_op jit(solution)/shard_map/ppermute | solution.py:500
  12.1 8.6 %collective-permute-start.4 = (f32[2,64,512]{2,1,0:T(8,128)S(1)}, f32[2,64,512]{2,1,0:T(8,128)S(1)}, u32[]{:S(2)}, u32[]{:S(2)}) collective-permute-start(f32[2,64,512]{2,1,0:T(8,128)S(1)} %collective-permute-done.refs_0_.refs_8_), channel_id=1, source_target_pairs={{0,30},{1,31},{2,4},{3,5},{4,2},{5,3},{6,8},{7,9},{8,6},{9,7},{10,... | collective-permute-start | bytes 786440 | tf_op jit(solution)/shard_map/ppermute | solution.py:500
  15.5 5.3 %collective-permute-start.3 = (f32[2,64,512]{2,1,0:T(8,128)S(1)}, f32[2,64,512]{2,1,0:T(8,128)S(1)}, u32[]{:S(2)}, u32[]{:S(2)}) collective-permute-start(f32[2,64,512]{2,1,0:T(8,128)S(1)} %collective-permute-done.refs_0_.refs_8_), channel_id=1, source_target_pairs={{0,2},{1,3},{2,0},{3,1},{4,6},{5,7},{6,4},{7,5},{8,10},{9,11},{10,... | collective-permute-start | bytes 786440 | tf_op jit(solution)/shard_map/ppermute | solution.py:500
  16.2 4.6 %copy-start.6 = (s32[32,5]{0,1:T(8,128)S(1)}, s32[32,5]{0,1:T(8,128)}, u32[]{:S(2)}) copy-start(s32[32,5]{0,1:T(8,128)} %param.6) | copy-start | bytes 1924
  16.2 14.4 %collective-permute-start.5 = (f32[512,256]{1,0:T(8,128)S(1)}, f32[512,256]{1,0:T(8,128)S(1)}, u32[]{:S(2)}, u32[]{:S(2)}) collective-permute-start(f32[512,256]{1,0:T(8,128)S(1)} %get-tuple-element.41), channel_id=1, source_target_pairs={{0,1},{1,0},{2,3},{3,2},{4,5},{5,4},{6,7},{7,6},{8,9},{9,8},{10,11... | collective-permute-start | bytes 1572872 | tf_op jit(solution)/shard_map/ppermute | solution.py:500
  20.8 9.8 %copy-start.3 = (s32[32,2,64]{2,1,0:T(2,128)S(1)}, s32[32,2,64]{2,1,0:T(2,128)}, u32[]{:S(2)}) copy-start(s32[32,2,64]{2,1,0:T(2,128)} %cells_ref.3) | copy-start | bytes 49156
  35.3 8.0 %collective-permute-start.8 = (f32[64,1024]{1,0:T(8,128)S(1)}, f32[64,1024]{1,0:T(8,128)S(1)}, u32[]{:S(2)}, u32[]{:S(2)}) collective-permute-start(f32[64,1024]{1,0:T(8,128)S(1)} %get-tuple-element.42.refs_5_), channel_id=1, source_target_pairs={{0,1},{1,0},{2,3},{3,2},{4,5},{5,4},{6,7},{7,6},{8,9},{9,8},{10,11... | collective-permute-start | bytes 786440 | tf_op jit(solution)/shard_map/ppermute | solution.py:500
  36.9 8.5 %collective-permute-start.7 = (f32[64,1024]{1,0:T(8,128)S(1)}, f32[64,1024]{1,0:T(8,128)S(1)}, u32[]{:S(2)}, u32[]{:S(2)}) collective-permute-start(f32[64,1024]{1,0:T(8,128)S(1)} %get-tuple-element.42.refs_5_), channel_id=1, source_target_pairs={{0,30},{1,31},{2,4},{3,5},{4,2},{5,3},{6,8},{7,9},{8,6},{9,7},{10,... | collective-permute-start | bytes 786440 | tf_op jit(solution)/shard_map/ppermute | solution.py:500
  37.9 7.5 %collective-permute-start.6 = (f32[64,1024]{1,0:T(8,128)S(1)}, f32[64,1024]{1,0:T(8,128)S(1)}, u32[]{:S(2)}, u32[]{:S(2)}) collective-permute-start(f32[64,1024]{1,0:T(8,128)S(1)} %get-tuple-element.42.refs_5_), channel_id=1, source_target_pairs={{0,2},{1,3},{2,0},{3,1},{4,6},{5,7},{6,4},{7,5},{8,10},{9,11},{10,... | collective-permute-start | bytes 786440 | tf_op jit(solution)/shard_map/ppermute | solution.py:500
  43.3 8.5 %collective-permute-start.10 = (f32[64,1024]{1,0:T(8,128)S(1)}, f32[64,1024]{1,0:T(8,128)S(1)}, u32[]{:S(2)}, u32[]{:S(2)}) collective-permute-start(f32[64,1024]{1,0:T(8,128)S(1)} %collective-permute-done.8.refs_8_), channel_id=1, source_target_pairs={{0,30},{1,31},{2,4},{3,5},{4,2},{5,3},{6,8},{7,9},{8,6},{9,7},{10,... | collective-permute-start | bytes 786440 | tf_op jit(solution)/shard_map/ppermute | solution.py:500
  43.3 8.5 %collective-permute-start.9 = (f32[64,1024]{1,0:T(8,128)S(1)}, f32[64,1024]{1,0:T(8,128)S(1)}, u32[]{:S(2)}, u32[]{:S(2)}) collective-permute-start(f32[64,1024]{1,0:T(8,128)S(1)} %collective-permute-done.8.refs_8_), channel_id=1, source_target_pairs={{0,2},{1,3},{2,0},{3,1},{4,6},{5,7},{6,4},{7,5},{8,10},{9,11},{10,... | collective-permute-start | bytes 786440 | tf_op jit(solution)/shard_map/ppermute | solution.py:500
  63.6 10.7 %collective-permute-start.11 = (f32[512,256]{1,0:T(8,128)S(1)}, f32[512,256]{1,0:T(8,128)S(1)}, u32[]{:S(2)}, u32[]{:S(2)}) collective-permute-start(f32[512,256]{1,0:T(8,128)S(1)} %get-tuple-element.56), channel_id=1, source_target_pairs={{0,1},{1,0},{2,3},{3,2},{4,5},{5,4},{6,7},{7,6},{8,9},{9,8},{10,11... | collective-permute-start | bytes 1572872 | tf_op jit(solution)/shard_map/ppermute | solution.py:500
